TPU v7x, 32 devices: a whole 2x2x4 slice. The times are simulated.
32 devices in a mesh: row: 4 (over z), col: 8 (over y, x, core).
Axes of the slice: x: 2, y: 2, z: 4, core: 2. Of those that a mesh axis runs over, the one named last changes fastest.
Arguments:
- tokens: bfloat16 [1024, 2560], P('row', 'col'), may hold values from -6 to 6
- w_down: bfloat16 [2560, 1056], P('col'), may hold values from -0.125 to 0.125
- q_gain: float32 [768], replicated, may hold values from 0.1 to 1.9
- kv_gain: float32 [256], replicated, may hold values from 0.1 to 1.9
- w_q_up: bfloat16 [768, 768], P(None, 'col'), may hold values from -8.8767604 to 8.8767604
- w_kv_up: bfloat16 [256, 1024], replicated, may hold values from -0.375 to 0.375
- w_out: bfloat16 [512, 2560], P('col'), may hold values from -0.75 to 0.75
- latent_cache: bfloat16 [4, 2048, 288], P('row', 'col'), may hold values from -6 to 6
- cache_len: int32 [4], replicated, may hold values from 1 to 2048, as said below
- new_len: int32 [4], replicated, may hold values from 1 to 256, as said below
- page_table: int32 [4, 32], replicated, may hold values from 0 to 31, each once within a row
- home_slot: int32 [4], replicated, may hold values from 0 to 3, each once
Outputs:
- output: bfloat16 [1024, 2560], P('row', 'col')
Inputs may be any that keep to these rules, and one draw needn't show every extreme that they name: `cache_len`: some slot has exactly 2048 cached tokens; about half the slots hold at most 256, the others at least 1792. `new_len`: some request has exactly 256 real new tokens.
All inputs are finite; a program needn't handle non-finite values.
Results may differ from a plain program's by a relative error of at most 0.023.
Values may be sent and summed in bfloat16 or wider, within the bound.
No kernel may reach another device: no remote copies, remote signals or barrier semaphores. Data moves between devices by JAX's collectives and lax.ppermute only.
A program may use at most 64 MiB of HBM per device.

v0:
```python
import math

import jax
import jax.numpy as jnp
from jax import lax
from jax.sharding import PartitionSpec as P

NOPE = 64
ROPE = 32
VDIM = 64


epsilon = 1e-05


def rms_scale(values, gain):
    return values * lax.rsqrt(jnp.mean(values * values, axis=-1, keepdims=True) + epsilon) * gain


def angle_tables(positions, width):
    half_dim = width // 2
    frequency = 10000.0 ** (-2.0 * jnp.arange(half_dim, dtype=jnp.float32) / width)
    angles = positions.astype(jnp.float32)[:, None] * frequency[None, :]
    return (jnp.cos(angles), jnp.sin(angles))


def rotary(values, cosine, sine_table):
    half_dim = values.shape[-1] // 2
    first_half = values[..., :half_dim]
    second_half = values[..., half_dim:]
    return jnp.concatenate(
        [
            first_half * cosine - second_half * sine_table,
            second_half * cosine + first_half * sine_table,
        ],
        -1,
    )


def body(
    tokens,
    w_down,
    q_gain,
    kv_gain,
    w_q_up,
    w_kv_up,
    w_out,
    latent_cache,
    cache_len,
    new_len,
    page_table,
    home_slot,
):
    columns = lax.axis_size("col")
    column_id = lax.axis_index("col")
    row_id = lax.axis_index("row")
    group_rows = tokens.shape[0]
    own_rows = group_rows // columns
    q_width = q_gain.shape[0]
    kv_width = kv_gain.shape[0]
    slot_index = home_slot[row_id]
    cached_count = cache_len[slot_index]
    live_count = new_len[row_id]
    combined = lax.psum_scatter(
        jnp.dot(tokens, w_down, preferred_element_type=jnp.float32),
        "col",
        scatter_dimension=0,
        tiled=True,
    )
    own_position = cached_count + column_id * own_rows + jnp.arange(own_rows, dtype=jnp.int32)
    own_cos, own_sin = angle_tables(own_position, ROPE)
    query_latent = rms_scale(combined[:, :q_width], q_gain).astype(jnp.bfloat16)
    new_latent = rms_scale(combined[:, q_width : q_width + kv_width], kv_gain).astype(jnp.bfloat16)
    new_rope = rotary(combined[:, q_width + kv_width :], own_cos, own_sin).astype(jnp.bfloat16)
    new_rows = jnp.concatenate([new_latent, new_rope], 1)
    projected = jnp.dot(
        lax.all_gather(query_latent, "col", axis=0, tiled=True),
        w_q_up,
        preferred_element_type=jnp.float32,
    )
    query_cos, query_sin = angle_tables(
        cached_count + jnp.arange(group_rows, dtype=jnp.int32), ROPE
    )
    queries = jnp.concatenate(
        [projected[:, :NOPE], rotary(projected[:, NOPE:], query_cos, query_sin)], 1
    ).astype(jnp.bfloat16)
    segment = lax.all_gather(latent_cache, "row", axis=0, tiled=True)
    matches = jnp.arange(segment.shape[0], dtype=jnp.int32) == slot_index
    own_cache = jnp.sum(
        jnp.where(matches[:, None, None], segment.astype(jnp.float32), 0.0), 0
    ).astype(jnp.bfloat16)
    head_width = NOPE + VDIM
    head_weight = lax.dynamic_slice_in_dim(w_kv_up, column_id * head_width, head_width, 1)

    def expand(latents):
        lifted = jnp.dot(
            latents[:, :kv_width], head_weight, preferred_element_type=jnp.float32
        ).astype(jnp.bfloat16)
        return (jnp.concatenate([lifted[:, :NOPE], latents[:, kv_width:]], 1), lifted[:, NOPE:])

    cache_latents, fresh_latents = (
        lax.all_gather(own_cache, "col", axis=0, tiled=True),
        lax.all_gather(new_rows, "col", axis=0, tiled=True),
    )
    cache_keys, cache_values = expand(cache_latents)
    fresh_keys, fresh_values = expand(fresh_latents)
    key_total = cache_keys.shape[0]
    page_row = page_table[slot_index]
    page_count = page_row.shape[0]
    page_size = key_total // page_count
    block_size = min(512, key_total)
    offsets = jnp.arange(page_size, dtype=jnp.int32)
    page_ids = jnp.arange(page_count, dtype=jnp.int32)
    logical_page = jnp.sum(
        page_ids[:, None] * (page_row[:, None] == page_ids[None, :]).astype(jnp.int32), 0
    )
    cached_visible = (logical_page[:, None] * page_size + offsets[None, :]).reshape(
        key_total
    ) < cached_count
    block_limit = key_total // block_size
    score_scale = 1.0 / math.sqrt(NOPE + ROPE)
    query_index = jnp.arange(group_rows, dtype=jnp.int32)[:, None]
    key_index = jnp.arange(group_rows, dtype=jnp.int32)[None, :]
    fresh_visible = (key_index <= query_index) & (key_index < live_count)
    fresh_scores = (
        jnp.einsum("qd,kd->qk", queries, fresh_keys, preferred_element_type=jnp.float32)
        * score_scale
    )
    fresh_scores = jnp.where(fresh_visible, fresh_scores, -jnp.inf)
    first_peak = jnp.max(fresh_scores, 1)
    fresh_exponent = jnp.exp(fresh_scores - first_peak[:, None])
    start_state = (
        first_peak,
        jnp.sum(fresh_exponent, 1),
        jnp.dot(
            fresh_exponent.astype(jnp.bfloat16), fresh_values, preferred_element_type=jnp.float32
        ),
    )

    def accumulate(block_id, running):
        row_peak, row_total, summed = running
        key_block = lax.dynamic_slice_in_dim(cache_keys, block_id * block_size, block_size, 0)
        mask_block = lax.dynamic_slice_in_dim(cached_visible, block_id * block_size, block_size, 0)
        value_block = lax.dynamic_slice_in_dim(cache_values, block_id * block_size, block_size, 0)
        raw_scores = (
            jnp.einsum("qd,kd->qk", queries, key_block, preferred_element_type=jnp.float32)
            * score_scale
        )
        raw_scores = jnp.where(mask_block[None, :], raw_scores, -jnp.inf)
        next_peak = jnp.maximum(row_peak, jnp.max(raw_scores, 1))
        factor = jnp.exp(row_peak - next_peak)
        exponent = jnp.exp(raw_scores - next_peak[:, None])
        next_total = row_total * factor + jnp.sum(exponent, 1)
        next_summed = summed * factor[:, None] + jnp.dot(
            exponent.astype(jnp.bfloat16), value_block, preferred_element_type=jnp.float32
        )
        return (next_peak, next_total, next_summed)

    row_peak, row_total, summed = lax.fori_loop(0, block_limit, accumulate, start_state)
    attended = (summed / row_total[:, None]).astype(jnp.bfloat16)
    live_rows = jnp.arange(group_rows, dtype=jnp.int32) < live_count
    attended = jnp.where(live_rows[:, None], attended, jnp.zeros_like(attended))
    summed_out = lax.psum_scatter(
        lax.dot_general(
            w_out, attended, (((0,), (1,)), ((), ())), preferred_element_type=jnp.float32
        ).astype(jnp.bfloat16),
        "col",
        scatter_dimension=0,
        tiled=True,
    ).astype(jnp.float32)
    result = summed_out.T.astype(jnp.bfloat16)
    return result


def solution(mesh):
    return jax.shard_map(
        body,
        mesh=mesh,
        in_specs=(
            P("row", "col"),
            P("col", None),
            P(),
            P(),
            P(None, "col"),
            P(),
            P("col", None),
            P("row", "col", None),
            P(),
            P(),
            P(),
            P(),
        ),
        out_specs=P("row", "col"),
        check_vma=False,
    )
```

profile of v0, /device:TPU:0, one launch (start us, length us, event | category | flops | bytes accessed | tf_op | source)
XLA Modules:
  0.0 127.3 jit_solution(13306079583204297522)
XLA Ops:
  6.5 1.1 copy-done
  7.7 2.4 %fusion.52 = f32[256,1056]{1,0:T(8,128)} fusion(bf16[256,320]{0,1:T(8,128)(2,1)} %param.14, bf16[320,1056]{1,0:T(8,128)(2,1)S(1)} %copy-done), kind=kOutput, calls=%fused_computation.87 | convolution fusion | flops 173015040 | bytes 1921024
  10.2 0.6 dynamic_slice.37
  10.8 0.6 iota_compare_fusion.3
  11.5 18.2 %all_gather.14 = bf16[4,256,288]{1,2,0:T(8,128)(2,1)S(1)} all-gather(bf16[1,256,288]{1,2,0:T(8,128)(2,1)S(1)} %copy-done.3), channel_id=1, replica_groups=mesh['row'=4,'col'=8] {'row'}, dimensions={0}, use_global_device_ids=true | all-gather | bytes 737280 | tf_op jit(solution)/shard_map/all_gather | solution.py:87
  29.6 0.8 select_reduce_fusion
  31.9 0.6 dynamic_slice.36
  32.5 0.6 iota_compare_fusion.2
  33.7 0.6 dynamic_slice.38
  34.4 0.6 add_convert_fusion
  35.6 0.7 dynamic-slice_bitcast_fusion
  36.4 0.7 add_compare_fusion
  37.2 12.9 %reduce-scatter.7.cloned.1.call-done = f32[32,1056]{1,0:T(8,128)} async-done(((f32[256,1056]{1,0:T(8,128)}), f32[32,1056]{1,0:T(8,128)}) %reduce-scatter.7.cloned.1.call-update) | async-done | bytes 135184
  50.1 0.9 fusion.50
  51.5 0.8 slice.71
  52.7 9.2 %all_gather.13 = bf16[256,288]{1,0:T(8,128)(2,1)S(1)} all-gather(bf16[32,288]{1,0:T(8,128)(2,1)S(1)} %pad_maximum_fusion.2), channel_id=1, replica_groups=mesh['row'=4,'col'=8] {'col'}, dimensions={0}, use_global_device_ids=true | all-gather | bytes 165888 | tf_op jit(solution)/shard_map/all_gather | solution.py:103
  61.9 1.1 convolution_convert_fusion.2
  63.6 8.7 %all_gather.12 = bf16[256,768]{1,0:T(8,128)(2,1)S(1)} all-gather(bf16[32,768]{1,0:T(8,128)(2,1)S(1)} %copy.34), channel_id=1, replica_groups=mesh['row'=4,'col'=8] {'col'}, dimensions={0}, use_global_device_ids=true | all-gather | bytes 442368 | tf_op jit(solution)/shard_map/all_gather | solution.py:77
  72.3 0.3 fusion.53
  72.9 0.3 fusion.51
  73.4 3.0 %all-gather.2.cloned.1.call-done = bf16[2048,288]{0,1:T(8,128)(2,1)} async-done(((bf16[256,288]{0,1:T(8,128)(2,1)}), bf16[2048,288]{0,1:T(8,128)(2,1)}) %all-gather.2.cloned.1.call-update) | async-done | bytes 1179664 | tf_op jit(solution)/shard_map/all_gather | solution.py:102
  76.3 1.6 %convolution_convert_fusion.1 = bf16[2048,128]{0,1:T(8,128)(2,1)S(1)} fusion(bf16[2048,288]{0,1:T(8,128)(2,1)} %all-gather.2.cloned.1.call-done, bf16[256,1024]{1,0:T(8,128)(2,1)} %param.19, s32[]{:T(128)S(6)} %select_n.43), kind=kOutput, calls=%fused_computation.15 | convolution fusion | flops 134479872 | bytes 1638404 | tf_op jit(solution)/shard_map/dot_general | solution.py:96
  78.1 3.2 %while.17 = (s32[]{:T(128)}, f32[256]{0:T(256)S(1)}, f32[256]{0:T(256)S(1)}, f32[256,64]{0,1:T(8,128)S(1)}, pred[2048]{0:T(1024)(128)(4,1)S(1)}, /*index=5*/bf16...) while((s32[]{:T(128)}, f32[256]{0:T(256)S(1)}, ...), condition=%wide.region_10.11_spmd, body=%wide.region_7.10_spmd.sunk | while | flops 42893828 | bytes 1951407 | solution.py:159
  78.2 0.3 fusion.68
  79.0 0.3 fusion.68
  79.8 0.3 fusion.68
  80.2 0.2 convolution_add_fusion.2
  80.5 0.3 fusion.68
  81.0 0.2 convolution_add_fusion.2
  81.3 0.5 fusion.9
  81.8 1.5 %copy.46 = bf16[2560,256]{1,0:T(8,128)(2,1)} copy(bf16[2560,256]{0,1:T(8,128)(2,1)S(1)} %fusion.9) | data formatting | bytes 2621440
  83.3 37.5 %reduce-scatter.9.cloned.1.call-done = bf16[320,256]{1,0:T(8,128)(2,1)} async-done(((bf16[2560,256]{1,0:T(8,128)(2,1)}), bf16[320,256]{1,0:T(8,128)(2,1)}) %reduce-scatter.9.cloned.1.call-update) | async-done | bytes 163856
  (81 shorter events, 3.9 us)
Async XLA Ops:
  6.5 1.1 copy-start
  6.5 3.6 %copy-start.6 = (s32[4]{0:T(128)S(1)}, s32[4]{0:T(128)}, u32[]{:S(2)}) copy-start(s32[4]{0:T(128)} %param.25) | copy-start | bytes 52
  6.5 4.9 %copy-start.3 = (bf16[1,256,288]{1,2,0:T(8,128)(2,1)S(1)}, bf16[1,256,288]{1,2,0:T(8,128)(2,1)}, u32[]{:S(2)}) copy-start(bf16[1,256,288]{1,2,0:T(8,128)(2,1)} %param.21) | copy-start | bytes 442372
  6.5 43.6 %reduce-scatter.7.cloned.1.call-start = ((), (), s32[]{:S(2)}) async-start(), calls=%async_computation.3 | async-start | bytes 1327104
  10.1 21.8 %copy-start.7 = (s32[4]{0:T(128)S(1)}, s32[4]{0:T(128)}, u32[]{:S(2)}) copy-start(s32[4]{0:T(128)} %param.23) | copy-start | bytes 52
  10.1 23.6 %copy-start.8 = (s32[4]{0:T(128)S(1)}, s32[4]{0:T(128)}, u32[]{:S(2)}) copy-start(s32[4]{0:T(128)} %param.22) | copy-start | bytes 52
  10.1 42.3 %copy-start.5 = (f32[256]{0:T(256)S(1)}, f32[256]{0:T(256)}, u32[]{:S(2)}) copy-start(f32[256]{0:T(256)} %param.17) | copy-start | bytes 3076
  10.1 66.2 %all-gather.2.cloned.1.call-start = ((), (), s32[]{:S(2)}) async-start(), calls=%async_computation.2 | async-start | bytes 1327104 | tf_op jit(solution)/shard_map/all_gather | solution.py:102
  30.5 90.3 %reduce-scatter.9.cloned.1.call-start = ((), (), s32[]{:S(2)}) async-start(), calls=%async_computation.4 | async-start | bytes 1474560
  50.1 12.9 %slice-start.1 = ((f32[32,1056]{1,0:T(8,128)}), f32[32,768]{1,0:T(8,128)S(1)}, s32[]{:S(2)}) async-start(f32[32,1056]{1,0:T(8,128)} %reduce-scatter.7.cloned.1.call-done), calls=%async_computation.6 | async-start | bytes 196608 | tf_op jit(solution)/shard_map/slice | solution.py:72
  52.3 11.0 %copy-start.4 = (f32[768]{0:T(1024)S(1)}, f32[768]{0:T(1024)}, u32[]{:S(2)}) copy-start(f32[768]{0:T(1024)} %param.16) | copy-start | bytes 9220
  63.0 9.3 %copy-start.2 = (bf16[768,96]{0,1:T(8,128)(2,1)S(1)}, bf16[768,96]{0,1:T(8,128)(2,1)}, u32[]{:S(2)}) copy-start(bf16[768,96]{0,1:T(8,128)(2,1)} %param.18) | copy-start | bytes 442372
  76.3 1.7 %slice-start = ((bf16[2048,288]{0,1:T(8,128)(2,1)}), bf16[2048,32]{0,1:T(8,128)(2,1)S(1)}, s32[]{:S(2)}) async-start(bf16[2048,288]{0,1:T(8,128)(2,1)} %all-gather.2.cloned.1.call-done), calls=%async_computation.5 | async-start | bytes 262144 | tf_op jit(solution)/shard_map/slice | solution.py:99
  78.0 3.2 %copy-start.1 = (bf16[64,2560]{1,0:T(8,128)(2,1)S(1)}, bf16[64,2560]{1,0:T(8,128)(2,1)}, u32[]{:S(2)}) copy-start(bf16[64,2560]{1,0:T(8,128)(2,1)} %param.20) | copy-start | bytes 983044
Sparse Core Ops, SparseCore 0:
  10.6 39.5 reduce-scatter.6
  52.2 24.1 all-gather.1
  83.4 37.3 reduce-scatter.8
where the time goes:
time: 128 us; the launch traced here: 127 us
  waiting for transfers between devices  53.4 us (42%)
  blocking collectives  36 us (28%)
  between operations  15.9 us (12%)
  matrix products  8.44 us (7%)
  local copies, waits for them, and re-layouts  8.19 us (6%)
  other arithmetic  5.07 us (4%)
    unnamed x5, waiting for transfers between devices  50.4 us
    all_gather x1, blocking collectives, body(): segment = lax.all_gather(latent_cache, 'row', axis=0, tiled=True)  18.2 us
    all_gather x1, blocking collectives, body(): lax.all_gather(new_rows, 'col', axis=0, tiled=True)  9.18 us
    all_gather x1, blocking collectives, body(): lax.all_gather(query_latent, 'col', axis=0, tiled=True)  8.66 us
    unnamed x24, local copies, waits for them, and re-layouts  3.06 us
    all_gather x1, waiting for transfers between devices, body(): lax.all_gather(own_cache, 'col', axis=0, tiled=True)  2.96 us
    dot_general x2, matrix products, expand(): jnp.dot(latents[:, :kv_width], head_weight, preferred_element_type=jnp.fl...  2.68 us
  transfers between devices with their start and end apart: 3, of which 3 were waited for; matrix products, arithmetic and copies ran while one was open for 9% of the time, Pallas kernels for 0%

commit v1 on v0

v1 whole, which is shorter than its diff:
```python
import functools
import math

import jax
import jax.numpy as jnp
from jax import lax
from jax.experimental import pallas as pl
from jax.experimental.pallas import tpu as pltpu
from jax.sharding import PartitionSpec as P

NOPE = 64
ROPE = 32
VDIM = 64
HEAD = NOPE + VDIM
SPAN = 4
epsilon = 1e-05
MASKED = -1e30
FLOOR = -1e29

bf16 = jnp.bfloat16
f32 = jnp.float32
VMEM = pl.BlockSpec(memory_space=pltpu.VMEM)
SMEM = pl.BlockSpec(memory_space=pltpu.SMEM)
PARAMS = pltpu.CompilerParams(vmem_limit_bytes=32 * 1024 * 1024)


def cost(flops, moved, special=0):
    return pl.CostEstimate(flops=flops, bytes_accessed=moved, transcendentals=special)


def angle_tables(positions, width):
    half_dim = width // 2
    frequency = 10000.0 ** (-2.0 * jnp.arange(half_dim, dtype=f32) / width)
    angles = positions.astype(f32)[:, None] * frequency[None, :]
    return (jnp.cos(angles), jnp.sin(angles))


def rotate(values, cosine, sine):
    half = ROPE // 2
    first, second = values[:, :half], values[:, half:]
    return jnp.concatenate(
        [first * cosine - second * sine, second * cosine + first * sine], axis=1
    )


def down_kernel(count, own, tokens_ref, w_ref, even_ref, odd_ref, sums):
    column = lax.axis_index("col")
    sums[...] = jnp.dot(tokens_ref[...], w_ref[...], preferred_element_type=f32)
    for j in range(count):
        start = pl.multiple_of((column ^ j) * own, own)
        target = odd_ref if j % 2 else even_ref
        target[j // 2] = sums[pl.ds(start, own), :].astype(bf16)


def norm_kernel(own, q_width, kv_width, cos_ref, sin_ref, q_gain_ref, kv_gain_ref, *refs):
    out_ref = refs[-1]
    column = lax.axis_index("col")
    total = refs[0][...].astype(f32)
    for ref in refs[1:-1]:
        total += ref[...].astype(f32)

    def scaled(values, gain):
        mean = jnp.mean(values * values, axis=-1, keepdims=True)
        return values * lax.rsqrt(mean + epsilon) * gain

    rows = pl.ds(pl.multiple_of(column * own, own), own)
    out_ref[:, :q_width] = scaled(total[:, :q_width], q_gain_ref[...]).astype(bf16)
    out_ref[:, q_width : q_width + kv_width] = scaled(
        total[:, q_width : q_width + kv_width], kv_gain_ref[...]
    ).astype(bf16)
    out_ref[:, q_width + kv_width :] = rotate(
        total[:, q_width + kv_width :], cos_ref[rows, :], sin_ref[rows, :]
    ).astype(bf16)


def split3(value):
    high = value.astype(bf16)
    rest = value - high.astype(f32)
    middle = rest.astype(bf16)
    low = (rest - middle.astype(f32)).astype(bf16)
    return [high, middle, low]


def attend_kernel(
    span, count, own, q_width, kv_width, merged,
    home_ref, cached_ref, live_ref, page_ref, cos_ref, sin_ref, w_kv_ref, *refs,
):
    heads = count // span
    weights, refs = refs[:heads], refs[heads:]
    blocks, refs = refs[:count], refs[count:]
    pieces, refs = refs[:span], refs[span:]
    outs, (query_rows, fresh, keys, limits) = refs[:-4], refs[-4:]
    column = lax.axis_index("col")
    slot = home_ref[lax.axis_index("row")]
    live = live_ref[lax.axis_index("row")]
    cached = cached_ref[slot]
    group = count * own
    piece = pieces[0].shape[0]
    page_count = page_ref.shape[1]
    page = piece * count // page_count
    held = piece * span
    for j in range(count):
        start = pl.multiple_of((column ^ j) * own, own)
        query_rows[pl.ds(start, own), :] = blocks[j][:, :q_width].astype(f32)
        if j < span:
            fresh[j * own : (j + 1) * own, :] = blocks[j][:, q_width:].astype(f32)
    for j in range(span):
        keys[j * piece : (j + 1) * piece, :] = pieces[j][...]
        offset = lax.broadcasted_iota(jnp.int32, (1, piece), 1)
        position = (column ^ j) * piece + offset
        page_id = position // page
        logical = jnp.zeros((1, piece), jnp.int32)
        for l in range(page_count):
            logical = jnp.where(page_id == page_ref[slot, l], l, logical)
        seen = logical * page + offset % page < cached
        limits[:, j * piece : (j + 1) * piece] = jnp.where(seen, 0.0, MASKED)
    keys[held:, :] = fresh[...].astype(bf16)
    query_id = lax.broadcasted_iota(jnp.int32, (group, span * own), 0)
    fresh_lane = lax.broadcasted_iota(jnp.int32, (1, span * own), 1)
    fresh_id = (column ^ (fresh_lane // own)) * own + fresh_lane % own
    fresh_bias = jnp.where((fresh_id <= query_id) & (fresh_id < live), 0.0, MASKED)
    latent = query_rows[...].astype(bf16)
    scale = 1.0 / math.sqrt(NOPE + ROPE)
    for k in range(heads):
        head = column ^ (k * span)
        lift = w_kv_ref[:, pl.ds(pl.multiple_of(head * HEAD, HEAD), HEAD)]
        projected = jnp.dot(latent, weights[k][...], preferred_element_type=f32)
        turned = rotate(projected[:, NOPE:], cos_ref[...], sin_ref[...]).astype(bf16)
        plain = lax.dot_general(
            projected[:, :NOPE].astype(bf16), lift[:, :NOPE],
            (((1,), (1,)), ((), ())), preferred_element_type=f32,
        ).astype(bf16)
        query = jnp.concatenate([plain, turned], axis=1)
        scores = lax.dot_general(
            query, keys[...], (((1,), (1,)), ((), ())), preferred_element_type=f32
        )
        old = scores[:, :held] + limits[...]
        new = scores[:, held:] + fresh_bias
        peak = jnp.maximum(jnp.max(old, 1, keepdims=True), jnp.max(new, 1, keepdims=True))
        peak = jnp.maximum(peak, FLOOR)
        old = jnp.exp((old - peak) * scale)
        new = jnp.exp((new - peak) * scale)
        total = jnp.sum(old, 1, keepdims=True) + jnp.sum(new, 1, keepdims=True)
        mixed = jnp.dot(
            old.astype(bf16), keys[:held, :kv_width], preferred_element_type=f32
        ) + jnp.dot(new.astype(bf16), keys[held:, :kv_width], preferred_element_type=f32)
        summed = jnp.dot(mixed.astype(bf16), lift, preferred_element_type=f32)
        if not merged:
            live_rows = lax.broadcasted_iota(jnp.int32, (group, 1), 0) < live
            outs[0][...] = jnp.where(live_rows, summed[:, NOPE:] / total, 0.0).astype(bf16)
        elif k == 0:
            outs[0][:, :NOPE] = summed[:, NOPE:]
            outs[0][:, NOPE : NOPE + 1] = peak
            outs[0][:, NOPE + 1 : NOPE + 2] = total
        else:
            outs[k][:, :VDIM] = summed[:, NOPE:].astype(bf16)
            for i, part in enumerate(split3(peak) + split3(total)):
                outs[k][:, VDIM + i : VDIM + i + 1] = part


def merge_kernel(live_ref, own_ref, *refs):
    out_ref = refs[-1]
    live = live_ref[lax.axis_index("row")]
    scale = 1.0 / math.sqrt(NOPE + ROPE)
    parts = [(own_ref[:, :VDIM], own_ref[:, VDIM : VDIM + 1], own_ref[:, VDIM + 1 : VDIM + 2])]
    for ref in refs[:-1]:
        lanes = [ref[:, VDIM + i : VDIM + i + 1].astype(f32) for i in range(6)]
        parts.append(
            (
                ref[:, :VDIM].astype(f32),
                lanes[0] + lanes[1] + lanes[2],
                lanes[3] + lanes[4] + lanes[5],
            )
        )
    peak = functools.reduce(jnp.maximum, [p[1] for p in parts])
    total = 0.0
    summed = 0.0
    for part in parts:
        factor = jnp.exp((part[1] - peak) * scale)
        total += part[2] * factor
        summed += part[0] * factor
    rows = lax.broadcasted_iota(jnp.int32, total.shape, 0)
    out_ref[...] = jnp.where(rows < live, summed / total, 0.0).astype(bf16)


def out_kernel(half, width, *refs):
    mine_ref, other_ref = refs[-2:]
    core = lax.axis_index("col") & 1
    total = 0.0
    for k in range(half):
        total += jnp.dot(refs[k][...], refs[half + k][...], preferred_element_type=f32)
    low, high = total[:, :width], total[:, width:]
    mine_ref[...] = jnp.where(core == 0, low, high)
    other_ref[...] = jnp.where(core == 0, high, low).astype(bf16)


def body(
    tokens, w_down, q_gain, kv_gain, w_q_up, w_kv_up, w_out, latent_cache,
    cache_len, new_len, page_table, home_slot,
):
    count = lax.axis_size("col")
    rows = lax.axis_size("row")
    column = lax.axis_index("col")
    row = lax.axis_index("row")
    group = tokens.shape[0]
    own = group // count
    q_width, kv_width, wide = q_gain.shape[0], kv_gain.shape[0], w_down.shape[1]
    span = min(SPAN, count)
    half = count // 2
    cols = w_out.shape[1] // count
    slot = home_slot[row]

    def swap(value, d):
        return lax.ppermute(value, "col", [(s, s ^ d) for s in range(count)])

    held = latent_cache[0]
    cache = held
    for d in range(1, rows):
        moved = lax.ppermute(held, "row", [(s, (s + d) % rows) for s in range(rows)])
        cache = jnp.where((row + rows - d) % rows == slot, moved, cache)

    def chip_columns(chip):
        return lax.dynamic_slice_in_dim(w_out, chip * 2 * cols, 2 * cols, 1)

    out_weights = [chip_columns(column // 2)] + [
        swap(chip_columns((column ^ d) // 2), d) for d in range(2, count, 2)
    ]
    query_weights = [w_q_up] + [swap(w_q_up, d) for d in range(span, count, span)]
    cosine, sine = angle_tables(cache_len[slot] + jnp.arange(group, dtype=jnp.int32), ROPE)

    even, odd = pl.pallas_call(
        functools.partial(down_kernel, count, own),
        out_shape=[jax.ShapeDtypeStruct((half, own, wide), bf16)] * 2,
        in_specs=[VMEM] * 2,
        out_specs=[VMEM] * 2,
        scratch_shapes=[pltpu.VMEM((group, wide), f32)],
        compiler_params=PARAMS,
        cost_estimate=cost(2 * group * tokens.shape[1] * wide, 2_000_000),
        name="down",
    )(tokens, w_down)
    paired = (even.astype(f32) + swap(odd, 1).astype(f32)).astype(bf16)
    partial = [paired[0]] + [swap(paired[k], 2 * k) for k in range(1, half)]
    block = pl.pallas_call(
        functools.partial(norm_kernel, own, q_width, kv_width),
        out_shape=jax.ShapeDtypeStruct((own, wide), bf16),
        in_specs=[VMEM] * (4 + half),
        out_specs=VMEM,
        compiler_params=PARAMS,
        cost_estimate=cost(1_000_000, 500_000),
        name="norm",
    )(cosine, sine, q_gain[None], kv_gain[None], *partial)

    blocks = [None] * count
    for d in range(0, count, 2):
        blocks[d] = swap(block, d) if d else block
        blocks[d + 1] = swap(blocks[d], 1)
    pieces = [None] * span
    for d in range(0, span, 2):
        pieces[d] = swap(cache, d) if d else cache
        pieces[d + 1] = swap(pieces[d], 1)

    merged = span < count
    heads = count // span
    if merged:
        shapes = [jax.ShapeDtypeStruct((group, 128), f32)] + [
            jax.ShapeDtypeStruct((group, 128), bf16)
        ] * (heads - 1)
    else:
        shapes = [jax.ShapeDtypeStruct((group, VDIM), bf16)]
    keys = span * (cache.shape[0] + own)
    states = pl.pallas_call(
        functools.partial(attend_kernel, span, count, own, q_width, kv_width, merged),
        out_shape=shapes,
        in_specs=[SMEM] * 4 + [VMEM] * (3 + heads + count + span),
        out_specs=[VMEM] * len(shapes),
        scratch_shapes=[
            pltpu.VMEM((group, q_width), f32),
            pltpu.VMEM((span * own, kv_width + ROPE), f32),
            pltpu.VMEM((keys, kv_width + ROPE), bf16),
            pltpu.VMEM((1, span * cache.shape[0]), f32),
        ],
        compiler_params=PARAMS,
        cost_estimate=cost(heads * 4 * group * keys * 300, 3_000_000, heads * group * keys),
        name="attend",
    )(
        home_slot, cache_len, new_len, page_table, cosine, sine, w_kv_up,
        *query_weights, *blocks, *pieces,
    )
    if merged:
        received = [swap(states[k], k * span) for k in range(1, heads)]
        attended = pl.pallas_call(
            merge_kernel,
            out_shape=jax.ShapeDtypeStruct((group, VDIM), bf16),
            in_specs=[SMEM] + [VMEM] * heads,
            out_specs=VMEM,
            compiler_params=PARAMS,
            cost_estimate=cost(1_000_000, 500_000),
            name="merge",
        )(new_len, states[0], *received)
    else:
        attended = states[0]
    gathered = [attended] + [swap(attended, d) for d in range(2, count, 2)]
    mine, other = pl.pallas_call(
        functools.partial(out_kernel, half, cols),
        out_shape=[
            jax.ShapeDtypeStruct((group, cols), f32),
            jax.ShapeDtypeStruct((group, cols), bf16),
        ],
        in_specs=[VMEM] * (2 * half),
        out_specs=[VMEM] * 2,
        compiler_params=PARAMS,
        cost_estimate=cost(2 * group * half * VDIM * 2 * cols, 1_000_000),
        name="out",
    )(*gathered, *out_weights)
    return (mine + swap(other, 1).astype(f32)).astype(bf16)


def solution(mesh):
    return jax.shard_map(
        body,
        mesh=mesh,
        in_specs=(
            P("row", "col"),
            P("col", None),
            P(),
            P(),
            P(None, "col"),
            P(),
            P("col", None),
            P("row", "col", None),
            P(),
            P(),
            P(),
            P(),
        ),
        out_specs=P("row", "col"),
        check_vma=False,
    )
```

time: 128 us -> 64.2 us (0.50)
  blocking collectives: 36 us -> 0 us
  waiting for transfers between devices: 53.4 us -> 19.5 us
  starting transfers between devices: 0.09 us -> 26.8 us
  between operations: 15.9 us -> 4.17 us
  matrix products: 8.44 us -> 0 us
  Pallas kernels: 0 us -> 6.13 us
  other arithmetic: 5.07 us -> 1.37 us
  local copies, waits for them, and re-layouts: 8.19 us -> 5.92 us
    unnamed x5 -> x0, waiting for transfers between devices: 50.4 us -> none
    all_gather x3 -> x0, blocking collectives: 36 us -> none  [the longest x1 18.2 us: body(): segment = lax.all_gather(latent_cache, 'row', axis=0, tiled=True)]
    ppermute x0 -> x26, starting transfers between devices: none -> 26.8 us  [the longest x23 20.9 us: swap(): return lax.ppermute(value, 'col', [(s, s ^ d) for s in range(count)])]
    ppermute x0 -> x26, waiting for transfers between devices: none -> 19.5 us  [the longest x23 13.3 us: swap(): return lax.ppermute(value, 'col', [(s, s ^ d) for s in range(count)])]
    pallas_call x0 -> x5, Pallas kernels: none -> 6.13 us  [the longest x1 3.81 us: body(): pl.pallas_call(functools.partial(attend_kernel, span, count, own, q_width...]
    dot_general x14 -> x0, matrix products: 6 us -> none  [the longest x2 2.68 us: expand(): jnp.dot(latents[:, :kv_width], head_weight, preferred_element_type=jnp.fl...]
    all_gather x1 -> x0, waiting for transfers between devices: 2.96 us -> none  [body(): lax.all_gather(own_cache, 'col', axis=0, tiled=True)]
    unnamed x1 -> x0, matrix products: 2.44 us -> none
  transfers between devices with their start and end apart: 3 -> 26, of which waited for: 3 -> 11; matrix products, arithmetic and copies ran while one was open for 9% -> 4% of each run, Pallas kernels for 0% -> 8%
where the time goes in v1:
time: 64.2 us; the launch traced here: 63.9 us
  starting transfers between devices  26.8 us (42%)
  waiting for transfers between devices  19.5 us (30%)
  Pallas kernels  6.13 us (10%)
  local copies, waits for them, and re-layouts  5.92 us (9%)
  between operations  4.17 us (6%)
  other arithmetic  1.37 us (2%)
    ppermute x23, starting transfers between devices, swap(): return lax.ppermute(value, 'col', [(s, s ^ d) for s in range(count)])  20.9 us
    ppermute x23, waiting for transfers between devices, swap(): return lax.ppermute(value, 'col', [(s, s ^ d) for s in range(count)])  13.3 us
    ppermute x3, waiting for transfers between devices, body(): lax.ppermute(held, 'row', [(s, (s + d) % rows) for s in range(rows)])  6.18 us
    ppermute x3, starting transfers between devices, body(): lax.ppermute(held, 'row', [(s, (s + d) % rows) for s in range(rows)])  5.95 us
    unnamed x25, local copies, waits for them, and re-layouts  3.89 us
    pallas_call x1, Pallas kernels, body(): pl.pallas_call(functools.partial(attend_kernel, span, count, own, q_width...  3.81 us
  transfers between devices with their start and end apart: 26, of which 11 were waited for; matrix products, arithmetic and copies ran while one was open for 4% of the time, Pallas kernels for 8%

profile of v1, /device:TPU:0, one launch (start us, length us, event | category | flops | bytes accessed | tf_op | source)
XLA Modules:
  0.0 63.9 jit_solution(9935768834018422531)
XLA Ops:
  0.0 1.1 %copy.20.tokens_ref = bf16[256,320]{1,0:T(8,128)(2,1)S(1)} copy(bf16[256,320]{0,1:T(8,128)(2,1)} %param.12) | data formatting | bytes 327680 | tf_op args[0]
  1.1 1.1 %copy-done = bf16[320,1056]{1,0:T(8,128)(2,1)S(1)} copy-done((bf16[320,1056]{1,0:T(8,128)(2,1)S(1)}, bf16[320,1056]{1,0:T(8,128)(2,1)}, u32[]{:S(2)}) %copy-start) | copy-done | bytes 675864
  3.4 4.9 %collective-permute-start.12 = (bf16[256,288]{1,0:T(8,128)(2,1)S(1)}, bf16[256,288]{1,0:T(8,128)(2,1)S(1)}, u32[]{:S(2)}, u32[]{:S(2)}) collective-permute-start(bf16[256,288]{1,0:T(8,128)(2,1)S(1)} %bitcast.14), channel_id=1, source_target_pairs={{0,24},{8,0},{16,8},{24,16},{1,25},{9,1},{17,9},{25,17},{2,26},{10... | collective-permute-start | bytes 442376 | tf_op jit(solution)/shard_map/ppermute | solution.py:219
  8.4 1.0 %collective-permute-start.14 = (bf16[256,288]{1,0:T(8,128)(2,1)S(1)}, bf16[256,288]{1,0:T(8,128)(2,1)S(1)}, u32[]{:S(2)}, u32[]{:S(2)}) collective-permute-start(bf16[256,288]{1,0:T(8,128)(2,1)S(1)} %bitcast.16), channel_id=1, source_target_pairs={{0,8},{8,16},{16,24},{24,0},{1,9},{9,17},{17,25},{25,1},{2,10},{10... | collective-permute-start | bytes 442376 | tf_op jit(solution)/shard_map/ppermute | solution.py:219
  9.6 1.6 %collective-permute-start = (bf16[768,96]{1,0:T(8,128)(2,1)S(1)}, bf16[768,96]{1,0:T(8,128)(2,1)S(1)}, u32[]{:S(2)}, u32[]{:S(2)}) collective-permute-start(bf16[768,96]{1,0:T(8,128)(2,1)S(1)} %copy.22.refs_0_), channel_id=1, source_target_pairs={{0,4},{1,5},{2,6},{3,7},{4,0},{5,1},{6,2},{7,3},{8,12},{9,13},{10,... | collective-permute-start | bytes 442376 | tf_op jit(solution)/shard_map/ppermute | solution.py:214
  11.2 0.7 %copy-done.5 = s32[4]{0:T(128)S(1)} copy-done((s32[4]{0:T(128)S(1)}, s32[4]{0:T(128)}, u32[]{:S(2)}) %copy-start.5) | copy-done | bytes 40
  11.8 0.6 dynamic_slice.18
  16.3 0.6 dynamic_slice.19
  16.9 0.7 %add_convert_fusion.2 = f32[256]{0:T(256)S(1)} fusion(s32[]{:T(128)} %bitcast.1), kind=kLoop, calls=%fused_computation.9 | loop fusion | flops 512 | bytes 1028 | tf_op jit(solution)/shard_map/convert_element_type | solution.py:34
  17.7 1.6 %collective-permute-start.2 = (bf16[32,1056]{1,0:T(8,128)(2,1)S(1)}, bf16[32,1056]{1,0:T(8,128)(2,1)S(1)}, u32[]{:S(2)}, u32[]{:S(2)}) collective-permute-start(bf16[32,1056]{1,0:T(8,128)(2,1)S(1)} %get-tuple-element.23), channel_id=1, source_target_pairs={{0,2},{1,3},{2,0},{3,1},{4,6},{5,7},{6,4},{7,5},{8,10},{9,11},{10,... | collective-permute-start | bytes 202760 | tf_op jit(solution)/shard_map/ppermute | solution.py:214
  19.3 6.2 %collective-permute-done.13 = bf16[256,288]{1,0:T(8,128)(2,1)S(1)} collective-permute-done((bf16[256,288]{1,0:T(8,128)(2,1)S(1)}, bf16[256,288]{1,0:T(8,128)(2,1)S(1)}, u32[]{:S(2)}, u32[]{:S(2)}) %collective-permute-start.13) | collective-permute-done | bytes 147488 | tf_op jit(solution)/shard_map/ppermute | solution.py:219
  25.5 1.6 %collective-permute-start.16 = (bf16[256,288]{1,0:T(8,128)(2,1)S(1)}, bf16[256,288]{1,0:T(8,128)(2,1)S(1)}, u32[]{:S(2)}, u32[]{:S(2)}) collective-permute-start(bf16[256,288]{1,0:T(8,128)(2,1)S(1)} %select_select_fusion.refs_10_), channel_id=1, source_target_pairs={{0,2},{1,3},{2,0},{3,1},{4,6},{5,7},{6,4},{7,5},{8,10},{9,11},{10,... | collective-permute-start | bytes 442376 | tf_op jit(solution)/shard_map/ppermute | solution.py:214
  27.1 1.5 %collective-permute-start.3 = (bf16[32,1056]{1,0:T(8,128)(2,1)S(1)}, bf16[32,1056]{1,0:T(8,128)(2,1)S(1)}, u32[]{:S(2)}, u32[]{:S(2)}) collective-permute-start(bf16[32,1056]{1,0:T(8,128)(2,1)S(1)} %get-tuple-element.22), channel_id=1, source_target_pairs={{0,4},{1,5},{2,6},{3,7},{4,0},{5,1},{6,2},{7,3},{8,12},{9,13},{10,... | collective-permute-start | bytes 202760 | tf_op jit(solution)/shard_map/ppermute | solution.py:214
  29.6 2.1 %collective-permute-done.3.refs_2_ = bf16[32,1056]{1,0:T(8,128)(2,1)S(1)} collective-permute-done((bf16[32,1056]{1,0:T(8,128)(2,1)S(1)}, bf16[32,1056]{1,0:T(8,128)(2,1)S(1)}, u32[]{:S(2)}, u32[]{:S(2)}) %collective-permute-start.3) | collective-permute-done | bytes 67616 | tf_op jit(solution)/shard_map/ppermute | solution.py:214
  31.8 2.6 %collective-permute-done.4.refs_3_ = bf16[32,1056]{1,0:T(8,128)(2,1)S(1)} collective-permute-done((bf16[32,1056]{1,0:T(8,128)(2,1)S(1)}, bf16[32,1056]{1,0:T(8,128)(2,1)S(1)}, u32[]{:S(2)}, u32[]{:S(2)}) %collective-permute-start.4) | collective-permute-done | bytes 67616 | tf_op jit(solution)/shard_map/ppermute | solution.py:214
  34.3 0.7 %copy-done.1 = f32[256]{0:T(256)S(1)} copy-done((f32[256]{0:T(256)S(1)}, f32[256]{0:T(256)}, u32[]{:S(2)}) %copy-start.1) | copy-done | bytes 1048
  35.2 1.5 %collective-permute-start.10 = (bf16[32,1056]{1,0:T(8,128)(2,1)S(1)}, bf16[32,1056]{1,0:T(8,128)(2,1)S(1)}, u32[]{:S(2)}, u32[]{:S(2)}) collective-permute-start(bf16[32,1056]{1,0:T(8,128)(2,1)S(1)} %norm.1.refs_2_), channel_id=1, source_target_pairs={{0,6},{1,7},{2,4},{3,5},{4,2},{5,3},{6,0},{7,1},{8,14},{9,15},{10,... | collective-permute-start | bytes 202760 | tf_op jit(solution)/shard_map/ppermute | solution.py:214
  37.2 1.5 %collective-permute-start.8 = (bf16[32,1056]{1,0:T(8,128)(2,1)S(1)}, bf16[32,1056]{1,0:T(8,128)(2,1)S(1)}, u32[]{:S(2)}, u32[]{:S(2)}) collective-permute-start(bf16[32,1056]{1,0:T(8,128)(2,1)S(1)} %norm.1.refs_2_), channel_id=1, source_target_pairs={{0,4},{1,5},{2,6},{3,7},{4,0},{5,1},{6,2},{7,3},{8,12},{9,13},{10,... | collective-permute-start | bytes 202760 | tf_op jit(solution)/shard_map/ppermute | solution.py:214
  39.2 1.6 %collective-permute-done.10.refs_8_ = bf16[32,1056]{1,0:T(8,128)(2,1)S(1)} collective-permute-done((bf16[32,1056]{1,0:T(8,128)(2,1)S(1)}, bf16[32,1056]{1,0:T(8,128)(2,1)S(1)}, u32[]{:S(2)}, u32[]{:S(2)}) %collective-permute-start.10) | collective-permute-done | bytes 67616 | tf_op jit(solution)/shard_map/ppermute | solution.py:214
  41.7 1.5 %collective-permute-start.22 = (bf16[64,640]{1,0:T(8,128)(2,1)S(1)}, bf16[64,640]{1,0:T(8,128)(2,1)S(1)}, u32[]{:S(2)}, u32[]{:S(2)}) collective-permute-start(bf16[64,640]{1,0:T(8,128)(2,1)S(1)} %get-tuple-element.18), channel_id=1, source_target_pairs={{0,2},{1,3},{2,0},{3,1},{4,6},{5,7},{6,4},{7,5},{8,10},{9,11},{10,... | collective-permute-start | bytes 245768 | tf_op jit(solution)/shard_map/ppermute | solution.py:214
  43.2 3.8 %attend.1 = (f32[256,128]{1,0:T(8,128)S(1)}, bf16[256,128]{1,0:T(8,128)(2,1)S(1)}) custom-call(s32[4]{0:T(128)S(1)} %copy-done.5, s32[4]{0:T(128)S(1)} %copy-done.6, s32[4]{0:T(128)S(1)} %copy-done.2, s32[4,32]{1,0:T(4,128)S(1)} %copy-done.4, f32[256,16]{1,0:T(8,128)S(1)} %get-tuple-element.26.cos_ref, f32[256,16]{1,0:T(8,128)S(1)} %get-tuple-element.25.sin_ref, ...), custom_call_target="tpu_custom_call" | custom-call | flops 707788800 | bytes 3000000 | tf_op jit(solution)/shard_map/attend/pallas_call | solution.py:271
  47.1 1.6 %collective-permute-start.18 = (bf16[256,128]{1,0:T(8,128)(2,1)S(1)}, bf16[256,128]{1,0:T(8,128)(2,1)S(1)}, u32[]{:S(2)}, u32[]{:S(2)}) collective-permute-start(bf16[256,128]{1,0:T(8,128)(2,1)S(1)} %get-tuple-element.14), channel_id=1, source_target_pairs={{0,4},{1,5},{2,6},{3,7},{4,0},{5,1},{6,2},{7,3},{8,12},{9,13},{10,... | collective-permute-start | bytes 196616 | tf_op jit(solution)/shard_map/ppermute | solution.py:214
  49.1 2.1 %collective-permute-start.24 = (bf16[64,640]{1,0:T(8,128)(2,1)S(1)}, bf16[64,640]{1,0:T(8,128)(2,1)S(1)}, u32[]{:S(2)}, u32[]{:S(2)}) collective-permute-start(bf16[64,640]{1,0:T(8,128)(2,1)S(1)} %get-tuple-element.17), channel_id=1, source_target_pairs={{0,6},{1,7},{2,4},{3,5},{4,2},{5,3},{6,0},{7,1},{8,14},{9,15},{10,... | collective-permute-start | bytes 245768 | tf_op jit(solution)/shard_map/ppermute | solution.py:214
  51.6 1.0 %merge.1.refs_0_ = bf16[256,64]{1,0:T(8,128)(2,1)S(1)} custom-call(s32[4]{0:T(128)S(1)} %copy-done.2, f32[256,128]{1,0:T(8,128)S(1)} %get-tuple-element.13.own_ref, bf16[256,128]{1,0:T(8,128)(2,1)S(1)} %collective-permute-done.18.refs_0_), custom_call_target="tpu_custom_call" | custom-call | flops 1000000 | bytes 500000 | tf_op jit(solution)/shard_map/merge/pallas_call | solution.py:291
  52.6 1.2 %collective-permute-start.19 = (bf16[256,64]{1,0:T(8,128)(2,1)S(1)}, bf16[256,64]{1,0:T(8,128)(2,1)S(1)}, u32[]{:S(2)}, u32[]{:S(2)}) collective-permute-start(bf16[256,64]{1,0:T(8,128)(2,1)S(1)} %merge.1.refs_0_), channel_id=1, source_target_pairs={{0,2},{1,3},{2,0},{3,1},{4,6},{5,7},{6,4},{7,5},{8,10},{9,11},{10,... | collective-permute-start | bytes 98312 | tf_op jit(solution)/shard_map/ppermute | solution.py:214
  53.9 1.9 %collective-permute-start.20 = (bf16[256,64]{1,0:T(8,128)(2,1)S(1)}, bf16[256,64]{1,0:T(8,128)(2,1)S(1)}, u32[]{:S(2)}, u32[]{:S(2)}) collective-permute-start(bf16[256,64]{1,0:T(8,128)(2,1)S(1)} %merge.1.refs_0_), channel_id=1, source_target_pairs={{0,4},{1,5},{2,6},{3,7},{4,0},{5,1},{6,2},{7,3},{8,12},{9,13},{10,... | collective-permute-start | bytes 98312 | tf_op jit(solution)/shard_map/ppermute | solution.py:214
  56.2 1.3 %collective-permute-done.19.refs_1_ = bf16[256,64]{1,0:T(8,128)(2,1)S(1)} collective-permute-done((bf16[256,64]{1,0:T(8,128)(2,1)S(1)}, bf16[256,64]{1,0:T(8,128)(2,1)S(1)}, u32[]{:S(2)}, u32[]{:S(2)}) %collective-permute-start.19) | collective-permute-done | bytes 32800 | tf_op jit(solution)/shard_map/ppermute | solution.py:214
  57.5 0.9 %collective-permute-done.20.refs_2_ = bf16[256,64]{1,0:T(8,128)(2,1)S(1)} collective-permute-done((bf16[256,64]{1,0:T(8,128)(2,1)S(1)}, bf16[256,64]{1,0:T(8,128)(2,1)S(1)}, u32[]{:S(2)}, u32[]{:S(2)}) %collective-permute-start.20) | collective-permute-done | bytes 32800 | tf_op jit(solution)/shard_map/ppermute | solution.py:214
  58.4 2.5 %collective-permute-done.21.refs_3_ = bf16[256,64]{1,0:T(8,128)(2,1)S(1)} collective-permute-done((bf16[256,64]{1,0:T(8,128)(2,1)S(1)}, bf16[256,64]{1,0:T(8,128)(2,1)S(1)}, u32[]{:S(2)}, u32[]{:S(2)}) %collective-permute-start.21) | collective-permute-done | bytes 32800 | tf_op jit(solution)/shard_map/ppermute | solution.py:214
  60.9 0.7 %out.1 = (f32[256,320]{1,0:T(8,128)S(1)}, bf16[256,320]{1,0:T(8,128)(2,1)S(1)}) custom-call(bf16[256,64]{1,0:T(8,128)(2,1)S(1)} %merge.1.refs_0_, bf16[256,64]{1,0:T(8,128)(2,1)S(1)} %collective-permute-done.19.refs_1_, bf16[256,64]{1,0:T(8,128)(2,1)S(1)} %collective-permute-done.20.refs_2_, bf16[256,64]{1,0:T(8,128)(2,1)S(1)} %collective-permute-done.21.refs_3_, ...), custom_call_target="tpu_custom_call" | custom-call | flops 83886080 | bytes 1000000 | tf_op jit(solution)/shard_map/out/pallas_call | solution.py:303
  61.6 1.4 %collective-permute-done.25 = bf16[256,320]{1,0:T(8,128)(2,1)S(1)} collective-permute-done((bf16[256,320]{1,0:T(8,128)(2,1)S(1)}, bf16[256,320]{1,0:T(8,128)(2,1)S(1)}, u32[]{:S(2)}, u32[]{:S(2)}) %collective-permute-start.25) | collective-permute-done | bytes 163872 | tf_op jit(solution)/shard_map/ppermute | solution.py:214
  63.1 0.8 %copy.23 = bf16[256,320]{0,1:T(8,128)(2,1)} copy(bf16[256,320]{1,0:T(8,128)(2,1)S(1)} %add_convert_fusion.1) | data formatting | bytes 327680 | tf_op jit(solution)/shard_map/convert_element_type | solution.py:315
  (62 shorter events, 6.2 us)
Async XLA Ops:
  1.1 1.1 %copy-start = (bf16[320,1056]{1,0:T(8,128)(2,1)S(1)}, bf16[320,1056]{1,0:T(8,128)(2,1)}, u32[]{:S(2)}) copy-start(bf16[320,1056]{1,0:T(8,128)(2,1)} %w_ref.1) | copy-start | bytes 2027524
  2.7 6.7 %copy-start.9 = (bf16[768,96]{0,1:T(8,128)(2,1)S(1)}, bf16[768,96]{0,1:T(8,128)(2,1)}, u32[]{:S(2)}) copy-start(bf16[768,96]{0,1:T(8,128)(2,1)} %param.16) | copy-start | bytes 442372
  2.7 14.8 %collective-permute-start.1 = (bf16[4,32,1056]{2,1,0:T(8,128)(2,1)S(1)}, bf16[4,32,1056]{2,1,0:T(8,128)(2,1)S(1)}, u32[]{:S(2)}, u32[]{:S(2)}) collective-permute-start(bf16[4,32,1056]{2,1,0:T(8,128)(2,1)S(1)} %get-tuple-element.12), channel_id=1, source_target_pairs={{0,1},{1,0},{2,3},{3,2},{4,5},{5,4},{6,7},{7,6},{8,9},{9,8},{10,11... | collective-permute-start | bytes 811016 | tf_op jit(solution)/shard_map/ppermute | solution.py:214
  3.4 15.8 %collective-permute-start.12 = (bf16[256,288]{1,0:T(8,128)(2,1)S(1)}, bf16[256,288]{1,0:T(8,128)(2,1)S(1)}, u32[]{:S(2)}, u32[]{:S(2)}) collective-permute-start(bf16[256,288]{1,0:T(8,128)(2,1)S(1)} %bitcast.14), channel_id=1, source_target_pairs={{0,24},{8,0},{16,8},{24,16},{1,25},{9,1},{17,9},{25,17},{2,26},{10... | collective-permute-start | bytes 442376 | tf_op jit(solution)/shard_map/ppermute | solution.py:219
  8.4 17.1 %collective-permute-start.13 = (bf16[256,288]{1,0:T(8,128)(2,1)S(1)}, bf16[256,288]{1,0:T(8,128)(2,1)S(1)}, u32[]{:S(2)}, u32[]{:S(2)}) collective-permute-start(bf16[256,288]{1,0:T(8,128)(2,1)S(1)} %bitcast.15), channel_id=1, source_target_pairs={{0,16},{8,24},{16,0},{24,8},{1,17},{9,25},{17,1},{25,9},{2,18},{10... | collective-permute-start | bytes 442376 | tf_op jit(solution)/shard_map/ppermute | solution.py:219
  8.4 17.1 %collective-permute-start.14 = (bf16[256,288]{1,0:T(8,128)(2,1)S(1)}, bf16[256,288]{1,0:T(8,128)(2,1)S(1)}, u32[]{:S(2)}, u32[]{:S(2)}) collective-permute-start(bf16[256,288]{1,0:T(8,128)(2,1)S(1)} %bitcast.16), channel_id=1, source_target_pairs={{0,8},{8,16},{16,24},{24,0},{1,9},{9,17},{17,25},{25,1},{2,10},{10... | collective-permute-start | bytes 442376 | tf_op jit(solution)/shard_map/ppermute | solution.py:219
  9.6 27.7 %collective-permute-start = (bf16[768,96]{1,0:T(8,128)(2,1)S(1)}, bf16[768,96]{1,0:T(8,128)(2,1)S(1)}, u32[]{:S(2)}, u32[]{:S(2)}) collective-permute-start(bf16[768,96]{1,0:T(8,128)(2,1)S(1)} %copy.22.refs_0_), channel_id=1, source_target_pairs={{0,4},{1,5},{2,6},{3,7},{4,0},{5,1},{6,2},{7,3},{8,12},{9,13},{10,... | collective-permute-start | bytes 442376 | tf_op jit(solution)/shard_map/ppermute | solution.py:214
  17.7 10.9 %collective-permute-start.2 = (bf16[32,1056]{1,0:T(8,128)(2,1)S(1)}, bf16[32,1056]{1,0:T(8,128)(2,1)S(1)}, u32[]{:S(2)}, u32[]{:S(2)}) collective-permute-start(bf16[32,1056]{1,0:T(8,128)(2,1)S(1)} %get-tuple-element.23), channel_id=1, source_target_pairs={{0,2},{1,3},{2,0},{3,1},{4,6},{5,7},{6,4},{7,5},{8,10},{9,11},{10,... | collective-permute-start | bytes 202760 | tf_op jit(solution)/shard_map/ppermute | solution.py:214
  25.5 13.2 %collective-permute-start.16 = (bf16[256,288]{1,0:T(8,128)(2,1)S(1)}, bf16[256,288]{1,0:T(8,128)(2,1)S(1)}, u32[]{:S(2)}, u32[]{:S(2)}) collective-permute-start(bf16[256,288]{1,0:T(8,128)(2,1)S(1)} %select_select_fusion.refs_10_), channel_id=1, source_target_pairs={{0,2},{1,3},{2,0},{3,1},{4,6},{5,7},{6,4},{7,5},{8,10},{9,11},{10,... | collective-permute-start | bytes 442376 | tf_op jit(solution)/shard_map/ppermute | solution.py:214
  27.1 11.7 %collective-permute-start.15 = (bf16[256,288]{1,0:T(8,128)(2,1)S(1)}, bf16[256,288]{1,0:T(8,128)(2,1)S(1)}, u32[]{:S(2)}, u32[]{:S(2)}) collective-permute-start(bf16[256,288]{1,0:T(8,128)(2,1)S(1)} %select_select_fusion.refs_10_), channel_id=1, source_target_pairs={{0,1},{1,0},{2,3},{3,2},{4,5},{5,4},{6,7},{7,6},{8,9},{9,8},{10,11... | collective-permute-start | bytes 442376 | tf_op jit(solution)/shard_map/ppermute | solution.py:214
  27.1 4.7 %collective-permute-start.3 = (bf16[32,1056]{1,0:T(8,128)(2,1)S(1)}, bf16[32,1056]{1,0:T(8,128)(2,1)S(1)}, u32[]{:S(2)}, u32[]{:S(2)}) collective-permute-start(bf16[32,1056]{1,0:T(8,128)(2,1)S(1)} %get-tuple-element.22), channel_id=1, source_target_pairs={{0,4},{1,5},{2,6},{3,7},{4,0},{5,1},{6,2},{7,3},{8,12},{9,13},{10,... | collective-permute-start | bytes 202760 | tf_op jit(solution)/shard_map/ppermute | solution.py:214
  28.6 5.7 %collective-permute-start.4 = (bf16[32,1056]{1,0:T(8,128)(2,1)S(1)}, bf16[32,1056]{1,0:T(8,128)(2,1)S(1)}, u32[]{:S(2)}, u32[]{:S(2)}) collective-permute-start(bf16[32,1056]{1,0:T(8,128)(2,1)S(1)} %get-tuple-element.21), channel_id=1, source_target_pairs={{0,6},{1,7},{2,4},{3,5},{4,2},{5,3},{6,0},{7,1},{8,14},{9,15},{10,... | collective-permute-start | bytes 202760 | tf_op jit(solution)/shard_map/ppermute | solution.py:214
  35.0 6.7 %copy-start.7 = (bf16[64,2560]{1,0:T(8,128)(2,1)S(1)}, bf16[64,2560]{1,0:T(8,128)(2,1)}, u32[]{:S(2)}) copy-start(bf16[64,2560]{1,0:T(8,128)(2,1)} %param.18) | copy-start | bytes 983044
  35.2 8.1 %copy-start.3 = (bf16[256,1024]{1,0:T(8,128)(2,1)S(1)}, bf16[256,1024]{1,0:T(8,128)(2,1)}, u32[]{:S(2)}) copy-start(bf16[256,1024]{1,0:T(8,128)(2,1)} %w_kv_ref.1) | copy-start | bytes 1572868
  35.2 5.7 %collective-permute-start.10 = (bf16[32,1056]{1,0:T(8,128)(2,1)S(1)}, bf16[32,1056]{1,0:T(8,128)(2,1)S(1)}, u32[]{:S(2)}, u32[]{:S(2)}) collective-permute-start(bf16[32,1056]{1,0:T(8,128)(2,1)S(1)} %norm.1.refs_2_), channel_id=1, source_target_pairs={{0,6},{1,7},{2,4},{3,5},{4,2},{5,3},{6,0},{7,1},{8,14},{9,15},{10,... | collective-permute-start | bytes 202760 | tf_op jit(solution)/shard_map/ppermute | solution.py:214
  36.7 4.4 %collective-permute-start.6 = (bf16[32,1056]{1,0:T(8,128)(2,1)S(1)}, bf16[32,1056]{1,0:T(8,128)(2,1)S(1)}, u32[]{:S(2)}, u32[]{:S(2)}) collective-permute-start(bf16[32,1056]{1,0:T(8,128)(2,1)S(1)} %norm.1.refs_2_), channel_id=1, source_target_pairs={{0,2},{1,3},{2,0},{3,1},{4,6},{5,7},{6,4},{7,5},{8,10},{9,11},{10,... | collective-permute-start | bytes 202760 | tf_op jit(solution)/shard_map/ppermute | solution.py:214
  37.2 4.4 %collective-permute-start.8 = (bf16[32,1056]{1,0:T(8,128)(2,1)S(1)}, bf16[32,1056]{1,0:T(8,128)(2,1)S(1)}, u32[]{:S(2)}, u32[]{:S(2)}) collective-permute-start(bf16[32,1056]{1,0:T(8,128)(2,1)S(1)} %norm.1.refs_2_), channel_id=1, source_target_pairs={{0,4},{1,5},{2,6},{3,7},{4,0},{5,1},{6,2},{7,3},{8,12},{9,13},{10,... | collective-permute-start | bytes 202760 | tf_op jit(solution)/shard_map/ppermute | solution.py:214
  38.7 4.5 %collective-permute-start.17 = (bf16[256,288]{1,0:T(8,128)(2,1)S(1)}, bf16[256,288]{1,0:T(8,128)(2,1)S(1)}, u32[]{:S(2)}, u32[]{:S(2)}) collective-permute-start(bf16[256,288]{1,0:T(8,128)(2,1)S(1)} %collective-permute-done.16.refs_12_), channel_id=1, source_target_pairs={{0,1},{1,0},{2,3},{3,2},{4,5},{5,4},{6,7},{7,6},{8,9},{9,8},{10,11... | collective-permute-start | bytes 442376 | tf_op jit(solution)/shard_map/ppermute | solution.py:214
  38.7 4.5 %copy-start.4 = (s32[4,32]{1,0:T(4,128)S(1)}, s32[4,32]{1,0:T(4,128)}, u32[]{:S(2)}) copy-start(s32[4,32]{1,0:T(4,128)} %page_ref.1) | copy-start | bytes 1540
  38.7 3.0 %collective-permute-start.5 = (bf16[32,1056]{1,0:T(8,128)(2,1)S(1)}, bf16[32,1056]{1,0:T(8,128)(2,1)S(1)}, u32[]{:S(2)}, u32[]{:S(2)}) collective-permute-start(bf16[32,1056]{1,0:T(8,128)(2,1)S(1)} %norm.1.refs_2_), channel_id=1, source_target_pairs={{0,1},{1,0},{2,3},{3,2},{4,5},{5,4},{6,7},{7,6},{8,9},{9,8},{10,11... | collective-permute-start | bytes 202760 | tf_op jit(solution)/shard_map/ppermute | solution.py:214
  40.9 2.3 %collective-permute-start.11 = (bf16[32,1056]{1,0:T(8,128)(2,1)S(1)}, bf16[32,1056]{1,0:T(8,128)(2,1)S(1)}, u32[]{:S(2)}, u32[]{:S(2)}) collective-permute-start(bf16[32,1056]{1,0:T(8,128)(2,1)S(1)} %collective-permute-done.10.refs_8_), channel_id=1, source_target_pairs={{0,1},{1,0},{2,3},{3,2},{4,5},{5,4},{6,7},{7,6},{8,9},{9,8},{10,11... | collective-permute-start | bytes 202760 | tf_op jit(solution)/shard_map/ppermute | solution.py:214
  41.0 2.2 %collective-permute-start.7 = (bf16[32,1056]{1,0:T(8,128)(2,1)S(1)}, bf16[32,1056]{1,0:T(8,128)(2,1)S(1)}, u32[]{:S(2)}, u32[]{:S(2)}) collective-permute-start(bf16[32,1056]{1,0:T(8,128)(2,1)S(1)} %collective-permute-done.6.refs_4_), channel_id=1, source_target_pairs={{0,1},{1,0},{2,3},{3,2},{4,5},{5,4},{6,7},{7,6},{8,9},{9,8},{10,11... | collective-permute-start | bytes 202760 | tf_op jit(solution)/shard_map/ppermute | solution.py:214
  41.6 1.5 %collective-permute-start.9 = (bf16[32,1056]{1,0:T(8,128)(2,1)S(1)}, bf16[32,1056]{1,0:T(8,128)(2,1)S(1)}, u32[]{:S(2)}, u32[]{:S(2)}) collective-permute-start(bf16[32,1056]{1,0:T(8,128)(2,1)S(1)} %collective-permute-done.8.refs_6_), channel_id=1, source_target_pairs={{0,1},{1,0},{2,3},{3,2},{4,5},{5,4},{6,7},{7,6},{8,9},{9,8},{10,11... | collective-permute-start | bytes 202760 | tf_op jit(solution)/shard_map/ppermute | solution.py:214
  41.7 1.5 %copy-start.2 = (s32[4]{0:T(128)S(1)}, s32[4]{0:T(128)}, u32[]{:S(2)}) copy-start(s32[4]{0:T(128)} %live_ref.3) | copy-start | bytes 52
  41.7 14.0 %collective-permute-start.22 = (bf16[64,640]{1,0:T(8,128)(2,1)S(1)}, bf16[64,640]{1,0:T(8,128)(2,1)S(1)}, u32[]{:S(2)}, u32[]{:S(2)}) collective-permute-start(bf16[64,640]{1,0:T(8,128)(2,1)S(1)} %get-tuple-element.18), channel_id=1, source_target_pairs={{0,2},{1,3},{2,0},{3,1},{4,6},{5,7},{6,4},{7,5},{8,10},{9,11},{10,... | collective-permute-start | bytes 245768 | tf_op jit(solution)/shard_map/ppermute | solution.py:214
  47.1 4.6 %collective-permute-start.18 = (bf16[256,128]{1,0:T(8,128)(2,1)S(1)}, bf16[256,128]{1,0:T(8,128)(2,1)S(1)}, u32[]{:S(2)}, u32[]{:S(2)}) collective-permute-start(bf16[256,128]{1,0:T(8,128)(2,1)S(1)} %get-tuple-element.14), channel_id=1, source_target_pairs={{0,4},{1,5},{2,6},{3,7},{4,0},{5,1},{6,2},{7,3},{8,12},{9,13},{10,... | collective-permute-start | bytes 196616 | tf_op jit(solution)/shard_map/ppermute | solution.py:214
  48.6 7.5 %collective-permute-start.23 = (bf16[64,640]{1,0:T(8,128)(2,1)S(1)}, bf16[64,640]{1,0:T(8,128)(2,1)S(1)}, u32[]{:S(2)}, u32[]{:S(2)}) collective-permute-start(bf16[64,640]{1,0:T(8,128)(2,1)S(1)} %get-tuple-element.20), channel_id=1, source_target_pairs={{0,4},{1,5},{2,6},{3,7},{4,0},{5,1},{6,2},{7,3},{8,12},{9,13},{10,... | collective-permute-start | bytes 245768 | tf_op jit(solution)/shard_map/ppermute | solution.py:214
  49.1 7.0 %collective-permute-start.24 = (bf16[64,640]{1,0:T(8,128)(2,1)S(1)}, bf16[64,640]{1,0:T(8,128)(2,1)S(1)}, u32[]{:S(2)}, u32[]{:S(2)}) collective-permute-start(bf16[64,640]{1,0:T(8,128)(2,1)S(1)} %get-tuple-element.17), channel_id=1, source_target_pairs={{0,6},{1,7},{2,4},{3,5},{4,2},{5,3},{6,0},{7,1},{8,14},{9,15},{10,... | collective-permute-start | bytes 245768 | tf_op jit(solution)/shard_map/ppermute | solution.py:214
  52.6 4.9 %collective-permute-start.19 = (bf16[256,64]{1,0:T(8,128)(2,1)S(1)}, bf16[256,64]{1,0:T(8,128)(2,1)S(1)}, u32[]{:S(2)}, u32[]{:S(2)}) collective-permute-start(bf16[256,64]{1,0:T(8,128)(2,1)S(1)} %merge.1.refs_0_), channel_id=1, source_target_pairs={{0,2},{1,3},{2,0},{3,1},{4,6},{5,7},{6,4},{7,5},{8,10},{9,11},{10,... | collective-permute-start | bytes 98312 | tf_op jit(solution)/shard_map/ppermute | solution.py:214
  53.9 4.5 %collective-permute-start.20 = (bf16[256,64]{1,0:T(8,128)(2,1)S(1)}, bf16[256,64]{1,0:T(8,128)(2,1)S(1)}, u32[]{:S(2)}, u32[]{:S(2)}) collective-permute-start(bf16[256,64]{1,0:T(8,128)(2,1)S(1)} %merge.1.refs_0_), channel_id=1, source_target_pairs={{0,4},{1,5},{2,6},{3,7},{4,0},{5,1},{6,2},{7,3},{8,12},{9,13},{10,... | collective-permute-start | bytes 98312 | tf_op jit(solution)/shard_map/ppermute | solution.py:214
  55.7 5.2 %collective-permute-start.21 = (bf16[256,64]{1,0:T(8,128)(2,1)S(1)}, bf16[256,64]{1,0:T(8,128)(2,1)S(1)}, u32[]{:S(2)}, u32[]{:S(2)}) collective-permute-start(bf16[256,64]{1,0:T(8,128)(2,1)S(1)} %merge.1.refs_0_), channel_id=1, source_target_pairs={{0,6},{1,7},{2,4},{3,5},{4,2},{5,3},{6,0},{7,1},{8,14},{9,15},{10,... | collective-permute-start | bytes 98312 | tf_op jit(solution)/shard_map/ppermute | solution.py:214
  61.6 1.5 %collective-permute-start.25 = (bf16[256,320]{1,0:T(8,128)(2,1)S(1)}, bf16[256,320]{1,0:T(8,128)(2,1)S(1)}, u32[]{:S(2)}, u32[]{:S(2)}) collective-permute-start(bf16[256,320]{1,0:T(8,128)(2,1)S(1)} %get-tuple-element.16), channel_id=1, source_target_pairs={{0,1},{1,0},{2,3},{3,2},{4,5},{5,4},{6,7},{7,6},{8,9},{9,8},{10,11... | collective-permute-start | bytes 491528 | tf_op jit(solution)/shard_map/ppermute | solution.py:214
  (5 other events, 4.1 us)

commit v2 on v1

v2 whole, which is shorter than its diff:
```python
import functools
import math

import jax
import jax.numpy as jnp
from jax import lax
from jax.experimental import pallas as pl
from jax.experimental.pallas import tpu as pltpu
from jax.sharding import PartitionSpec as P

NOPE = 64
ROPE = 32
VDIM = 64
HEAD = NOPE + VDIM
SPAN = 4
epsilon = 1e-05
MASKED = -1e30
FLOOR = -1e29

bf16 = jnp.bfloat16
f32 = jnp.float32
VMEM = pl.BlockSpec(memory_space=pltpu.VMEM)
SMEM = pl.BlockSpec(memory_space=pltpu.SMEM)
PARAMS = pltpu.CompilerParams(vmem_limit_bytes=32 * 1024 * 1024)


def cost(flops, moved, special=0):
    return pl.CostEstimate(flops=flops, bytes_accessed=moved, transcendentals=special)


def rotate(values, cosine, sine, axis):
    half = ROPE // 2
    first = lax.slice_in_dim(values, 0, half, axis=axis)
    second = lax.slice_in_dim(values, half, 2 * half, axis=axis)
    return jnp.concatenate(
        [first * cosine - second * sine, second * cosine + first * sine], axis=axis
    )


def down_kernel(count, own, tokens_ref, w_ref, even_ref, odd_ref, sums):
    column = lax.axis_index("col")
    sums[...] = lax.dot_general(
        tokens_ref[...], w_ref[...], (((0,), (0,)), ((), ())), preferred_element_type=f32
    )
    for j in range(count):
        start = pl.multiple_of((column ^ j) * own, own)
        target = odd_ref if j % 2 else even_ref
        target[j // 2] = sums[pl.ds(start, own), :].astype(bf16)


def prepare_kernel(
    span, count, own, page, home_ref, cached_ref, live_ref, page_ref, w_out_ref,
    own_cos, own_sin, cosine, sine, limits, fresh_limits, alive, choice, *refs,
):
    columns, logical = refs[:-1], refs[-1]
    column = lax.axis_index("col")
    row = lax.axis_index("row")
    slot = home_ref[row]
    live = live_ref[row]
    cached = cached_ref[slot]
    rows = choice.shape[0]
    group = count * own
    half = ROPE // 2
    rate = -2.0 * math.log(10000.0) / ROPE

    place = cached + column * own + lax.broadcasted_iota(jnp.int32, (own, half), 0)
    step = lax.broadcasted_iota(jnp.int32, (own, half), 1).astype(f32)
    angle = place.astype(f32) * jnp.exp(step * rate)
    own_cos[...] = jnp.cos(angle)
    own_sin[...] = jnp.sin(angle)
    place = cached + lax.broadcasted_iota(jnp.int32, (half, group), 1)
    step = lax.broadcasted_iota(jnp.int32, (half, group), 0).astype(f32)
    angle = place.astype(f32) * jnp.exp(step * rate)
    cosine[...] = jnp.cos(angle)
    sine[...] = jnp.sin(angle)

    for l in range(page_ref.shape[1]):
        logical[page_ref[slot, l]] = l
    per_piece = limits.shape[0] // span // page
    offset = lax.broadcasted_iota(jnp.int32, (page, 128), 0)
    for j in range(span):
        for p in range(per_piece):
            seen = offset < cached - logical[(column ^ j) * per_piece + p] * page
            start = (j * per_piece + p) * page
            limits[start : start + page, :] = jnp.where(seen, 0.0, MASKED)
    query_id = lax.broadcasted_iota(jnp.int32, (own, group), 1)
    offset = lax.broadcasted_iota(jnp.int32, (own, group), 0)
    for j in range(span):
        fresh_id = (column ^ j) * own + offset
        seen = (fresh_id <= query_id) & (fresh_id < live)
        fresh_limits[j * own : (j + 1) * own, :] = jnp.where(seen, 0.0, MASKED)
    token = lax.broadcasted_iota(jnp.int32, (1, group), 1)
    alive[...] = jnp.where(token < live, 1.0, 0.0)
    source = lax.broadcasted_iota(jnp.int32, choice.shape, 0)
    source = jnp.where(row >= source, row - source, row - source + rows)
    choice[...] = jnp.where(source == slot, 1.0, 0.0)

    width = columns[0].shape[1]
    for i, ref in enumerate(columns):
        start = ((column // 2) ^ i) * width
        if width % 128 == 0:
            ref[...] = w_out_ref[:, pl.ds(pl.multiple_of(start, 128), width)]
        else:
            taken = w_out_ref[:, :width]
            for chip in range(1, count // 2):
                taken = jnp.where(
                    (column // 2) ^ i == chip, w_out_ref[:, chip * width : (chip + 1) * width], taken
                )
            ref[...] = taken


def norm_kernel(q_width, kv_width, cos_ref, sin_ref, q_gain_ref, kv_gain_ref, *refs):
    out_ref = refs[-1]
    total = refs[0][...].astype(f32)
    for ref in refs[1:-1]:
        total += ref[...].astype(f32)

    def scaled(values, gain):
        mean = jnp.mean(values * values, axis=-1, keepdims=True)
        return values * lax.rsqrt(mean + epsilon) * gain

    out_ref[:, :q_width] = scaled(total[:, :q_width], q_gain_ref[...]).astype(bf16)
    out_ref[:, q_width : q_width + kv_width] = scaled(
        total[:, q_width : q_width + kv_width], kv_gain_ref[...]
    ).astype(bf16)
    out_ref[:, q_width + kv_width :] = rotate(
        total[:, q_width + kv_width :], cos_ref[...], sin_ref[...], 1
    ).astype(bf16)


def split3(value):
    high = value.astype(bf16).astype(f32)
    middle = (value - high).astype(bf16).astype(f32)
    return [high, middle, value - high - middle]


def attend_kernel(span, count, own, q_width, kv_width, cos_ref, sin_ref, limits, fresh_limits, w_kv_ref, *refs):
    heads = count // span
    weights, refs = refs[:heads], refs[heads:]
    blocks, refs = refs[:count], refs[count:]
    pieces, (out_ref, query_rows, fresh, keys) = refs[:span], refs[span:]
    column = lax.axis_index("col")
    group = count * own
    piece = pieces[0].shape[1]
    held = span * piece
    for j in range(count):
        start = pl.multiple_of((column ^ j) * own, own)
        query_rows[pl.ds(start, own), :] = blocks[j][:, :q_width].astype(f32)
        if j < span:
            fresh[j * own : (j + 1) * own, :] = blocks[j][:, q_width:].astype(f32)
    for j in range(span):
        keys[:, j * piece : (j + 1) * piece] = pieces[j][...]
    fresh_keys = fresh[...].astype(bf16)
    latent = query_rows[...].astype(bf16)
    scale = 1.0 / math.sqrt(NOPE + ROPE)
    stats = []
    for k in range(heads):
        head = column ^ (k * span)
        lift = w_kv_ref[:, pl.ds(pl.multiple_of(head * HEAD, HEAD), HEAD)]
        projected = lax.dot_general(
            weights[k][...], latent, (((1,), (1,)), ((), ())), preferred_element_type=f32
        )
        turned = rotate(projected[NOPE:], cos_ref[...], sin_ref[...], 0)
        plain = jnp.dot(
            lift[:, :NOPE], projected[:NOPE].astype(bf16), preferred_element_type=f32
        )
        query = jnp.concatenate([plain.astype(bf16), turned.astype(bf16)], axis=0)
        old = lax.dot_general(
            keys[...], query, (((0,), (0,)), ((), ())), preferred_element_type=f32
        )
        old += jnp.concatenate([limits[...]] * (group // 128), axis=1)
        new = jnp.dot(fresh_keys, query, preferred_element_type=f32) + fresh_limits[...]
        peak = jnp.maximum(jnp.max(old, 0, keepdims=True), jnp.max(new, 0, keepdims=True))
        peak = jnp.maximum(peak, FLOOR)
        old = jnp.exp((old - peak) * scale)
        new = jnp.exp((new - peak) * scale)
        total = jnp.sum(old, 0, keepdims=True) + jnp.sum(new, 0, keepdims=True)
        mixed = jnp.dot(
            keys[:kv_width, :], old.astype(bf16), preferred_element_type=f32
        ) + lax.dot_general(
            fresh_keys[:, :kv_width], new.astype(bf16),
            (((0,), (0,)), ((), ())), preferred_element_type=f32,
        )
        summed = lax.dot_general(
            lift, mixed.astype(bf16), (((0,), (0,)), ((), ())), preferred_element_type=f32
        )
        out_ref[k * VDIM : (k + 1) * VDIM, :] = summed[NOPE:].astype(bf16)
        stats += split3(peak) + split3(total) + [jnp.zeros_like(total)] * 2
    out_ref[heads * VDIM :, :] = jnp.concatenate(stats, axis=0).astype(bf16)


def out_kernel(span, count, width, alive_ref, *refs):
    half = count // 2
    heads = count // span
    columns, refs = refs[:half], refs[half:]
    states, (mine_ref, other_ref, attended, weights) = refs[:half], refs[half:]
    scale = 1.0 / math.sqrt(NOPE + ROPE)
    for i in range(half):
        weights[i * VDIM : (i + 1) * VDIM, :] = columns[i][...]
        parts = []
        for k in range(heads):
            ref = states[i ^ (k * span // 2)]
            lanes = ref[heads * VDIM :, :].astype(f32)[8 * k : 8 * k + 6]
            parts.append(
                (
                    ref[k * VDIM : (k + 1) * VDIM, :].astype(f32),
                    lanes[0:1] + lanes[1:2] + lanes[2:3],
                    lanes[3:4] + lanes[4:5] + lanes[5:6],
                )
            )
        peak = functools.reduce(jnp.maximum, [p[1] for p in parts])
        total = 0.0
        summed = 0.0
        for part in parts:
            factor = jnp.exp((part[1] - peak) * scale)
            total += part[2] * factor
            summed += part[0] * factor
        factor = jnp.where(alive_ref[...] > 0, 1.0 / total, 0.0)
        attended[i * VDIM : (i + 1) * VDIM, :] = (summed * factor).astype(bf16)
    product = lax.dot_general(
        weights[...], attended[...], (((0,), (0,)), ((), ())), preferred_element_type=f32
    )
    low, high = product[:width], product[width:]
    core = lax.axis_index("col") & 1
    mine_ref[...] = jnp.where(core == 0, low, high)
    other_ref[...] = jnp.where(core == 0, high, low).astype(bf16)


def body(
    tokens, w_down, q_gain, kv_gain, w_q_up, w_kv_up, w_out, latent_cache,
    cache_len, new_len, page_table, home_slot,
):
    count = lax.axis_size("col")
    rows = lax.axis_size("row")
    group = tokens.shape[0]
    own = group // count
    q_width, kv_width, wide = q_gain.shape[0], kv_gain.shape[0], w_down.shape[1]
    span = min(SPAN, count)
    half = count // 2
    heads = count // span
    cols = w_out.shape[1] // count
    piece = latent_cache.shape[1]
    page = piece * count // page_table.shape[1]

    def swap(value, d):
        return lax.ppermute(value, "col", [(s, s ^ d) for s in range(count)])

    def call(kernel, name, shapes, operands, scratch=(), scalars=0):
        single = not isinstance(shapes, list)
        return pl.pallas_call(
            kernel,
            out_shape=shapes,
            in_specs=[SMEM] * scalars + [VMEM] * (len(operands) - scalars),
            out_specs=VMEM if single else [VMEM] * len(shapes),
            scratch_shapes=list(scratch),
            compiler_params=PARAMS,
            cost_estimate=cost(1000, 1000),
            name=name,
        )(*operands)

    shape = jax.ShapeDtypeStruct
    held = latent_cache[0].T
    moved = [
        lax.ppermute(held, "row", [(s, (s + d) % rows) for s in range(rows)])
        for d in range(1, rows)
    ]
    query_weights = [w_q_up.T] + [swap(w_q_up.T, d) for d in range(span, count, span)]
    even, odd = call(
        functools.partial(down_kernel, count, own), "down",
        [shape((half, own, wide), bf16)] * 2, (tokens.T, w_down),
        [pltpu.VMEM((group, wide), f32)],
    )
    paired = (even.astype(f32) + swap(odd, 1).astype(f32)).astype(bf16)
    paired, w_out, home_slot = lax.optimization_barrier((paired, w_out, home_slot))
    partial = [paired[0]] + [swap(paired[k], 2 * k) for k in range(1, half)]
    own_cos, own_sin, cosine, sine, limits, fresh_limits, alive, choice, *columns = call(
        functools.partial(prepare_kernel, span, count, own, page), "prepare",
        [shape((own, ROPE // 2), f32)] * 2
        + [shape((ROPE // 2, group), f32)] * 2
        + [shape((span * piece, 128), f32), shape((span * own, group), f32)]
        + [shape((1, group), f32), shape((rows, group), f32)]
        + [shape((w_out.shape[0], 2 * cols), bf16)] * half,
        (home_slot, cache_len, new_len, page_table, w_out),
        [pltpu.SMEM((page_table.shape[1],), jnp.int32)], 4,
    )
    columns = columns[:1] + [swap(columns[i], 2 * i) for i in range(1, half)]
    block = call(
        functools.partial(norm_kernel, q_width, kv_width), "norm", shape((own, wide), bf16),
        (own_cos, own_sin, q_gain[None], kv_gain[None], *partial),
    )
    block, *moved = lax.optimization_barrier((block, *moved))
    cache = held
    for d in range(1, rows):
        cache = jnp.where(choice[d, :piece] > 0, moved[d - 1], cache)
    blocks = [None] * count
    for d in range(0, count, 2):
        blocks[d] = swap(block, d) if d else block
        blocks[d + 1] = swap(blocks[d], 1)
    pieces = [None] * span
    for d in range(0, span, 2):
        pieces[d] = swap(cache, d) if d else cache
        pieces[d + 1] = swap(pieces[d], 1)
    state = call(
        functools.partial(attend_kernel, span, count, own, q_width, kv_width), "attend",
        shape((heads * (VDIM + 8), group), bf16),
        (cosine, sine, limits, fresh_limits, w_kv_up, *query_weights, *blocks, *pieces),
        [
            pltpu.VMEM((group, q_width), f32),
            pltpu.VMEM((span * own, kv_width + ROPE), f32),
            pltpu.VMEM((kv_width + ROPE, span * piece), bf16),
        ],
    )
    states = [state] + [swap(state, d) for d in range(2, count, 2)]
    mine, other = call(
        functools.partial(out_kernel, span, count, cols), "out",
        [shape((cols, group), f32), shape((cols, group), bf16)],
        (alive, *columns, *states),
        [
            pltpu.VMEM((half * VDIM, group), bf16),
            pltpu.VMEM((half * VDIM, 2 * cols), bf16),
        ],
    )
    return (mine + swap(other, 1).astype(f32)).astype(bf16).T


def solution(mesh):
    return jax.shard_map(
        body,
        mesh=mesh,
        in_specs=(
            P("row", "col"),
            P("col", None),
            P(),
            P(),
            P(None, "col"),
            P(),
            P("col", None),
            P("row", "col", None),
            P(),
            P(),
            P(),
            P(),
        ),
        out_specs=P("row", "col"),
        check_vma=False,
    )
```

time: 64.2 us -> 51 us (0.79)
  between operations: 4.17 us -> 0.16 us
  starting transfers between devices: 26.8 us -> 23.2 us
  local copies, waits for them, and re-layouts: 5.92 us -> 2.85 us
  waiting for transfers between devices: 19.5 us -> 18.1 us
    ppermute x23 -> x22, starting transfers between devices: 20.9 us -> 18.5 us  [swap(): return lax.ppermute(value, 'col', [(s, s ^ d) for s in range(count)])]
    ppermute x3, waiting for transfers between devices: 6.18 us -> 4.73 us  [body(): lax.ppermute(held, 'row', [(s, (s + d) % rows) for s in range(rows)])]
    ppermute x3, starting transfers between devices: 5.95 us -> 4.61 us  [body(): lax.ppermute(held, 'row', [(s, (s + d) % rows) for s in range(rows)])]
    dynamic_slice x3 -> x0, local copies, waits for them, and re-layouts: 1.2 us -> none  [the longest x1 0.59 us: body(): cache_len[slot] + jnp.arange(group, dtype=jnp.int32)]
    unnamed x25 -> x24, local copies, waits for them, and re-layouts: 3.89 us -> 2.82 us
    convert_element_type x1 -> x0, local copies, waits for them, and re-layouts: 0.8 us -> none  [body(): return (mine + swap(other, 1).astype(f32)).astype(bf16)]
    transpose x0 -> x1, other arithmetic: none -> 0.7 us  [body(): return (mine + swap(other, 1).astype(f32)).astype(bf16).T]
    convert_element_type x2 -> x0, other arithmetic: 0.7 us -> none  [the longest x1 0.65 us: angle_tables(): angles = positions.astype(f32)[:, None] * frequency[None, :]]
  transfers between devices with their start and end apart: 26 -> 25, of which waited for: 11 -> 12; matrix products, arithmetic and copies ran while one was open for 4% -> 0% of each run, Pallas kernels for 8% -> 9%
where the time goes in v2:
time: 51 us; the launch traced here: 50.8 us
  starting transfers between devices  23.2 us (45%)
  waiting for transfers between devices  18.1 us (35%)
  Pallas kernels  5.69 us (11%)
  local copies, waits for them, and re-layouts  2.85 us (6%)
  other arithmetic  0.84 us (2%)
    ppermute x22, starting transfers between devices, swap(): return lax.ppermute(value, 'col', [(s, s ^ d) for s in range(count)])  18.5 us
    ppermute x22, waiting for transfers between devices, swap(): return lax.ppermute(value, 'col', [(s, s ^ d) for s in range(count)])  13.4 us
    pallas_call x5, Pallas kernels, call(): pl.pallas_call(kernel, out_shape=shapes, in_specs=[SMEM] * scalars + [VME...  5.69 us
    ppermute x3, waiting for transfers between devices, body(): lax.ppermute(held, 'row', [(s, (s + d) % rows) for s in range(rows)])  4.73 us
    ppermute x3, starting transfers between devices, body(): lax.ppermute(held, 'row', [(s, (s + d) % rows) for s in range(rows)])  4.61 us
    unnamed x24, local copies, waits for them, and re-layouts  2.82 us
  transfers between devices with their start and end apart: 25, of which 12 were waited for; matrix products, arithmetic and copies ran while one was open for 0% of the time, Pallas kernels for 9%

profile of v2, /device:TPU:0, one launch (start us, length us, event | category | flops | bytes accessed | tf_op | source)
XLA Modules:
  0.0 50.8 jit_solution(14252583346210751818)
XLA Ops:
  0.0 1.1 %copy-done = bf16[320,1056]{1,0:T(8,128)(2,1)S(1)} copy-done((bf16[320,1056]{1,0:T(8,128)(2,1)S(1)}, bf16[320,1056]{1,0:T(8,128)(2,1)}, u32[]{:S(2)}) %copy-start) | copy-done | bytes 675864
  1.1 0.9 %copy-done.3 = bf16[256,320]{0,1:T(8,128)(2,1)S(1)} copy-done((bf16[256,320]{0,1:T(8,128)(2,1)S(1)}, bf16[256,320]{0,1:T(8,128)(2,1)}, u32[]{:S(2)}) %copy-start.3) | copy-done | bytes 163864
  2.0 0.6 %down.1 = (bf16[4,32,1056]{2,1,0:T(8,128)(2,1)S(1)}, bf16[4,32,1056]{2,1,0:T(8,128)(2,1)S(1)}) custom-call(bf16[320,256]{1,0:T(8,128)(2,1)S(1)} %bitcast.17, bf16[320,1056]{1,0:T(8,128)(2,1)S(1)} %copy-done), custom_call_target="tpu_custom_call" | custom-call | flops 1000 | bytes 1000 | tf_op jit(solution)/shard_map/down/pallas_call | solution.py:250
  2.6 0.5 %collective-permute-start = (bf16[4,32,1056]{2,1,0:T(8,128)(2,1)S(1)}, bf16[4,32,1056]{2,1,0:T(8,128)(2,1)S(1)}, u32[]{:S(2)}, u32[]{:S(2)}) collective-permute-start(bf16[4,32,1056]{2,1,0:T(8,128)(2,1)S(1)} %get-tuple-element.29), channel_id=1, source_target_pairs={{0,1},{1,0},{2,3},{3,2},{4,5},{5,4},{6,7},{7,6},{8,9},{9,8},{10,11... | collective-permute-start | bytes 811016 | tf_op jit(solution)/shard_map/ppermute | solution.py:246
  3.1 1.2 %collective-permute-done = bf16[4,32,1056]{2,1,0:T(8,128)(2,1)S(1)} collective-permute-done((bf16[4,32,1056]{2,1,0:T(8,128)(2,1)S(1)}, bf16[4,32,1056]{2,1,0:T(8,128)(2,1)S(1)}, u32[]{:S(2)}, u32[]{:S(2)}) %collective-permute-start) | collective-permute-done | bytes 270368 | tf_op jit(solution)/shard_map/ppermute | solution.py:246
  4.5 3.9 %collective-permute-start.7 = (bf16[32,1056]{1,0:T(8,128)(2,1)S(1)}, bf16[32,1056]{1,0:T(8,128)(2,1)S(1)}, u32[]{:S(2)}, u32[]{:S(2)}) collective-permute-start(bf16[32,1056]{1,0:T(8,128)(2,1)S(1)} %get-tuple-element.54), channel_id=1, source_target_pairs={{0,6},{1,7},{2,4},{3,5},{4,2},{5,3},{6,0},{7,1},{8,14},{9,15},{10,... | collective-permute-start | bytes 202760 | tf_op jit(solution)/shard_map/ppermute | solution.py:246
  8.4 3.6 %collective-permute-start.10 = (bf16[288,256]{1,0:T(8,128)(2,1)S(1)}, bf16[288,256]{1,0:T(8,128)(2,1)S(1)}, u32[]{:S(2)}, u32[]{:S(2)}) collective-permute-start(bf16[288,256]{1,0:T(8,128)(2,1)S(1)} %bitcast.21), channel_id=1, source_target_pairs={{0,24},{8,0},{16,8},{24,16},{1,25},{9,1},{17,9},{25,17},{2,26},{10... | collective-permute-start | bytes 442376 | tf_op jit(solution)/shard_map/ppermute | solution.py:264
  12.0 1.0 %collective-permute-start.8 = (bf16[288,256]{1,0:T(8,128)(2,1)S(1)}, bf16[288,256]{1,0:T(8,128)(2,1)S(1)}, u32[]{:S(2)}, u32[]{:S(2)}) collective-permute-start(bf16[288,256]{1,0:T(8,128)(2,1)S(1)} %bitcast.23), channel_id=1, source_target_pairs={{0,8},{8,16},{16,24},{24,0},{1,9},{9,17},{17,25},{25,1},{2,10},{10... | collective-permute-start | bytes 442376 | tf_op jit(solution)/shard_map/ppermute | solution.py:264
  13.0 0.6 %collective-permute-start.6 = (bf16[32,1056]{1,0:T(8,128)(2,1)S(1)}, bf16[32,1056]{1,0:T(8,128)(2,1)S(1)}, u32[]{:S(2)}, u32[]{:S(2)}) collective-permute-start(bf16[32,1056]{1,0:T(8,128)(2,1)S(1)} %get-tuple-element.55), channel_id=1, source_target_pairs={{0,4},{1,5},{2,6},{3,7},{4,0},{5,1},{6,2},{7,3},{8,12},{9,13},{10,... | collective-permute-start | bytes 202760 | tf_op jit(solution)/shard_map/ppermute | solution.py:246
  13.7 0.8 %prepare.1 = (f32[32,16]{1,0:T(8,128)S(1)}, f32[32,16]{1,0:T(8,128)S(1)}, f32[16,256]{1,0:T(8,128)S(1)}, f32[16,256]{1,0:T(8,128)S(1)}, f32[1024,128]{1,0:T(8,12...) custom-call(s32[4]{0:T(128)S(1)} %copy-done.7, ...), custom_call_target="tpu_custom_call" | custom-call | flops 1000 | bytes 1000 | tf_op jit(solution)/shard_map/prepare/pallas_call | solution.py:250
  14.5 0.8 %collective-permute-start.5 = (bf16[32,1056]{1,0:T(8,128)(2,1)S(1)}, bf16[32,1056]{1,0:T(8,128)(2,1)S(1)}, u32[]{:S(2)}, u32[]{:S(2)}) collective-permute-start(bf16[32,1056]{1,0:T(8,128)(2,1)S(1)} %get-tuple-element.56), channel_id=1, source_target_pairs={{0,2},{1,3},{2,0},{3,1},{4,6},{5,7},{6,4},{7,5},{8,10},{9,11},{10,... | collective-permute-start | bytes 202760 | tf_op jit(solution)/shard_map/ppermute | solution.py:246
  15.4 2.1 %collective-permute-done.6.refs_2_ = bf16[32,1056]{1,0:T(8,128)(2,1)S(1)} collective-permute-done((bf16[32,1056]{1,0:T(8,128)(2,1)S(1)}, bf16[32,1056]{1,0:T(8,128)(2,1)S(1)}, u32[]{:S(2)}, u32[]{:S(2)}) %collective-permute-start.6) | collective-permute-done | bytes 67616 | tf_op jit(solution)/shard_map/ppermute | solution.py:246
  18.0 0.9 %collective-permute-done.5.refs_1_ = bf16[32,1056]{1,0:T(8,128)(2,1)S(1)} collective-permute-done((bf16[32,1056]{1,0:T(8,128)(2,1)S(1)}, bf16[32,1056]{1,0:T(8,128)(2,1)S(1)}, u32[]{:S(2)}, u32[]{:S(2)}) %collective-permute-start.5) | collective-permute-done | bytes 67616 | tf_op jit(solution)/shard_map/ppermute | solution.py:246
  18.9 0.7 %copy-done.6 = f32[256]{0:T(256)S(1)} copy-done((f32[256]{0:T(256)S(1)}, f32[256]{0:T(256)}, u32[]{:S(2)}) %copy-start.6) | copy-done | bytes 1048
  19.8 4.7 %collective-permute-done.9 = bf16[288,256]{1,0:T(8,128)(2,1)S(1)} collective-permute-done((bf16[288,256]{1,0:T(8,128)(2,1)S(1)}, bf16[288,256]{1,0:T(8,128)(2,1)S(1)}, u32[]{:S(2)}, u32[]{:S(2)}) %collective-permute-start.9) | collective-permute-done | bytes 147488 | tf_op jit(solution)/shard_map/ppermute | solution.py:264
  24.5 0.6 %collective-permute-start.19 = (bf16[288,256]{1,0:T(8,128)(2,1)S(1)}, bf16[288,256]{1,0:T(8,128)(2,1)S(1)}, u32[]{:S(2)}, u32[]{:S(2)}) collective-permute-start(bf16[288,256]{1,0:T(8,128)(2,1)S(1)} %select_select_fusion.refs_10_), channel_id=1, source_target_pairs={{0,2},{1,3},{2,0},{3,1},{4,6},{5,7},{6,4},{7,5},{8,10},{9,11},{10,... | collective-permute-start | bytes 442376 | tf_op jit(solution)/shard_map/ppermute | solution.py:246
  25.1 1.4 %collective-permute-start.16 = (bf16[32,1056]{1,0:T(8,128)(2,1)S(1)}, bf16[32,1056]{1,0:T(8,128)(2,1)S(1)}, u32[]{:S(2)}, u32[]{:S(2)}) collective-permute-start(bf16[32,1056]{1,0:T(8,128)(2,1)S(1)} %norm.1.refs_2_), channel_id=1, source_target_pairs={{0,6},{1,7},{2,4},{3,5},{4,2},{5,3},{6,0},{7,1},{8,14},{9,15},{10,... | collective-permute-start | bytes 202760 | tf_op jit(solution)/shard_map/ppermute | solution.py:246
  26.6 1.5 %collective-permute-start.14 = (bf16[32,1056]{1,0:T(8,128)(2,1)S(1)}, bf16[32,1056]{1,0:T(8,128)(2,1)S(1)}, u32[]{:S(2)}, u32[]{:S(2)}) collective-permute-start(bf16[32,1056]{1,0:T(8,128)(2,1)S(1)} %norm.1.refs_2_), channel_id=1, source_target_pairs={{0,4},{1,5},{2,6},{3,7},{4,0},{5,1},{6,2},{7,3},{8,12},{9,13},{10,... | collective-permute-start | bytes 202760 | tf_op jit(solution)/shard_map/ppermute | solution.py:246
  28.1 0.5 %collective-permute-start.12 = (bf16[32,1056]{1,0:T(8,128)(2,1)S(1)}, bf16[32,1056]{1,0:T(8,128)(2,1)S(1)}, u32[]{:S(2)}, u32[]{:S(2)}) collective-permute-start(bf16[32,1056]{1,0:T(8,128)(2,1)S(1)} %norm.1.refs_2_), channel_id=1, source_target_pairs={{0,2},{1,3},{2,0},{3,1},{4,6},{5,7},{6,4},{7,5},{8,10},{9,11},{10,... | collective-permute-start | bytes 202760 | tf_op jit(solution)/shard_map/ppermute | solution.py:246
  28.6 2.7 %collective-permute-done.19.refs_12_ = bf16[288,256]{1,0:T(8,128)(2,1)S(1)} collective-permute-done((bf16[288,256]{1,0:T(8,128)(2,1)S(1)}, bf16[288,256]{1,0:T(8,128)(2,1)S(1)}, u32[]{:S(2)}, u32[]{:S(2)}) %collective-permute-start.19) | collective-permute-done | bytes 147488 | tf_op jit(solution)/shard_map/ppermute | solution.py:246
  31.3 0.7 %collective-permute-done.16.refs_8_ = bf16[32,1056]{1,0:T(8,128)(2,1)S(1)} collective-permute-done((bf16[32,1056]{1,0:T(8,128)(2,1)S(1)}, bf16[32,1056]{1,0:T(8,128)(2,1)S(1)}, u32[]{:S(2)}, u32[]{:S(2)}) %collective-permute-start.16) | collective-permute-done | bytes 67616 | tf_op jit(solution)/shard_map/ppermute | solution.py:246
  32.9 0.9 %collective-permute-start.1 = (bf16[64,640]{1,0:T(8,128)(2,1)S(1)}, bf16[64,640]{1,0:T(8,128)(2,1)S(1)}, u32[]{:S(2)}, u32[]{:S(2)}) collective-permute-start(bf16[64,640]{1,0:T(8,128)(2,1)S(1)} %get-tuple-element.34), channel_id=1, source_target_pairs={{0,2},{1,3},{2,0},{3,1},{4,6},{5,7},{6,4},{7,5},{8,10},{9,11},{10,... | collective-permute-start | bytes 245768 | tf_op jit(solution)/shard_map/ppermute | solution.py:246
  34.3 0.8 %collective-permute-done.15.refs_7_ = bf16[32,1056]{1,0:T(8,128)(2,1)S(1)} collective-permute-done((bf16[32,1056]{1,0:T(8,128)(2,1)S(1)}, bf16[32,1056]{1,0:T(8,128)(2,1)S(1)}, u32[]{:S(2)}, u32[]{:S(2)}) %collective-permute-start.15) | collective-permute-done | bytes 67616 | tf_op jit(solution)/shard_map/ppermute | solution.py:246
  35.1 1.0 %collective-permute-start.2 = (bf16[64,640]{1,0:T(8,128)(2,1)S(1)}, bf16[64,640]{1,0:T(8,128)(2,1)S(1)}, u32[]{:S(2)}, u32[]{:S(2)}) collective-permute-start(bf16[64,640]{1,0:T(8,128)(2,1)S(1)} %get-tuple-element.35), channel_id=1, source_target_pairs={{0,4},{1,5},{2,6},{3,7},{4,0},{5,1},{6,2},{7,3},{8,12},{9,13},{10,... | collective-permute-start | bytes 245768 | tf_op jit(solution)/shard_map/ppermute | solution.py:246
  36.1 1.6 %collective-permute-start.3 = (bf16[64,640]{1,0:T(8,128)(2,1)S(1)}, bf16[64,640]{1,0:T(8,128)(2,1)S(1)}, u32[]{:S(2)}, u32[]{:S(2)}) collective-permute-start(bf16[64,640]{1,0:T(8,128)(2,1)S(1)} %get-tuple-element.36), channel_id=1, source_target_pairs={{0,6},{1,7},{2,4},{3,5},{4,2},{5,3},{6,0},{7,1},{8,14},{9,15},{10,... | collective-permute-start | bytes 245768 | tf_op jit(solution)/shard_map/ppermute | solution.py:246
  37.7 3.8 %attend.1.refs_4_ = bf16[144,256]{1,0:T(8,128)(2,1)S(1)} custom-call(f32[16,256]{1,0:T(8,128)S(1)} %get-tuple-element.37.cos_ref, f32[16,256]{1,0:T(8,128)S(1)} %get-tuple-element.38.sin_ref, f32[1024,128]{1,0:T(8,128)S(1)} %get-tuple-element.39.limits, f32[128,256]{1,0:T(8,128)S(1)} %get-tuple-element.40.fresh_limits, bf16[256,1024]{1,0:T(8,128)(2,1)S(1)} %copy-done.1, ...), custom_call_target="tpu_custom_call" | custom-call | flops 1000 | bytes 1000 | tf_op jit(solution)/shard_map/attend/pallas_call | solution.py:250
  41.5 1.4 %collective-permute-start.23 = (bf16[144,256]{1,0:T(8,128)(2,1)S(1)}, bf16[144,256]{1,0:T(8,128)(2,1)S(1)}, u32[]{:S(2)}, u32[]{:S(2)}) collective-permute-start(bf16[144,256]{1,0:T(8,128)(2,1)S(1)} %attend.1.refs_4_), channel_id=1, source_target_pairs={{0,6},{1,7},{2,4},{3,5},{4,2},{5,3},{6,0},{7,1},{8,14},{9,15},{10,... | collective-permute-start | bytes 221192 | tf_op jit(solution)/shard_map/ppermute | solution.py:246
  43.0 1.0 %collective-permute-start.22 = (bf16[144,256]{1,0:T(8,128)(2,1)S(1)}, bf16[144,256]{1,0:T(8,128)(2,1)S(1)}, u32[]{:S(2)}, u32[]{:S(2)}) collective-permute-start(bf16[144,256]{1,0:T(8,128)(2,1)S(1)} %attend.1.refs_4_), channel_id=1, source_target_pairs={{0,4},{1,5},{2,6},{3,7},{4,0},{5,1},{6,2},{7,3},{8,12},{9,13},{10,... | collective-permute-start | bytes 221192 | tf_op jit(solution)/shard_map/ppermute | solution.py:246
  43.9 1.1 %collective-permute-start.21 = (bf16[144,256]{1,0:T(8,128)(2,1)S(1)}, bf16[144,256]{1,0:T(8,128)(2,1)S(1)}, u32[]{:S(2)}, u32[]{:S(2)}) collective-permute-start(bf16[144,256]{1,0:T(8,128)(2,1)S(1)} %attend.1.refs_4_), channel_id=1, source_target_pairs={{0,2},{1,3},{2,0},{3,1},{4,6},{5,7},{6,4},{7,5},{8,10},{9,11},{10,... | collective-permute-start | bytes 221192 | tf_op jit(solution)/shard_map/ppermute | solution.py:246
  45.1 2.5 %collective-permute-done.23.refs_7_ = bf16[144,256]{1,0:T(8,128)(2,1)S(1)} collective-permute-done((bf16[144,256]{1,0:T(8,128)(2,1)S(1)}, bf16[144,256]{1,0:T(8,128)(2,1)S(1)}, u32[]{:S(2)}, u32[]{:S(2)}) %collective-permute-start.23) | collective-permute-done | bytes 73760 | tf_op jit(solution)/shard_map/ppermute | solution.py:246
  48.7 1.4 %collective-permute-done.24 = bf16[320,256]{1,0:T(8,128)(2,1)S(1)} collective-permute-done((bf16[320,256]{1,0:T(8,128)(2,1)S(1)}, bf16[320,256]{1,0:T(8,128)(2,1)S(1)}, u32[]{:S(2)}, u32[]{:S(2)}) %collective-permute-start.24) | collective-permute-done | bytes 163872 | tf_op jit(solution)/shard_map/ppermute | solution.py:246
  50.1 0.7 %fusion = bf16[256,320]{0,1:T(8,128)(2,1)} fusion(f32[320,256]{1,0:T(8,128)S(1)} %get-tuple-element.49, bf16[320,256]{1,0:T(8,128)(2,1)S(1)} %collective-permute-done.24), kind=kLoop, calls=%fused_computation.2 | loop fusion | flops 245760 | bytes 655360 | tf_op jit(solution)/shard_map/transpose | solution.py:323
  (53 shorter events, 3.5 us)
Async XLA Ops:
  0.0 1.1 %copy-start = (bf16[320,1056]{1,0:T(8,128)(2,1)S(1)}, bf16[320,1056]{1,0:T(8,128)(2,1)}, u32[]{:S(2)}) copy-start(bf16[320,1056]{1,0:T(8,128)(2,1)} %w_ref.1) | copy-start | bytes 2027524
  2.6 1.7 %collective-permute-start = (bf16[4,32,1056]{2,1,0:T(8,128)(2,1)S(1)}, bf16[4,32,1056]{2,1,0:T(8,128)(2,1)S(1)}, u32[]{:S(2)}, u32[]{:S(2)}) collective-permute-start(bf16[4,32,1056]{2,1,0:T(8,128)(2,1)S(1)} %get-tuple-element.29), channel_id=1, source_target_pairs={{0,1},{1,0},{2,3},{3,2},{4,5},{5,4},{6,7},{7,6},{8,9},{9,8},{10,11... | collective-permute-start | bytes 811016 | tf_op jit(solution)/shard_map/ppermute | solution.py:246
  4.4 4.0 %copy-start.10 = (bf16[1,256,288]{1,2,0:T(8,128)(2,1)S(1)}, bf16[1,256,288]{1,2,0:T(8,128)(2,1)}, u32[]{:S(2)}) copy-start(bf16[1,256,288]{1,2,0:T(8,128)(2,1)} %param.19) | copy-start | bytes 442372
  4.4 8.6 %copy-start.11 = (f32[768]{0:T(1024)S(1)}, f32[768]{0:T(1024)}, u32[]{:S(2)}) copy-start(f32[768]{0:T(1024)} %param.14) | copy-start | bytes 9220
  4.4 9.2 %copy-start.2 = (bf16[64,2560]{1,0:T(8,128)(2,1)S(1)}, bf16[64,2560]{1,0:T(8,128)(2,1)}, u32[]{:S(2)}) copy-start(bf16[64,2560]{1,0:T(8,128)(2,1)} %w_out_ref) | copy-start | bytes 983044
  4.5 9.2 %copy-start.5 = (s32[4,32]{1,0:T(4,128)S(1)}, s32[4,32]{1,0:T(4,128)}, u32[]{:S(2)}) copy-start(s32[4,32]{1,0:T(4,128)} %page_ref.1) | copy-start | bytes 1540
  4.5 10.0 %collective-permute-start.7 = (bf16[32,1056]{1,0:T(8,128)(2,1)S(1)}, bf16[32,1056]{1,0:T(8,128)(2,1)S(1)}, u32[]{:S(2)}, u32[]{:S(2)}) collective-permute-start(bf16[32,1056]{1,0:T(8,128)(2,1)S(1)} %get-tuple-element.54), channel_id=1, source_target_pairs={{0,6},{1,7},{2,4},{3,5},{4,2},{5,3},{6,0},{7,1},{8,14},{9,15},{10,... | collective-permute-start | bytes 202760 | tf_op jit(solution)/shard_map/ppermute | solution.py:246
  8.4 11.4 %collective-permute-start.10 = (bf16[288,256]{1,0:T(8,128)(2,1)S(1)}, bf16[288,256]{1,0:T(8,128)(2,1)S(1)}, u32[]{:S(2)}, u32[]{:S(2)}) collective-permute-start(bf16[288,256]{1,0:T(8,128)(2,1)S(1)} %bitcast.21), channel_id=1, source_target_pairs={{0,24},{8,0},{16,8},{24,16},{1,25},{9,1},{17,9},{25,17},{2,26},{10... | collective-permute-start | bytes 442376 | tf_op jit(solution)/shard_map/ppermute | solution.py:264
  12.0 12.5 %collective-permute-start.9 = (bf16[288,256]{1,0:T(8,128)(2,1)S(1)}, bf16[288,256]{1,0:T(8,128)(2,1)S(1)}, u32[]{:S(2)}, u32[]{:S(2)}) collective-permute-start(bf16[288,256]{1,0:T(8,128)(2,1)S(1)} %bitcast.22), channel_id=1, source_target_pairs={{0,16},{8,24},{16,0},{24,8},{1,17},{9,25},{17,1},{25,9},{2,18},{10... | collective-permute-start | bytes 442376 | tf_op jit(solution)/shard_map/ppermute | solution.py:264
  12.0 12.5 %collective-permute-start.8 = (bf16[288,256]{1,0:T(8,128)(2,1)S(1)}, bf16[288,256]{1,0:T(8,128)(2,1)S(1)}, u32[]{:S(2)}, u32[]{:S(2)}) collective-permute-start(bf16[288,256]{1,0:T(8,128)(2,1)S(1)} %bitcast.23), channel_id=1, source_target_pairs={{0,8},{8,16},{16,24},{24,0},{1,9},{9,17},{17,25},{25,1},{2,10},{10... | collective-permute-start | bytes 442376 | tf_op jit(solution)/shard_map/ppermute | solution.py:264
  13.0 4.4 %copy-start.4 = (bf16[768,96]{0,1:T(8,128)(2,1)S(1)}, bf16[768,96]{0,1:T(8,128)(2,1)}, u32[]{:S(2)}) copy-start(bf16[768,96]{0,1:T(8,128)(2,1)} %param.16) | copy-start | bytes 442372
  13.0 4.4 %collective-permute-start.6 = (bf16[32,1056]{1,0:T(8,128)(2,1)S(1)}, bf16[32,1056]{1,0:T(8,128)(2,1)S(1)}, u32[]{:S(2)}, u32[]{:S(2)}) collective-permute-start(bf16[32,1056]{1,0:T(8,128)(2,1)S(1)} %get-tuple-element.55), channel_id=1, source_target_pairs={{0,4},{1,5},{2,6},{3,7},{4,0},{5,1},{6,2},{7,3},{8,12},{9,13},{10,... | collective-permute-start | bytes 202760 | tf_op jit(solution)/shard_map/ppermute | solution.py:246
  14.5 4.4 %collective-permute-start.5 = (bf16[32,1056]{1,0:T(8,128)(2,1)S(1)}, bf16[32,1056]{1,0:T(8,128)(2,1)S(1)}, u32[]{:S(2)}, u32[]{:S(2)}) collective-permute-start(bf16[32,1056]{1,0:T(8,128)(2,1)S(1)} %get-tuple-element.56), channel_id=1, source_target_pairs={{0,2},{1,3},{2,0},{3,1},{4,6},{5,7},{6,4},{7,5},{8,10},{9,11},{10,... | collective-permute-start | bytes 202760 | tf_op jit(solution)/shard_map/ppermute | solution.py:246
  17.5 11.2 %collective-permute-start.4 = (bf16[96,768]{1,0:T(8,128)(2,1)S(1)}, bf16[96,768]{1,0:T(8,128)(2,1)S(1)}, u32[]{:S(2)}, u32[]{:S(2)}) collective-permute-start(bf16[96,768]{1,0:T(8,128)(2,1)S(1)} %bitcast.18), channel_id=1, source_target_pairs={{0,4},{1,5},{2,6},{3,7},{4,0},{5,1},{6,2},{7,3},{8,12},{9,13},{10,... | collective-permute-start | bytes 442376 | tf_op jit(solution)/shard_map/ppermute | solution.py:246
  19.6 18.1 %copy-start.1 = (bf16[256,1024]{1,0:T(8,128)(2,1)S(1)}, bf16[256,1024]{1,0:T(8,128)(2,1)}, u32[]{:S(2)}) copy-start(bf16[256,1024]{1,0:T(8,128)(2,1)} %w_kv_ref.1) | copy-start | bytes 1572868
  24.5 6.8 %collective-permute-start.19 = (bf16[288,256]{1,0:T(8,128)(2,1)S(1)}, bf16[288,256]{1,0:T(8,128)(2,1)S(1)}, u32[]{:S(2)}, u32[]{:S(2)}) collective-permute-start(bf16[288,256]{1,0:T(8,128)(2,1)S(1)} %select_select_fusion.refs_10_), channel_id=1, source_target_pairs={{0,2},{1,3},{2,0},{3,1},{4,6},{5,7},{6,4},{7,5},{8,10},{9,11},{10,... | collective-permute-start | bytes 442376 | tf_op jit(solution)/shard_map/ppermute | solution.py:246
  25.1 6.9 %collective-permute-start.16 = (bf16[32,1056]{1,0:T(8,128)(2,1)S(1)}, bf16[32,1056]{1,0:T(8,128)(2,1)S(1)}, u32[]{:S(2)}, u32[]{:S(2)}) collective-permute-start(bf16[32,1056]{1,0:T(8,128)(2,1)S(1)} %norm.1.refs_2_), channel_id=1, source_target_pairs={{0,6},{1,7},{2,4},{3,5},{4,2},{5,3},{6,0},{7,1},{8,14},{9,15},{10,... | collective-permute-start | bytes 202760 | tf_op jit(solution)/shard_map/ppermute | solution.py:246
  26.6 5.5 %collective-permute-start.14 = (bf16[32,1056]{1,0:T(8,128)(2,1)S(1)}, bf16[32,1056]{1,0:T(8,128)(2,1)S(1)}, u32[]{:S(2)}, u32[]{:S(2)}) collective-permute-start(bf16[32,1056]{1,0:T(8,128)(2,1)S(1)} %norm.1.refs_2_), channel_id=1, source_target_pairs={{0,4},{1,5},{2,6},{3,7},{4,0},{5,1},{6,2},{7,3},{8,12},{9,13},{10,... | collective-permute-start | bytes 202760 | tf_op jit(solution)/shard_map/ppermute | solution.py:246
  28.1 4.8 %collective-permute-start.12 = (bf16[32,1056]{1,0:T(8,128)(2,1)S(1)}, bf16[32,1056]{1,0:T(8,128)(2,1)S(1)}, u32[]{:S(2)}, u32[]{:S(2)}) collective-permute-start(bf16[32,1056]{1,0:T(8,128)(2,1)S(1)} %norm.1.refs_2_), channel_id=1, source_target_pairs={{0,2},{1,3},{2,0},{3,1},{4,6},{5,7},{6,4},{7,5},{8,10},{9,11},{10,... | collective-permute-start | bytes 202760 | tf_op jit(solution)/shard_map/ppermute | solution.py:246
  28.6 9.0 %collective-permute-start.18 = (bf16[288,256]{1,0:T(8,128)(2,1)S(1)}, bf16[288,256]{1,0:T(8,128)(2,1)S(1)}, u32[]{:S(2)}, u32[]{:S(2)}) collective-permute-start(bf16[288,256]{1,0:T(8,128)(2,1)S(1)} %select_select_fusion.refs_10_), channel_id=1, source_target_pairs={{0,1},{1,0},{2,3},{3,2},{4,5},{5,4},{6,7},{7,6},{8,9},{9,8},{10,11... | collective-permute-start | bytes 442376 | tf_op jit(solution)/shard_map/ppermute | solution.py:246
  31.3 6.3 %collective-permute-start.20 = (bf16[288,256]{1,0:T(8,128)(2,1)S(1)}, bf16[288,256]{1,0:T(8,128)(2,1)S(1)}, u32[]{:S(2)}, u32[]{:S(2)}) collective-permute-start(bf16[288,256]{1,0:T(8,128)(2,1)S(1)} %collective-permute-done.19.refs_12_), channel_id=1, source_target_pairs={{0,1},{1,0},{2,3},{3,2},{4,5},{5,4},{6,7},{7,6},{8,9},{9,8},{10,11... | collective-permute-start | bytes 442376 | tf_op jit(solution)/shard_map/ppermute | solution.py:246
  32.1 1.7 %collective-permute-start.11 = (bf16[32,1056]{1,0:T(8,128)(2,1)S(1)}, bf16[32,1056]{1,0:T(8,128)(2,1)S(1)}, u32[]{:S(2)}, u32[]{:S(2)}) collective-permute-start(bf16[32,1056]{1,0:T(8,128)(2,1)S(1)} %norm.1.refs_2_), channel_id=1, source_target_pairs={{0,1},{1,0},{2,3},{3,2},{4,5},{5,4},{6,7},{7,6},{8,9},{9,8},{10,11... | collective-permute-start | bytes 202760 | tf_op jit(solution)/shard_map/ppermute | solution.py:246
  32.1 1.7 %collective-permute-start.17 = (bf16[32,1056]{1,0:T(8,128)(2,1)S(1)}, bf16[32,1056]{1,0:T(8,128)(2,1)S(1)}, u32[]{:S(2)}, u32[]{:S(2)}) collective-permute-start(bf16[32,1056]{1,0:T(8,128)(2,1)S(1)} %collective-permute-done.16.refs_8_), channel_id=1, source_target_pairs={{0,1},{1,0},{2,3},{3,2},{4,5},{5,4},{6,7},{7,6},{8,9},{9,8},{10,11... | collective-permute-start | bytes 202760 | tf_op jit(solution)/shard_map/ppermute | solution.py:246
  32.9 11.0 %collective-permute-start.1 = (bf16[64,640]{1,0:T(8,128)(2,1)S(1)}, bf16[64,640]{1,0:T(8,128)(2,1)S(1)}, u32[]{:S(2)}, u32[]{:S(2)}) collective-permute-start(bf16[64,640]{1,0:T(8,128)(2,1)S(1)} %get-tuple-element.34), channel_id=1, source_target_pairs={{0,2},{1,3},{2,0},{3,1},{4,6},{5,7},{6,4},{7,5},{8,10},{9,11},{10,... | collective-permute-start | bytes 245768 | tf_op jit(solution)/shard_map/ppermute | solution.py:246
  33.8 1.3 %collective-permute-start.15 = (bf16[32,1056]{1,0:T(8,128)(2,1)S(1)}, bf16[32,1056]{1,0:T(8,128)(2,1)S(1)}, u32[]{:S(2)}, u32[]{:S(2)}) collective-permute-start(bf16[32,1056]{1,0:T(8,128)(2,1)S(1)} %collective-permute-done.14.refs_6_), channel_id=1, source_target_pairs={{0,1},{1,0},{2,3},{3,2},{4,5},{5,4},{6,7},{7,6},{8,9},{9,8},{10,11... | collective-permute-start | bytes 202760 | tf_op jit(solution)/shard_map/ppermute | solution.py:246
  33.8 2.3 %collective-permute-start.13 = (bf16[32,1056]{1,0:T(8,128)(2,1)S(1)}, bf16[32,1056]{1,0:T(8,128)(2,1)S(1)}, u32[]{:S(2)}, u32[]{:S(2)}) collective-permute-start(bf16[32,1056]{1,0:T(8,128)(2,1)S(1)} %collective-permute-done.12.refs_4_), channel_id=1, source_target_pairs={{0,1},{1,0},{2,3},{3,2},{4,5},{5,4},{6,7},{7,6},{8,9},{9,8},{10,11... | collective-permute-start | bytes 202760 | tf_op jit(solution)/shard_map/ppermute | solution.py:246
  35.1 10.0 %collective-permute-start.2 = (bf16[64,640]{1,0:T(8,128)(2,1)S(1)}, bf16[64,640]{1,0:T(8,128)(2,1)S(1)}, u32[]{:S(2)}, u32[]{:S(2)}) collective-permute-start(bf16[64,640]{1,0:T(8,128)(2,1)S(1)} %get-tuple-element.35), channel_id=1, source_target_pairs={{0,4},{1,5},{2,6},{3,7},{4,0},{5,1},{6,2},{7,3},{8,12},{9,13},{10,... | collective-permute-start | bytes 245768 | tf_op jit(solution)/shard_map/ppermute | solution.py:246
  36.1 9.0 %collective-permute-start.3 = (bf16[64,640]{1,0:T(8,128)(2,1)S(1)}, bf16[64,640]{1,0:T(8,128)(2,1)S(1)}, u32[]{:S(2)}, u32[]{:S(2)}) collective-permute-start(bf16[64,640]{1,0:T(8,128)(2,1)S(1)} %get-tuple-element.36), channel_id=1, source_target_pairs={{0,6},{1,7},{2,4},{3,5},{4,2},{5,3},{6,0},{7,1},{8,14},{9,15},{10,... | collective-permute-start | bytes 245768 | tf_op jit(solution)/shard_map/ppermute | solution.py:246
  41.5 6.1 %collective-permute-start.23 = (bf16[144,256]{1,0:T(8,128)(2,1)S(1)}, bf16[144,256]{1,0:T(8,128)(2,1)S(1)}, u32[]{:S(2)}, u32[]{:S(2)}) collective-permute-start(bf16[144,256]{1,0:T(8,128)(2,1)S(1)} %attend.1.refs_4_), channel_id=1, source_target_pairs={{0,6},{1,7},{2,4},{3,5},{4,2},{5,3},{6,0},{7,1},{8,14},{9,15},{10,... | collective-permute-start | bytes 221192 | tf_op jit(solution)/shard_map/ppermute | solution.py:246
  43.0 4.9 %collective-permute-start.22 = (bf16[144,256]{1,0:T(8,128)(2,1)S(1)}, bf16[144,256]{1,0:T(8,128)(2,1)S(1)}, u32[]{:S(2)}, u32[]{:S(2)}) collective-permute-start(bf16[144,256]{1,0:T(8,128)(2,1)S(1)} %attend.1.refs_4_), channel_id=1, source_target_pairs={{0,4},{1,5},{2,6},{3,7},{4,0},{5,1},{6,2},{7,3},{8,12},{9,13},{10,... | collective-permute-start | bytes 221192 | tf_op jit(solution)/shard_map/ppermute | solution.py:246
  43.9 4.4 %collective-permute-start.21 = (bf16[144,256]{1,0:T(8,128)(2,1)S(1)}, bf16[144,256]{1,0:T(8,128)(2,1)S(1)}, u32[]{:S(2)}, u32[]{:S(2)}) collective-permute-start(bf16[144,256]{1,0:T(8,128)(2,1)S(1)} %attend.1.refs_4_), channel_id=1, source_target_pairs={{0,2},{1,3},{2,0},{3,1},{4,6},{5,7},{6,4},{7,5},{8,10},{9,11},{10,... | collective-permute-start | bytes 221192 | tf_op jit(solution)/shard_map/ppermute | solution.py:246
  48.7 1.5 %collective-permute-start.24 = (bf16[320,256]{1,0:T(8,128)(2,1)S(1)}, bf16[320,256]{1,0:T(8,128)(2,1)S(1)}, u32[]{:S(2)}, u32[]{:S(2)}) collective-permute-start(bf16[320,256]{1,0:T(8,128)(2,1)S(1)} %get-tuple-element.50), channel_id=1, source_target_pairs={{0,1},{1,0},{2,3},{3,2},{4,5},{5,4},{6,7},{7,6},{8,9},{9,8},{10,11... | collective-permute-start | bytes 491528 | tf_op jit(solution)/shard_map/ppermute | solution.py:246
  (5 other events, 3.6 us)

commit v3 on v2

--- a/solution.py
+++ b/solution.py
@@ -13,6 +13,7 @@
 VDIM = 64
 HEAD = NOPE + VDIM
 SPAN = 4
+EXTRA = 16
 epsilon = 1e-05
 MASKED = -1e30
 FLOOR = -1e29
@@ -26,6 +27,10 @@
 
 def cost(flops, moved, special=0):
     return pl.CostEstimate(flops=flops, bytes_accessed=moved, transcendentals=special)
+
+
+def padded(lanes):
+    return -(-lanes // 128) * 128
 
 
 def rotate(values, cosine, sine, axis):
@@ -49,10 +54,11 @@
 
 
 def prepare_kernel(
-    span, count, own, page, home_ref, cached_ref, live_ref, page_ref, w_out_ref,
-    own_cos, own_sin, cosine, sine, limits, fresh_limits, alive, choice, *refs,
+    span, count, own, page, home_ref, cached_ref, live_ref, page_ref, q_gain_ref, kv_gain_ref,
+    own_cos, own_sin, cosine, sine, limits, fresh_limits, alive, choice, q_gain, kv_gain, logical,
 ):
-    columns, logical = refs[:-1], refs[-1]
+    q_gain[...] = q_gain_ref[...]
+    kv_gain[...] = kv_gain_ref[...]
     column = lax.axis_index("col")
     row = lax.axis_index("row")
     slot = home_ref[row]
@@ -76,13 +82,14 @@
 
     for l in range(page_ref.shape[1]):
         logical[page_ref[slot, l]] = l
-    per_piece = limits.shape[0] // span // page
-    offset = lax.broadcasted_iota(jnp.int32, (page, 128), 0)
+    per_piece = limits.shape[1] // span // page
+    offset = lax.broadcasted_iota(jnp.int32, (EXTRA, page), 1)
+    line = lax.broadcasted_iota(jnp.int32, (EXTRA, page), 0)
     for j in range(span):
         for p in range(per_piece):
             seen = offset < cached - logical[(column ^ j) * per_piece + p] * page
             start = (j * per_piece + p) * page
-            limits[start : start + page, :] = jnp.where(seen, 0.0, MASKED)
+            limits[:, start : start + page] = jnp.where(seen | (line > 0), 0.0, MASKED).astype(bf16)
     query_id = lax.broadcasted_iota(jnp.int32, (own, group), 1)
     offset = lax.broadcasted_iota(jnp.int32, (own, group), 0)
     for j in range(span):
@@ -95,25 +102,32 @@
     source = jnp.where(row >= source, row - source, row - source + rows)
     choice[...] = jnp.where(source == slot, 1.0, 0.0)
 
-    width = columns[0].shape[1]
-    for i, ref in enumerate(columns):
-        start = ((column // 2) ^ i) * width
+
+def sum_kernel(count, wide, even_ref, odd_ref, w_out_ref, *outs):
+    half = count // 2
+    own = even_ref.shape[1]
+    width = 2 * (w_out_ref.shape[1] // count)
+    chip = lax.axis_index("col") // 2
+    for i, ref in enumerate(outs):
+        ref[:, :wide] = (even_ref[i].astype(f32) + odd_ref[i].astype(f32)).astype(bf16)
+        start = (chip ^ i) * width
         if width % 128 == 0:
-            ref[...] = w_out_ref[:, pl.ds(pl.multiple_of(start, 128), width)]
+            taken = w_out_ref[:, pl.ds(pl.multiple_of(start, 128), width)]
         else:
             taken = w_out_ref[:, :width]
-            for chip in range(1, count // 2):
-                taken = jnp.where(
-                    (column // 2) ^ i == chip, w_out_ref[:, chip * width : (chip + 1) * width], taken
-                )
-            ref[...] = taken
+            for k in range(1, half):
+                taken = jnp.where(chip ^ i == k, w_out_ref[:, k * width : (k + 1) * width], taken)
+        for p in range(taken.shape[0] // own):
+            lane = padded(wide) + p * padded(width)
+            ref[:, lane : lane + width] = taken[p * own : (p + 1) * own]
 
 
 def norm_kernel(q_width, kv_width, cos_ref, sin_ref, q_gain_ref, kv_gain_ref, *refs):
     out_ref = refs[-1]
-    total = refs[0][...].astype(f32)
+    wide = out_ref.shape[1]
+    total = refs[0][:, :wide].astype(f32)
     for ref in refs[1:-1]:
-        total += ref[...].astype(f32)
+        total += ref[:, :wide].astype(f32)
 
     def scaled(values, gain):
         mean = jnp.mean(values * values, axis=-1, keepdims=True)
@@ -134,7 +148,9 @@
     return [high, middle, value - high - middle]
 
 
-def attend_kernel(span, count, own, q_width, kv_width, cos_ref, sin_ref, limits, fresh_limits, w_kv_ref, *refs):
+def attend_kernel(
+    span, count, own, q_width, kv_width, cos_ref, sin_ref, limits, fresh_limits, w_kv_ref, *refs
+):
     heads = count // span
     weights, refs = refs[:heads], refs[heads:]
     blocks, refs = refs[:count], refs[count:]
@@ -149,10 +165,13 @@
         if j < span:
             fresh[j * own : (j + 1) * own, :] = blocks[j][:, q_width:].astype(f32)
     for j in range(span):
-        keys[:, j * piece : (j + 1) * piece] = pieces[j][...]
+        keys[: kv_width + ROPE, j * piece : (j + 1) * piece] = pieces[j][...]
+    keys[kv_width + ROPE :, :] = limits[...]
     fresh_keys = fresh[...].astype(bf16)
     latent = query_rows[...].astype(bf16)
     scale = 1.0 / math.sqrt(NOPE + ROPE)
+    line = lax.broadcasted_iota(jnp.int32, (EXTRA, group), 0)
+    first_row = jnp.where(line == 0, 1.0, 0.0).astype(bf16)
     stats = []
     for k in range(heads):
         head = column ^ (k * span)
@@ -166,9 +185,9 @@
         )
         query = jnp.concatenate([plain.astype(bf16), turned.astype(bf16)], axis=0)
         old = lax.dot_general(
-            keys[...], query, (((0,), (0,)), ((), ())), preferred_element_type=f32
-        )
-        old += jnp.concatenate([limits[...]] * (group // 128), axis=1)
+            keys[...], jnp.concatenate([query, first_row], axis=0),
+            (((0,), (0,)), ((), ())), preferred_element_type=f32,
+        )
         new = jnp.dot(fresh_keys, query, preferred_element_type=f32) + fresh_limits[...]
         peak = jnp.maximum(jnp.max(old, 0, keepdims=True), jnp.max(new, 0, keepdims=True))
         peak = jnp.maximum(peak, FLOOR)
@@ -189,14 +208,18 @@
     out_ref[heads * VDIM :, :] = jnp.concatenate(stats, axis=0).astype(bf16)
 
 
-def out_kernel(span, count, width, alive_ref, *refs):
+def out_kernel(span, count, width, wide, alive_ref, *refs):
     half = count // 2
     heads = count // span
     columns, refs = refs[:half], refs[half:]
     states, (mine_ref, other_ref, attended, weights) = refs[:half], refs[half:]
     scale = 1.0 / math.sqrt(NOPE + ROPE)
     for i in range(half):
-        weights[i * VDIM : (i + 1) * VDIM, :] = columns[i][...]
+        own = columns[i].shape[0]
+        for p in range(VDIM // own):
+            lane = padded(wide) + p * padded(2 * width)
+            row = i * VDIM + p * own
+            weights[row : row + own, :] = columns[i][:, lane : lane + 2 * width].astype(f32)
         parts = []
         for k in range(heads):
             ref = states[i ^ (k * span // 2)]
@@ -218,7 +241,7 @@
         factor = jnp.where(alive_ref[...] > 0, 1.0 / total, 0.0)
         attended[i * VDIM : (i + 1) * VDIM, :] = (summed * factor).astype(bf16)
     product = lax.dot_general(
-        weights[...], attended[...], (((0,), (0,)), ((), ())), preferred_element_type=f32
+        weights[...].astype(bf16), attended[...], (((0,), (0,)), ((), ())), preferred_element_type=f32
     )
     low, high = product[:width], product[width:]
     core = lax.axis_index("col") & 1
@@ -247,7 +270,7 @@
 
     def call(kernel, name, shapes, operands, scratch=(), scalars=0):
         single = not isinstance(shapes, list)
-        return pl.pallas_call(
+        result = pl.pallas_call(
             kernel,
             out_shape=shapes,
             in_specs=[SMEM] * scalars + [VMEM] * (len(operands) - scalars),
@@ -257,6 +280,7 @@
             cost_estimate=cost(1000, 1000),
             name=name,
         )(*operands)
+        return result if single else list(result)
 
     shape = jax.ShapeDtypeStruct
     held = latent_cache[0].T
@@ -270,31 +294,37 @@
         [shape((half, own, wide), bf16)] * 2, (tokens.T, w_down),
         [pltpu.VMEM((group, wide), f32)],
     )
-    paired = (even.astype(f32) + swap(odd, 1).astype(f32)).astype(bf16)
-    paired, w_out, home_slot = lax.optimization_barrier((paired, w_out, home_slot))
+    length = padded(wide) + VDIM // own * padded(2 * cols)
+    paired = call(
+        functools.partial(sum_kernel, count, wide), "sum",
+        [shape((own, length), bf16)] * half, (even, swap(odd, 1), w_out),
+    )
+    paired[0], home_slot = lax.optimization_barrier((paired[0], home_slot))
     partial = [paired[0]] + [swap(paired[k], 2 * k) for k in range(1, half)]
-    own_cos, own_sin, cosine, sine, limits, fresh_limits, alive, choice, *columns = call(
+    own_cos, own_sin, cosine, sine, limits, fresh_limits, alive, choice, q_scale, kv_scale = call(
         functools.partial(prepare_kernel, span, count, own, page), "prepare",
         [shape((own, ROPE // 2), f32)] * 2
         + [shape((ROPE // 2, group), f32)] * 2
-        + [shape((span * piece, 128), f32), shape((span * own, group), f32)]
+        + [shape((EXTRA, span * piece), bf16), shape((span * own, group), f32)]
         + [shape((1, group), f32), shape((rows, group), f32)]
-        + [shape((w_out.shape[0], 2 * cols), bf16)] * half,
-        (home_slot, cache_len, new_len, page_table, w_out),
+        + [shape((1, q_width), f32), shape((1, kv_width), f32)],
+        (home_slot, cache_len, new_len, page_table, q_gain[None], kv_gain[None]),
         [pltpu.SMEM((page_table.shape[1],), jnp.int32)], 4,
     )
-    columns = columns[:1] + [swap(columns[i], 2 * i) for i in range(1, half)]
     block = call(
         functools.partial(norm_kernel, q_width, kv_width), "norm", shape((own, wide), bf16),
-        (own_cos, own_sin, q_gain[None], kv_gain[None], *partial),
-    )
-    block, *moved = lax.optimization_barrier((block, *moved))
+        (own_cos, own_sin, q_scale, kv_scale, *partial),
+    )
+    blocks = [None] * count
+    for d in range(0, count, 2):
+        blocks[d] = swap(block, d) if d else block
+    block, moved[-1] = lax.optimization_barrier((block, moved[-1]))
+    tied = lax.optimization_barrier((*blocks[2::2], *moved[:-1]))
+    blocks[2::2], moved[:-1] = tied[: half - 1], tied[half - 1 :]
     cache = held
     for d in range(1, rows):
         cache = jnp.where(choice[d, :piece] > 0, moved[d - 1], cache)
-    blocks = [None] * count
     for d in range(0, count, 2):
-        blocks[d] = swap(block, d) if d else block
         blocks[d + 1] = swap(blocks[d], 1)
     pieces = [None] * span
     for d in range(0, span, 2):
@@ -307,17 +337,17 @@
         [
             pltpu.VMEM((group, q_width), f32),
             pltpu.VMEM((span * own, kv_width + ROPE), f32),
-            pltpu.VMEM((kv_width + ROPE, span * piece), bf16),
+            pltpu.VMEM((kv_width + ROPE + EXTRA, span * piece), bf16),
         ],
     )
     states = [state] + [swap(state, d) for d in range(2, count, 2)]
     mine, other = call(
-        functools.partial(out_kernel, span, count, cols), "out",
+        functools.partial(out_kernel, span, count, cols, wide), "out",
         [shape((cols, group), f32), shape((cols, group), bf16)],
-        (alive, *columns, *states),
+        (alive, *partial, *states),
         [
             pltpu.VMEM((half * VDIM, group), bf16),
-            pltpu.VMEM((half * VDIM, 2 * cols), bf16),
+            pltpu.VMEM((half * VDIM, 2 * cols), f32),
         ],
     )
     return (mine + swap(other, 1).astype(f32)).astype(bf16).T

time: 51 us -> 47 us (0.922)
  waiting for transfers between devices: 18.1 us -> 15.9 us
  starting transfers between devices: 23.2 us -> 21.6 us
    ppermute x22 -> x19, starting transfers between devices: 18.5 us -> 16.2 us  [swap(): return lax.ppermute(value, 'col', [(s, s ^ d) for s in range(count)])]
    ppermute x22 -> x19, waiting for transfers between devices: 13.4 us -> 11.1 us  [swap(): return lax.ppermute(value, 'col', [(s, s ^ d) for s in range(count)])]
    ppermute x3, starting transfers between devices: 4.61 us -> 5.41 us  [body(): lax.ppermute(held, 'row', [(s, (s + d) % rows) for s in range(rows)])]
    pallas_call x5 -> x6, Pallas kernels: 5.69 us -> 5.72 us  [call(): pl.pallas_call(kernel, out_shape=shapes, in_specs=[SMEM] * scalars + [VME...]
  transfers between devices with their start and end apart: 25 -> 22, of which waited for: 12 -> 12; matrix products, arithmetic and copies ran while one was open for 0% -> 0% of each run, Pallas kernels for 9% -> 2%
where the time goes in v3:
time: 47 us; the launch traced here: 46.8 us
  starting transfers between devices  21.6 us (46%)
  waiting for transfers between devices  15.9 us (34%)
  Pallas kernels  5.72 us (12%)
  local copies, waits for them, and re-layouts  2.73 us (6%)
  other arithmetic  0.77 us (2%)
    ppermute x19, starting transfers between devices, swap(): return lax.ppermute(value, 'col', [(s, s ^ d) for s in range(count)])  16.2 us
    ppermute x19, waiting for transfers between devices, swap(): return lax.ppermute(value, 'col', [(s, s ^ d) for s in range(count)])  11.1 us
    pallas_call x6, Pallas kernels, call(): pl.pallas_call(kernel, out_shape=shapes, in_specs=[SMEM] * scalars + [VME...  5.72 us
    ppermute x3, starting transfers between devices, body(): lax.ppermute(held, 'row', [(s, (s + d) % rows) for s in range(rows)])  5.41 us
    ppermute x3, waiting for transfers between devices, body(): lax.ppermute(held, 'row', [(s, (s + d) % rows) for s in range(rows)])  4.77 us
    unnamed x24, local copies, waits for them, and re-layouts  2.72 us
  transfers between devices with their start and end apart: 22, of which 12 were waited for; matrix products, arithmetic and copies ran while one was open for 0% of the time, Pallas kernels for 2%

profile of v3, /device:TPU:0, one launch (start us, length us, event | category | flops | bytes accessed | tf_op | source)
XLA Modules:
  0.0 46.8 jit_solution(12373345620738385870)
XLA Ops:
  0.0 1.1 %copy-done = bf16[320,1056]{1,0:T(8,128)(2,1)S(1)} copy-done((bf16[320,1056]{1,0:T(8,128)(2,1)S(1)}, bf16[320,1056]{1,0:T(8,128)(2,1)}, u32[]{:S(2)}) %copy-start) | copy-done | bytes 675864
  1.1 0.9 %copy-done.3 = bf16[256,320]{0,1:T(8,128)(2,1)S(1)} copy-done((bf16[256,320]{0,1:T(8,128)(2,1)S(1)}, bf16[256,320]{0,1:T(8,128)(2,1)}, u32[]{:S(2)}) %copy-start.3) | copy-done | bytes 163864
  2.0 0.6 %down.1 = (bf16[4,32,1056]{2,1,0:T(8,128)(2,1)S(1)}, bf16[4,32,1056]{2,1,0:T(8,128)(2,1)S(1)}) custom-call(bf16[320,256]{1,0:T(8,128)(2,1)S(1)} %bitcast.9, bf16[320,1056]{1,0:T(8,128)(2,1)S(1)} %copy-done), custom_call_target="tpu_custom_call" | custom-call | flops 1000 | bytes 1000 | tf_op jit(solution)/shard_map/down/pallas_call | solution.py:273
  2.6 0.5 %collective-permute-start = (bf16[4,32,1056]{2,1,0:T(8,128)(2,1)S(1)}, bf16[4,32,1056]{2,1,0:T(8,128)(2,1)S(1)}, u32[]{:S(2)}, u32[]{:S(2)}) collective-permute-start(bf16[4,32,1056]{2,1,0:T(8,128)(2,1)S(1)} %get-tuple-element.32), channel_id=1, source_target_pairs={{0,1},{1,0},{2,3},{3,2},{4,5},{5,4},{6,7},{7,6},{8,9},{9,8},{10,11... | collective-permute-start | bytes 811016 | tf_op jit(solution)/shard_map/ppermute | solution.py:269
  3.1 1.2 %collective-permute-done.odd_ref = bf16[4,32,1056]{2,1,0:T(8,128)(2,1)S(1)} collective-permute-done((bf16[4,32,1056]{2,1,0:T(8,128)(2,1)S(1)}, bf16[4,32,1056]{2,1,0:T(8,128)(2,1)S(1)}, u32[]{:S(2)}, u32[]{:S(2)}) %collective-permute-start) | collective-permute-done | bytes 270368 | tf_op jit(solution)/shard_map/ppermute | solution.py:269
  4.5 2.9 %collective-permute-start.1 = (bf16[32,2432]{1,0:T(8,128)(2,1)S(1)}, bf16[32,2432]{1,0:T(8,128)(2,1)S(1)}, u32[]{:S(2)}, u32[]{:S(2)}) collective-permute-start(bf16[32,2432]{1,0:T(8,128)(2,1)S(1)} %get-tuple-element.37), channel_id=1, source_target_pairs={{0,2},{1,3},{2,0},{3,1},{4,6},{5,7},{6,4},{7,5},{8,10},{9,11},{10,... | collective-permute-start | bytes 466952 | tf_op jit(solution)/shard_map/ppermute | solution.py:269
  7.4 1.5 %collective-permute-start.2 = (bf16[32,2432]{1,0:T(8,128)(2,1)S(1)}, bf16[32,2432]{1,0:T(8,128)(2,1)S(1)}, u32[]{:S(2)}, u32[]{:S(2)}) collective-permute-start(bf16[32,2432]{1,0:T(8,128)(2,1)S(1)} %get-tuple-element.38), channel_id=1, source_target_pairs={{0,4},{1,5},{2,6},{3,7},{4,0},{5,1},{6,2},{7,3},{8,12},{9,13},{10,... | collective-permute-start | bytes 466952 | tf_op jit(solution)/shard_map/ppermute | solution.py:269
  8.9 4.1 %collective-permute-start.14 = (bf16[288,256]{1,0:T(8,128)(2,1)S(1)}, bf16[288,256]{1,0:T(8,128)(2,1)S(1)}, u32[]{:S(2)}, u32[]{:S(2)}) collective-permute-start(bf16[288,256]{1,0:T(8,128)(2,1)S(1)} %bitcast.13), channel_id=1, source_target_pairs={{0,24},{8,0},{16,8},{24,16},{1,25},{9,1},{17,9},{25,17},{2,26},{10... | collective-permute-start | bytes 442376 | tf_op jit(solution)/shard_map/ppermute | solution.py:288
  13.0 1.3 %collective-permute-start.9 = (bf16[288,256]{1,0:T(8,128)(2,1)S(1)}, bf16[288,256]{1,0:T(8,128)(2,1)S(1)}, u32[]{:S(2)}, u32[]{:S(2)}) collective-permute-start(bf16[288,256]{1,0:T(8,128)(2,1)S(1)} %bitcast.15), channel_id=1, source_target_pairs={{0,8},{8,16},{16,24},{24,0},{1,9},{9,17},{17,25},{25,1},{2,10},{10... | collective-permute-start | bytes 442376 | tf_op jit(solution)/shard_map/ppermute | solution.py:288
  14.4 0.6 %copy-done.5 = s32[4,32]{1,0:T(4,128)S(1)} copy-done((s32[4,32]{1,0:T(4,128)S(1)}, s32[4,32]{1,0:T(4,128)}, u32[]{:S(2)}) %copy-start.5) | copy-done | bytes 536
  15.0 0.8 %prepare.1 = (f32[32,16]{1,0:T(8,128)S(1)}, f32[32,16]{1,0:T(8,128)S(1)}, f32[16,256]{1,0:T(8,128)S(1)}, f32[16,256]{1,0:T(8,128)S(1)}, bf16[16,1024]{1,0:T(8,12...) custom-call(s32[4]{0:T(128)S(1)} %copy-done.7, ...), custom_call_target="tpu_custom_call" | custom-call | flops 1000 | bytes 1000 | tf_op jit(solution)/shard_map/prepare/pallas_call | solution.py:273
  15.9 0.6 %collective-permute-done.2.refs_2_ = bf16[32,2432]{1,0:T(8,128)(2,1)S(1)} collective-permute-done((bf16[32,2432]{1,0:T(8,128)(2,1)S(1)}, bf16[32,2432]{1,0:T(8,128)(2,1)S(1)}, u32[]{:S(2)}, u32[]{:S(2)}) %collective-permute-start.2) | collective-permute-done | bytes 155680 | tf_op jit(solution)/shard_map/ppermute | solution.py:269
  16.7 1.9 %collective-permute-start.8 = (bf16[32,1056]{1,0:T(8,128)(2,1)S(1)}, bf16[32,1056]{1,0:T(8,128)(2,1)S(1)}, u32[]{:S(2)}, u32[]{:S(2)}) collective-permute-start(bf16[32,1056]{1,0:T(8,128)(2,1)S(1)} %norm.1.refs_2_), channel_id=1, source_target_pairs={{0,6},{1,7},{2,4},{3,5},{4,2},{5,3},{6,0},{7,1},{8,14},{9,15},{10,... | collective-permute-start | bytes 202760 | tf_op jit(solution)/shard_map/ppermute | solution.py:269
  18.6 0.9 %collective-permute-start.7 = (bf16[32,1056]{1,0:T(8,128)(2,1)S(1)}, bf16[32,1056]{1,0:T(8,128)(2,1)S(1)}, u32[]{:S(2)}, u32[]{:S(2)}) collective-permute-start(bf16[32,1056]{1,0:T(8,128)(2,1)S(1)} %norm.1.refs_2_), channel_id=1, source_target_pairs={{0,4},{1,5},{2,6},{3,7},{4,0},{5,1},{6,2},{7,3},{8,12},{9,13},{10,... | collective-permute-start | bytes 202760 | tf_op jit(solution)/shard_map/ppermute | solution.py:269
  19.4 0.8 %collective-permute-start.6 = (bf16[32,1056]{1,0:T(8,128)(2,1)S(1)}, bf16[32,1056]{1,0:T(8,128)(2,1)S(1)}, u32[]{:S(2)}, u32[]{:S(2)}) collective-permute-start(bf16[32,1056]{1,0:T(8,128)(2,1)S(1)} %norm.1.refs_2_), channel_id=1, source_target_pairs={{0,2},{1,3},{2,0},{3,1},{4,6},{5,7},{6,4},{7,5},{8,10},{9,11},{10,... | collective-permute-start | bytes 202760 | tf_op jit(solution)/shard_map/ppermute | solution.py:269
  20.3 4.8 %collective-permute-done.10 = bf16[288,256]{1,0:T(8,128)(2,1)S(1)} collective-permute-done((bf16[288,256]{1,0:T(8,128)(2,1)S(1)}, bf16[288,256]{1,0:T(8,128)(2,1)S(1)}, u32[]{:S(2)}, u32[]{:S(2)}) %collective-permute-start.10) | collective-permute-done | bytes 147488 | tf_op jit(solution)/shard_map/ppermute | solution.py:288
  25.1 1.6 %collective-permute-start.16 = (bf16[288,256]{1,0:T(8,128)(2,1)S(1)}, bf16[288,256]{1,0:T(8,128)(2,1)S(1)}, u32[]{:S(2)}, u32[]{:S(2)}) collective-permute-start(bf16[288,256]{1,0:T(8,128)(2,1)S(1)} %select_select_fusion.refs_10_), channel_id=1, source_target_pairs={{0,2},{1,3},{2,0},{3,1},{4,6},{5,7},{6,4},{7,5},{8,10},{9,11},{10,... | collective-permute-start | bytes 442376 | tf_op jit(solution)/shard_map/ppermute | solution.py:269
  26.7 1.5 %collective-permute-start.4 = (bf16[96,768]{1,0:T(8,128)(2,1)S(1)}, bf16[96,768]{1,0:T(8,128)(2,1)S(1)}, u32[]{:S(2)}, u32[]{:S(2)}) collective-permute-start(bf16[96,768]{1,0:T(8,128)(2,1)S(1)} %bitcast.10), channel_id=1, source_target_pairs={{0,4},{1,5},{2,6},{3,7},{4,0},{5,1},{6,2},{7,3},{8,12},{9,13},{10,... | collective-permute-start | bytes 442376 | tf_op jit(solution)/shard_map/ppermute | solution.py:269
  28.2 2.2 %collective-permute-done.16.refs_12_ = bf16[288,256]{1,0:T(8,128)(2,1)S(1)} collective-permute-done((bf16[288,256]{1,0:T(8,128)(2,1)S(1)}, bf16[288,256]{1,0:T(8,128)(2,1)S(1)}, u32[]{:S(2)}, u32[]{:S(2)}) %collective-permute-start.16) | collective-permute-done | bytes 147488 | tf_op jit(solution)/shard_map/ppermute | solution.py:269
  30.4 0.5 %collective-permute-start.5 = (bf16[32,1056]{1,0:T(8,128)(2,1)S(1)}, bf16[32,1056]{1,0:T(8,128)(2,1)S(1)}, u32[]{:S(2)}, u32[]{:S(2)}) collective-permute-start(bf16[32,1056]{1,0:T(8,128)(2,1)S(1)} %norm.1.refs_2_), channel_id=1, source_target_pairs={{0,1},{1,0},{2,3},{3,2},{4,5},{5,4},{6,7},{7,6},{8,9},{9,8},{10,11... | collective-permute-start | bytes 202760 | tf_op jit(solution)/shard_map/ppermute | solution.py:269
  30.9 0.9 %collective-permute-done.4.refs_1_ = bf16[96,768]{1,0:T(8,128)(2,1)S(1)} collective-permute-done((bf16[96,768]{1,0:T(8,128)(2,1)S(1)}, bf16[96,768]{1,0:T(8,128)(2,1)S(1)}, u32[]{:S(2)}, u32[]{:S(2)}) %collective-permute-start.4) | collective-permute-done | bytes 147488 | tf_op jit(solution)/shard_map/ppermute | solution.py:269
  31.9 0.4 collective-permute-start.13
  32.3 0.7 %collective-permute-done.12.refs_7_ = bf16[32,1056]{1,0:T(8,128)(2,1)S(1)} collective-permute-done((bf16[32,1056]{1,0:T(8,128)(2,1)S(1)}, bf16[32,1056]{1,0:T(8,128)(2,1)S(1)}, u32[]{:S(2)}, u32[]{:S(2)}) %collective-permute-start.12) | collective-permute-done | bytes 67616 | tf_op jit(solution)/shard_map/ppermute | solution.py:269
  33.2 3.7 %attend.1.refs_4_ = bf16[144,256]{1,0:T(8,128)(2,1)S(1)} custom-call(f32[16,256]{1,0:T(8,128)S(1)} %get-tuple-element.40.cos_ref, f32[16,256]{1,0:T(8,128)S(1)} %get-tuple-element.41.sin_ref, bf16[16,1024]{1,0:T(8,128)(2,1)S(1)} %get-tuple-element.42.limits, f32[128,256]{1,0:T(8,128)S(1)} %get-tuple-element.43.fresh_limits, bf16[256,1024]{1,0:T(8,128)(2,1)S(1)} %copy-done.1, ...), custom_call_target="tpu_custom_call" | custom-call | flops 1000 | bytes 1000 | tf_op jit(solution)/shard_map/attend/pallas_call | solution.py:273
  37.0 2.5 %collective-permute-start.20 = (bf16[144,256]{1,0:T(8,128)(2,1)S(1)}, bf16[144,256]{1,0:T(8,128)(2,1)S(1)}, u32[]{:S(2)}, u32[]{:S(2)}) collective-permute-start(bf16[144,256]{1,0:T(8,128)(2,1)S(1)} %attend.1.refs_4_), channel_id=1, source_target_pairs={{0,6},{1,7},{2,4},{3,5},{4,2},{5,3},{6,0},{7,1},{8,14},{9,15},{10,... | collective-permute-start | bytes 221192 | tf_op jit(solution)/shard_map/ppermute | solution.py:269
  39.4 0.5 %collective-permute-start.19 = (bf16[144,256]{1,0:T(8,128)(2,1)S(1)}, bf16[144,256]{1,0:T(8,128)(2,1)S(1)}, u32[]{:S(2)}, u32[]{:S(2)}) collective-permute-start(bf16[144,256]{1,0:T(8,128)(2,1)S(1)} %attend.1.refs_4_), channel_id=1, source_target_pairs={{0,4},{1,5},{2,6},{3,7},{4,0},{5,1},{6,2},{7,3},{8,12},{9,13},{10,... | collective-permute-start | bytes 221192 | tf_op jit(solution)/shard_map/ppermute | solution.py:269
  39.9 0.6 %collective-permute-start.18 = (bf16[144,256]{1,0:T(8,128)(2,1)S(1)}, bf16[144,256]{1,0:T(8,128)(2,1)S(1)}, u32[]{:S(2)}, u32[]{:S(2)}) collective-permute-start(bf16[144,256]{1,0:T(8,128)(2,1)S(1)} %attend.1.refs_4_), channel_id=1, source_target_pairs={{0,2},{1,3},{2,0},{3,1},{4,6},{5,7},{6,4},{7,5},{8,10},{9,11},{10,... | collective-permute-start | bytes 221192 | tf_op jit(solution)/shard_map/ppermute | solution.py:269
  40.6 2.0 %collective-permute-done.20.refs_7_ = bf16[144,256]{1,0:T(8,128)(2,1)S(1)} collective-permute-done((bf16[144,256]{1,0:T(8,128)(2,1)S(1)}, bf16[144,256]{1,0:T(8,128)(2,1)S(1)}, u32[]{:S(2)}, u32[]{:S(2)}) %collective-permute-start.20) | collective-permute-done | bytes 73760 | tf_op jit(solution)/shard_map/ppermute | solution.py:269
  42.5 1.5 %collective-permute-done.19.refs_6_ = bf16[144,256]{1,0:T(8,128)(2,1)S(1)} collective-permute-done((bf16[144,256]{1,0:T(8,128)(2,1)S(1)}, bf16[144,256]{1,0:T(8,128)(2,1)S(1)}, u32[]{:S(2)}, u32[]{:S(2)}) %collective-permute-start.19) | collective-permute-done | bytes 73760 | tf_op jit(solution)/shard_map/ppermute | solution.py:269
  44.3 0.4 out.1
  44.7 1.4 %collective-permute-done.21 = bf16[320,256]{1,0:T(8,128)(2,1)S(1)} collective-permute-done((bf16[320,256]{1,0:T(8,128)(2,1)S(1)}, bf16[320,256]{1,0:T(8,128)(2,1)S(1)}, u32[]{:S(2)}, u32[]{:S(2)}) %collective-permute-start.21) | collective-permute-done | bytes 163872 | tf_op jit(solution)/shard_map/ppermute | solution.py:269
  46.1 0.7 %fusion = bf16[256,320]{0,1:T(8,128)(2,1)} fusion(f32[320,256]{1,0:T(8,128)S(1)} %get-tuple-element.55, bf16[320,256]{1,0:T(8,128)(2,1)S(1)} %collective-permute-done.21), kind=kLoop, calls=%fused_computation.1 | loop fusion | flops 245760 | bytes 655360 | tf_op jit(solution)/shard_map/transpose | solution.py:353
  (46 shorter events, 1.0 us)
Async XLA Ops:
  0.0 1.1 %copy-start = (bf16[320,1056]{1,0:T(8,128)(2,1)S(1)}, bf16[320,1056]{1,0:T(8,128)(2,1)}, u32[]{:S(2)}) copy-start(bf16[320,1056]{1,0:T(8,128)(2,1)} %w_ref.1) | copy-start | bytes 2027524
  1.1 0.9 %copy-start.3 = (bf16[256,320]{0,1:T(8,128)(2,1)S(1)}, bf16[256,320]{0,1:T(8,128)(2,1)}, u32[]{:S(2)}) copy-start(bf16[256,320]{0,1:T(8,128)(2,1)} %param.12) | copy-start | bytes 491524
  2.0 2.3 %copy-start.2 = (bf16[64,2560]{1,0:T(8,128)(2,1)S(1)}, bf16[64,2560]{1,0:T(8,128)(2,1)}, u32[]{:S(2)}) copy-start(bf16[64,2560]{1,0:T(8,128)(2,1)} %w_out_ref.1) | copy-start | bytes 983044
  2.6 1.7 %collective-permute-start = (bf16[4,32,1056]{2,1,0:T(8,128)(2,1)S(1)}, bf16[4,32,1056]{2,1,0:T(8,128)(2,1)S(1)}, u32[]{:S(2)}, u32[]{:S(2)}) collective-permute-start(bf16[4,32,1056]{2,1,0:T(8,128)(2,1)S(1)} %get-tuple-element.32), channel_id=1, source_target_pairs={{0,1},{1,0},{2,3},{3,2},{4,5},{5,4},{6,7},{7,6},{8,9},{9,8},{10,11... | collective-permute-start | bytes 811016 | tf_op jit(solution)/shard_map/ppermute | solution.py:269
  4.4 4.6 %copy-start.10 = (bf16[1,256,288]{1,2,0:T(8,128)(2,1)S(1)}, bf16[1,256,288]{1,2,0:T(8,128)(2,1)}, u32[]{:S(2)}) copy-start(bf16[1,256,288]{1,2,0:T(8,128)(2,1)} %param.19) | copy-start | bytes 442372
  4.4 10.0 %copy-start.8 = (s32[4]{0:T(128)S(1)}, s32[4]{0:T(128)}, u32[]{:S(2)}) copy-start(s32[4]{0:T(128)} %cached_ref.1) | copy-start | bytes 52
  4.4 10.0 %copy-start.9 = (s32[4]{0:T(128)S(1)}, s32[4]{0:T(128)}, u32[]{:S(2)}) copy-start(s32[4]{0:T(128)} %live_ref.1) | copy-start | bytes 52
  4.4 9.9 %copy-start.11 = (f32[768]{0:T(1024)S(1)}, f32[768]{0:T(1024)}, u32[]{:S(2)}) copy-start(f32[768]{0:T(1024)} %param.14) | copy-start | bytes 9220
  4.5 8.5 %collective-permute-start.1 = (bf16[32,2432]{1,0:T(8,128)(2,1)S(1)}, bf16[32,2432]{1,0:T(8,128)(2,1)S(1)}, u32[]{:S(2)}, u32[]{:S(2)}) collective-permute-start(bf16[32,2432]{1,0:T(8,128)(2,1)S(1)} %get-tuple-element.37), channel_id=1, source_target_pairs={{0,2},{1,3},{2,0},{3,1},{4,6},{5,7},{6,4},{7,5},{8,10},{9,11},{10,... | collective-permute-start | bytes 466952 | tf_op jit(solution)/shard_map/ppermute | solution.py:269
  7.4 9.1 %collective-permute-start.2 = (bf16[32,2432]{1,0:T(8,128)(2,1)S(1)}, bf16[32,2432]{1,0:T(8,128)(2,1)S(1)}, u32[]{:S(2)}, u32[]{:S(2)}) collective-permute-start(bf16[32,2432]{1,0:T(8,128)(2,1)S(1)} %get-tuple-element.38), channel_id=1, source_target_pairs={{0,4},{1,5},{2,6},{3,7},{4,0},{5,1},{6,2},{7,3},{8,12},{9,13},{10,... | collective-permute-start | bytes 466952 | tf_op jit(solution)/shard_map/ppermute | solution.py:269
  8.9 7.6 %collective-permute-start.3 = (bf16[32,2432]{1,0:T(8,128)(2,1)S(1)}, bf16[32,2432]{1,0:T(8,128)(2,1)S(1)}, u32[]{:S(2)}, u32[]{:S(2)}) collective-permute-start(bf16[32,2432]{1,0:T(8,128)(2,1)S(1)} %get-tuple-element.39), channel_id=1, source_target_pairs={{0,6},{1,7},{2,4},{3,5},{4,2},{5,3},{6,0},{7,1},{8,14},{9,15},{10,... | collective-permute-start | bytes 466952 | tf_op jit(solution)/shard_map/ppermute | solution.py:269
  8.9 10.5 %collective-permute-start.14 = (bf16[288,256]{1,0:T(8,128)(2,1)S(1)}, bf16[288,256]{1,0:T(8,128)(2,1)S(1)}, u32[]{:S(2)}, u32[]{:S(2)}) collective-permute-start(bf16[288,256]{1,0:T(8,128)(2,1)S(1)} %bitcast.13), channel_id=1, source_target_pairs={{0,24},{8,0},{16,8},{24,16},{1,25},{9,1},{17,9},{25,17},{2,26},{10... | collective-permute-start | bytes 442376 | tf_op jit(solution)/shard_map/ppermute | solution.py:288
  13.0 12.0 %collective-permute-start.10 = (bf16[288,256]{1,0:T(8,128)(2,1)S(1)}, bf16[288,256]{1,0:T(8,128)(2,1)S(1)}, u32[]{:S(2)}, u32[]{:S(2)}) collective-permute-start(bf16[288,256]{1,0:T(8,128)(2,1)S(1)} %bitcast.14), channel_id=1, source_target_pairs={{0,16},{8,24},{16,0},{24,8},{1,17},{9,25},{17,1},{25,9},{2,18},{10... | collective-permute-start | bytes 442376 | tf_op jit(solution)/shard_map/ppermute | solution.py:288
  13.0 12.0 %collective-permute-start.9 = (bf16[288,256]{1,0:T(8,128)(2,1)S(1)}, bf16[288,256]{1,0:T(8,128)(2,1)S(1)}, u32[]{:S(2)}, u32[]{:S(2)}) collective-permute-start(bf16[288,256]{1,0:T(8,128)(2,1)S(1)} %bitcast.15), channel_id=1, source_target_pairs={{0,8},{8,16},{16,24},{24,0},{1,9},{9,17},{17,25},{25,1},{2,10},{10... | collective-permute-start | bytes 442376 | tf_op jit(solution)/shard_map/ppermute | solution.py:288
  14.4 0.7 %copy-start.6 = (f32[256]{0:T(256)S(1)}, f32[256]{0:T(256)}, u32[]{:S(2)}) copy-start(f32[256]{0:T(256)} %param.15) | copy-start | bytes 3076
  16.7 16.6 %copy-start.1 = (bf16[256,1024]{1,0:T(8,128)(2,1)S(1)}, bf16[256,1024]{1,0:T(8,128)(2,1)}, u32[]{:S(2)}) copy-start(bf16[256,1024]{1,0:T(8,128)(2,1)} %w_kv_ref.1) | copy-start | bytes 1572868
  16.7 8.4 %collective-permute-start.8 = (bf16[32,1056]{1,0:T(8,128)(2,1)S(1)}, bf16[32,1056]{1,0:T(8,128)(2,1)S(1)}, u32[]{:S(2)}, u32[]{:S(2)}) collective-permute-start(bf16[32,1056]{1,0:T(8,128)(2,1)S(1)} %norm.1.refs_2_), channel_id=1, source_target_pairs={{0,6},{1,7},{2,4},{3,5},{4,2},{5,3},{6,0},{7,1},{8,14},{9,15},{10,... | collective-permute-start | bytes 202760 | tf_op jit(solution)/shard_map/ppermute | solution.py:269
  18.6 6.5 %collective-permute-start.7 = (bf16[32,1056]{1,0:T(8,128)(2,1)S(1)}, bf16[32,1056]{1,0:T(8,128)(2,1)S(1)}, u32[]{:S(2)}, u32[]{:S(2)}) collective-permute-start(bf16[32,1056]{1,0:T(8,128)(2,1)S(1)} %norm.1.refs_2_), channel_id=1, source_target_pairs={{0,4},{1,5},{2,6},{3,7},{4,0},{5,1},{6,2},{7,3},{8,12},{9,13},{10,... | collective-permute-start | bytes 202760 | tf_op jit(solution)/shard_map/ppermute | solution.py:269
  19.4 5.6 %collective-permute-start.6 = (bf16[32,1056]{1,0:T(8,128)(2,1)S(1)}, bf16[32,1056]{1,0:T(8,128)(2,1)S(1)}, u32[]{:S(2)}, u32[]{:S(2)}) collective-permute-start(bf16[32,1056]{1,0:T(8,128)(2,1)S(1)} %norm.1.refs_2_), channel_id=1, source_target_pairs={{0,2},{1,3},{2,0},{3,1},{4,6},{5,7},{6,4},{7,5},{8,10},{9,11},{10,... | collective-permute-start | bytes 202760 | tf_op jit(solution)/shard_map/ppermute | solution.py:269
  25.0 1.6 %copy-start.4 = (bf16[768,96]{0,1:T(8,128)(2,1)S(1)}, bf16[768,96]{0,1:T(8,128)(2,1)}, u32[]{:S(2)}) copy-start(bf16[768,96]{0,1:T(8,128)(2,1)} %param.16) | copy-start | bytes 442372
  25.1 5.3 %collective-permute-start.16 = (bf16[288,256]{1,0:T(8,128)(2,1)S(1)}, bf16[288,256]{1,0:T(8,128)(2,1)S(1)}, u32[]{:S(2)}, u32[]{:S(2)}) collective-permute-start(bf16[288,256]{1,0:T(8,128)(2,1)S(1)} %select_select_fusion.refs_10_), channel_id=1, source_target_pairs={{0,2},{1,3},{2,0},{3,1},{4,6},{5,7},{6,4},{7,5},{8,10},{9,11},{10,... | collective-permute-start | bytes 442376 | tf_op jit(solution)/shard_map/ppermute | solution.py:269
  26.7 5.1 %collective-permute-start.4 = (bf16[96,768]{1,0:T(8,128)(2,1)S(1)}, bf16[96,768]{1,0:T(8,128)(2,1)S(1)}, u32[]{:S(2)}, u32[]{:S(2)}) collective-permute-start(bf16[96,768]{1,0:T(8,128)(2,1)S(1)} %bitcast.10), channel_id=1, source_target_pairs={{0,4},{1,5},{2,6},{3,7},{4,0},{5,1},{6,2},{7,3},{8,12},{9,13},{10,... | collective-permute-start | bytes 442376 | tf_op jit(solution)/shard_map/ppermute | solution.py:269
  28.2 5.1 %collective-permute-start.15 = (bf16[288,256]{1,0:T(8,128)(2,1)S(1)}, bf16[288,256]{1,0:T(8,128)(2,1)S(1)}, u32[]{:S(2)}, u32[]{:S(2)}) collective-permute-start(bf16[288,256]{1,0:T(8,128)(2,1)S(1)} %select_select_fusion.refs_10_), channel_id=1, source_target_pairs={{0,1},{1,0},{2,3},{3,2},{4,5},{5,4},{6,7},{7,6},{8,9},{9,8},{10,11... | collective-permute-start | bytes 442376 | tf_op jit(solution)/shard_map/ppermute | solution.py:269
  30.4 2.8 %collective-permute-start.17 = (bf16[288,256]{1,0:T(8,128)(2,1)S(1)}, bf16[288,256]{1,0:T(8,128)(2,1)S(1)}, u32[]{:S(2)}, u32[]{:S(2)}) collective-permute-start(bf16[288,256]{1,0:T(8,128)(2,1)S(1)} %collective-permute-done.16.refs_12_), channel_id=1, source_target_pairs={{0,1},{1,0},{2,3},{3,2},{4,5},{5,4},{6,7},{7,6},{8,9},{9,8},{10,11... | collective-permute-start | bytes 442376 | tf_op jit(solution)/shard_map/ppermute | solution.py:269
  30.4 1.5 %collective-permute-start.5 = (bf16[32,1056]{1,0:T(8,128)(2,1)S(1)}, bf16[32,1056]{1,0:T(8,128)(2,1)S(1)}, u32[]{:S(2)}, u32[]{:S(2)}) collective-permute-start(bf16[32,1056]{1,0:T(8,128)(2,1)S(1)} %norm.1.refs_2_), channel_id=1, source_target_pairs={{0,1},{1,0},{2,3},{3,2},{4,5},{5,4},{6,7},{7,6},{8,9},{9,8},{10,11... | collective-permute-start | bytes 202760 | tf_op jit(solution)/shard_map/ppermute | solution.py:269
  30.9 1.4 %collective-permute-start.11 = (bf16[32,1056]{1,0:T(8,128)(2,1)S(1)}, bf16[32,1056]{1,0:T(8,128)(2,1)S(1)}, u32[]{:S(2)}, u32[]{:S(2)}) collective-permute-start(bf16[32,1056]{1,0:T(8,128)(2,1)S(1)} %collective-permute-done.6.refs_4_), channel_id=1, source_target_pairs={{0,1},{1,0},{2,3},{3,2},{4,5},{5,4},{6,7},{7,6},{8,9},{9,8},{10,11... | collective-permute-start | bytes 202760 | tf_op jit(solution)/shard_map/ppermute | solution.py:269
  31.8 1.3 %collective-permute-start.12 = (bf16[32,1056]{1,0:T(8,128)(2,1)S(1)}, bf16[32,1056]{1,0:T(8,128)(2,1)S(1)}, u32[]{:S(2)}, u32[]{:S(2)}) collective-permute-start(bf16[32,1056]{1,0:T(8,128)(2,1)S(1)} %collective-permute-done.7.refs_6_), channel_id=1, source_target_pairs={{0,1},{1,0},{2,3},{3,2},{4,5},{5,4},{6,7},{7,6},{8,9},{9,8},{10,11... | collective-permute-start | bytes 202760 | tf_op jit(solution)/shard_map/ppermute | solution.py:269
  31.9 1.3 %collective-permute-start.13 = (bf16[32,1056]{1,0:T(8,128)(2,1)S(1)}, bf16[32,1056]{1,0:T(8,128)(2,1)S(1)}, u32[]{:S(2)}, u32[]{:S(2)}) collective-permute-start(bf16[32,1056]{1,0:T(8,128)(2,1)S(1)} %collective-permute-done.8.refs_8_), channel_id=1, source_target_pairs={{0,1},{1,0},{2,3},{3,2},{4,5},{5,4},{6,7},{7,6},{8,9},{9,8},{10,11... | collective-permute-start | bytes 202760 | tf_op jit(solution)/shard_map/ppermute | solution.py:269
  37.0 5.5 %collective-permute-start.20 = (bf16[144,256]{1,0:T(8,128)(2,1)S(1)}, bf16[144,256]{1,0:T(8,128)(2,1)S(1)}, u32[]{:S(2)}, u32[]{:S(2)}) collective-permute-start(bf16[144,256]{1,0:T(8,128)(2,1)S(1)} %attend.1.refs_4_), channel_id=1, source_target_pairs={{0,6},{1,7},{2,4},{3,5},{4,2},{5,3},{6,0},{7,1},{8,14},{9,15},{10,... | collective-permute-start | bytes 221192 | tf_op jit(solution)/shard_map/ppermute | solution.py:269
  39.4 4.6 %collective-permute-start.19 = (bf16[144,256]{1,0:T(8,128)(2,1)S(1)}, bf16[144,256]{1,0:T(8,128)(2,1)S(1)}, u32[]{:S(2)}, u32[]{:S(2)}) collective-permute-start(bf16[144,256]{1,0:T(8,128)(2,1)S(1)} %attend.1.refs_4_), channel_id=1, source_target_pairs={{0,4},{1,5},{2,6},{3,7},{4,0},{5,1},{6,2},{7,3},{8,12},{9,13},{10,... | collective-permute-start | bytes 221192 | tf_op jit(solution)/shard_map/ppermute | solution.py:269
  39.9 4.4 %collective-permute-start.18 = (bf16[144,256]{1,0:T(8,128)(2,1)S(1)}, bf16[144,256]{1,0:T(8,128)(2,1)S(1)}, u32[]{:S(2)}, u32[]{:S(2)}) collective-permute-start(bf16[144,256]{1,0:T(8,128)(2,1)S(1)} %attend.1.refs_4_), channel_id=1, source_target_pairs={{0,2},{1,3},{2,0},{3,1},{4,6},{5,7},{6,4},{7,5},{8,10},{9,11},{10,... | collective-permute-start | bytes 221192 | tf_op jit(solution)/shard_map/ppermute | solution.py:269
  44.7 1.5 %collective-permute-start.21 = (bf16[320,256]{1,0:T(8,128)(2,1)S(1)}, bf16[320,256]{1,0:T(8,128)(2,1)S(1)}, u32[]{:S(2)}, u32[]{:S(2)}) collective-permute-start(bf16[320,256]{1,0:T(8,128)(2,1)S(1)} %get-tuple-element.56), channel_id=1, source_target_pairs={{0,1},{1,0},{2,3},{3,2},{4,5},{5,4},{6,7},{7,6},{8,9},{9,8},{10,11... | collective-permute-start | bytes 491528 | tf_op jit(solution)/shard_map/ppermute | solution.py:269
  (2 other events, 1.4 us)

commit v4 on v3

--- a/solution.py
+++ b/solution.py
@@ -124,7 +124,7 @@
 
 def norm_kernel(q_width, kv_width, cos_ref, sin_ref, q_gain_ref, kv_gain_ref, *refs):
     out_ref = refs[-1]
-    wide = out_ref.shape[1]
+    wide = q_width + kv_width + ROPE
     total = refs[0][:, :wide].astype(f32)
     for ref in refs[1:-1]:
         total += ref[:, :wide].astype(f32)
@@ -137,9 +137,10 @@
     out_ref[:, q_width : q_width + kv_width] = scaled(
         total[:, q_width : q_width + kv_width], kv_gain_ref[...]
     ).astype(bf16)
-    out_ref[:, q_width + kv_width :] = rotate(
+    out_ref[:, q_width + kv_width : wide] = rotate(
         total[:, q_width + kv_width :], cos_ref[...], sin_ref[...], 1
     ).astype(bf16)
+    out_ref[:, wide:] = jnp.zeros_like(out_ref[:, wide:])
 
 
 def split3(value):
@@ -148,64 +149,118 @@
     return [high, middle, value - high - middle]
 
 
-def attend_kernel(
+def weigh(query, keys, fresh, fresh_bias, kv_width):
+    scale = 1.0 / math.sqrt(NOPE + ROPE)
+    scores = [
+        lax.dot_general(keys, query, (((0,), (0,)), ((), ())), preferred_element_type=f32)
+    ]
+    if fresh is not None:
+        new = jnp.dot(fresh, query[: fresh.shape[1]], preferred_element_type=f32)
+        scores.append(new + jnp.concatenate([fresh_bias] * (new.shape[1] // fresh_bias.shape[1]), 1))
+    peak = functools.reduce(jnp.maximum, [jnp.max(s, 0, keepdims=True) for s in scores])
+    peak = jnp.maximum(peak, FLOOR)
+    weights = [jnp.exp((s - peak) * scale) for s in scores]
+    total = sum(jnp.sum(w, 0, keepdims=True) for w in weights)
+    mixed = jnp.dot(keys[:kv_width], weights[0].astype(bf16), preferred_element_type=f32)
+    if fresh is not None:
+        mixed += lax.dot_general(
+            fresh[:, :kv_width], weights[1].astype(bf16),
+            (((0,), (0,)), ((), ())), preferred_element_type=f32,
+        )
+    return peak, total, mixed.astype(bf16)
+
+
+def lifted(w_kv_ref, column, k, span):
+    head = column ^ (k * span)
+    return w_kv_ref[:, pl.ds(pl.multiple_of(head * HEAD, HEAD), HEAD)]
+
+
+def begin_kernel(
     span, count, own, q_width, kv_width, cos_ref, sin_ref, limits, fresh_limits, w_kv_ref, *refs
 ):
     heads = count // span
     weights, refs = refs[:heads], refs[heads:]
     blocks, refs = refs[:count], refs[count:]
-    pieces, (out_ref, query_rows, fresh, keys) = refs[:span], refs[span:]
+    pieces, (query_ref, summed_ref, peak_ref, total_ref, query_rows, fresh, keys) = refs[:2], refs[2:]
     column = lax.axis_index("col")
     group = count * own
     piece = pieces[0].shape[1]
-    held = span * piece
+    wide = kv_width + ROPE
     for j in range(count):
         start = pl.multiple_of((column ^ j) * own, own)
-        query_rows[pl.ds(start, own), :] = blocks[j][:, :q_width].astype(f32)
+        query_rows[pl.ds(start, own), :] = blocks[j][:, :q_width].astype(query_rows.dtype)
         if j < span:
-            fresh[j * own : (j + 1) * own, :] = blocks[j][:, q_width:].astype(f32)
-    for j in range(span):
-        keys[: kv_width + ROPE, j * piece : (j + 1) * piece] = pieces[j][...]
-    keys[kv_width + ROPE :, :] = limits[...]
-    fresh_keys = fresh[...].astype(bf16)
+            fresh[j * own : (j + 1) * own, :] = blocks[j][:, q_width : q_width + wide].astype(fresh.dtype)
+    for j in range(2):
+        keys[:wide, j * piece : (j + 1) * piece] = pieces[j][...]
+    keys[wide:, :] = limits[:, : 2 * piece]
     latent = query_rows[...].astype(bf16)
-    scale = 1.0 / math.sqrt(NOPE + ROPE)
     line = lax.broadcasted_iota(jnp.int32, (EXTRA, group), 0)
     first_row = jnp.where(line == 0, 1.0, 0.0).astype(bf16)
+    for k in range(heads):
+        projected = lax.dot_general(
+            weights[k][...], latent, (((1,), (1,)), ((), ())), preferred_element_type=f32
+        )
+        turned = rotate(projected[NOPE:], cos_ref[...], sin_ref[...], 0)
+        plain = jnp.dot(
+            lifted(w_kv_ref, column, k, span)[:, :NOPE],
+            projected[:NOPE].astype(bf16), preferred_element_type=f32,
+        )
+        lanes = slice(k * group, (k + 1) * group)
+        query_ref[:kv_width, lanes] = plain.astype(bf16)
+        query_ref[kv_width:wide, lanes] = turned.astype(bf16)
+        query_ref[wide:, lanes] = first_row
+    peak, total, mixed = weigh(
+        query_ref[...], keys[...], fresh[...].astype(bf16), fresh_limits[...], kv_width
+    )
+    peak_ref[...] = peak
+    total_ref[...] = total
+    for k in range(heads):
+        summed = lax.dot_general(
+            lifted(w_kv_ref, column, k, span), mixed[:, k * group : (k + 1) * group],
+            (((0,), (0,)), ((), ())), preferred_element_type=f32,
+        )
+        summed_ref[k * VDIM : (k + 1) * VDIM, :] = summed[NOPE:]
+
+
+def further_kernel(
+    span, count, kv_width, last, query_ref, summed_ref, peak_ref, total_ref, limits, w_kv_ref,
+    piece_ref, *refs,
+):
+    outs, keys = refs[:-1], refs[-1]
+    heads = count // span
+    column = lax.axis_index("col")
+    group = summed_ref.shape[1]
+    wide = kv_width + ROPE
+    keys[:wide, :] = piece_ref[...]
+    keys[wide:, :] = limits[...]
+    peak, total, mixed = weigh(query_ref[...], keys[...], None, None, kv_width)
+    scale = 1.0 / math.sqrt(NOPE + ROPE)
+    top = jnp.maximum(peak, peak_ref[...])
+    before = jnp.exp((peak_ref[...] - top) * scale)
+    after = jnp.exp((peak - top) * scale)
+    total = total_ref[...] * before + total * after
     stats = []
     for k in range(heads):
-        head = column ^ (k * span)
-        lift = w_kv_ref[:, pl.ds(pl.multiple_of(head * HEAD, HEAD), HEAD)]
-        projected = lax.dot_general(
-            weights[k][...], latent, (((1,), (1,)), ((), ())), preferred_element_type=f32
-        )
-        turned = rotate(projected[NOPE:], cos_ref[...], sin_ref[...], 0)
-        plain = jnp.dot(
-            lift[:, :NOPE], projected[:NOPE].astype(bf16), preferred_element_type=f32
-        )
-        query = jnp.concatenate([plain.astype(bf16), turned.astype(bf16)], axis=0)
-        old = lax.dot_general(
-            keys[...], jnp.concatenate([query, first_row], axis=0),
+        lanes = slice(k * group, (k + 1) * group)
+        summed = lax.dot_general(
+            lifted(w_kv_ref, column, k, span), mixed[:, lanes],
             (((0,), (0,)), ((), ())), preferred_element_type=f32,
         )
-        new = jnp.dot(fresh_keys, query, preferred_element_type=f32) + fresh_limits[...]
-        peak = jnp.maximum(jnp.max(old, 0, keepdims=True), jnp.max(new, 0, keepdims=True))
-        peak = jnp.maximum(peak, FLOOR)
-        old = jnp.exp((old - peak) * scale)
-        new = jnp.exp((new - peak) * scale)
-        total = jnp.sum(old, 0, keepdims=True) + jnp.sum(new, 0, keepdims=True)
-        mixed = jnp.dot(
-            keys[:kv_width, :], old.astype(bf16), preferred_element_type=f32
-        ) + lax.dot_general(
-            fresh_keys[:, :kv_width], new.astype(bf16),
-            (((0,), (0,)), ((), ())), preferred_element_type=f32,
-        )
-        summed = lax.dot_general(
-            lift, mixed.astype(bf16), (((0,), (0,)), ((), ())), preferred_element_type=f32
-        )
-        out_ref[k * VDIM : (k + 1) * VDIM, :] = summed[NOPE:].astype(bf16)
-        stats += split3(peak) + split3(total) + [jnp.zeros_like(total)] * 2
-    out_ref[heads * VDIM :, :] = jnp.concatenate(stats, axis=0).astype(bf16)
+        summed = (
+            summed_ref[k * VDIM : (k + 1) * VDIM, :] * before[:, lanes]
+            + summed[NOPE:] * after[:, lanes]
+        )
+        outs[0][k * VDIM : (k + 1) * VDIM, :] = summed.astype(outs[0].dtype)
+        stats += split3(top[:, lanes]) + split3(total[:, lanes])
+        stats += [jnp.zeros_like(total[:, lanes])] * 2
+    if last:
+        outs[0][heads * VDIM :, :] = jnp.concatenate(stats, axis=0).astype(bf16)
+        outs[1][: outs[0].shape[0], :] = outs[0][...]
+        outs[1][outs[0].shape[0] :, :] = jnp.zeros_like(outs[1][outs[0].shape[0] :, :])
+    else:
+        outs[1][...] = top
+        outs[2][...] = total
 
 
 def out_kernel(span, count, width, wide, alive_ref, *refs):
@@ -268,7 +323,7 @@
     def swap(value, d):
         return lax.ppermute(value, "col", [(s, s ^ d) for s in range(count)])
 
-    def call(kernel, name, shapes, operands, scratch=(), scalars=0):
+    def call(kernel, name, shapes, operands, scratch=(), flops=1000, scalars=0):
         single = not isinstance(shapes, list)
         result = pl.pallas_call(
             kernel,
@@ -277,17 +332,22 @@
             out_specs=VMEM if single else [VMEM] * len(shapes),
             scratch_shapes=list(scratch),
             compiler_params=PARAMS,
-            cost_estimate=cost(1000, 1000),
+            cost_estimate=cost(flops, 1000),
             name=name,
         )(*operands)
         return result if single else list(result)
 
     shape = jax.ShapeDtypeStruct
     held = latent_cache[0].T
-    moved = [
-        lax.ppermute(held, "row", [(s, (s + d) % rows) for s in range(rows)])
-        for d in range(1, rows)
-    ]
+
+    def pass_on(value, d):
+        return lax.ppermute(value, "row", [(s, (s + d) % rows) for s in range(rows)])
+
+    moved = {0: held}
+    for d in range(1, rows // 2 + 1):
+        moved[d] = pass_on(moved[d - 1], 1)
+        if rows - d > d:
+            moved[rows - d] = pass_on(moved[(rows - d + 1) % rows], -1)
     query_weights = [w_q_up.T] + [swap(w_q_up.T, d) for d in range(span, count, span)]
     even, odd = call(
         functools.partial(down_kernel, count, own), "down",
@@ -309,38 +369,58 @@
         + [shape((1, group), f32), shape((rows, group), f32)]
         + [shape((1, q_width), f32), shape((1, kv_width), f32)],
         (home_slot, cache_len, new_len, page_table, q_gain[None], kv_gain[None]),
-        [pltpu.SMEM((page_table.shape[1],), jnp.int32)], 4,
+        [pltpu.SMEM((page_table.shape[1],), jnp.int32)], scalars=4,
     )
     block = call(
-        functools.partial(norm_kernel, q_width, kv_width), "norm", shape((own, wide), bf16),
+        functools.partial(norm_kernel, q_width, kv_width), "norm", shape((own, padded(wide) + 128), bf16),
         (own_cos, own_sin, q_scale, kv_scale, *partial),
     )
     blocks = [None] * count
     for d in range(0, count, 2):
         blocks[d] = swap(block, d) if d else block
-    block, moved[-1] = lax.optimization_barrier((block, moved[-1]))
-    tied = lax.optimization_barrier((*blocks[2::2], *moved[:-1]))
-    blocks[2::2], moved[:-1] = tied[: half - 1], tied[half - 1 :]
+    last = rows // 2
+    block, moved[last], moved[rows - 1] = lax.optimization_barrier((block, moved[last], moved[rows - 1]))
+    blocks[0] = block
     cache = held
     for d in range(1, rows):
-        cache = jnp.where(choice[d, :piece] > 0, moved[d - 1], cache)
+        cache = jnp.where(choice[d, :piece] > 0, moved[d], cache)
     for d in range(0, count, 2):
         blocks[d + 1] = swap(blocks[d], 1)
-    pieces = [None] * span
-    for d in range(0, span, 2):
-        pieces[d] = swap(cache, d) if d else cache
-        pieces[d + 1] = swap(pieces[d], 1)
-    state = call(
-        functools.partial(attend_kernel, span, count, own, q_width, kv_width), "attend",
-        shape((heads * (VDIM + 8), group), bf16),
-        (cosine, sine, limits, fresh_limits, w_kv_up, *query_weights, *blocks, *pieces),
+    pieces = [cache, swap(cache, 1)]
+    held_as = f32 if own % 16 else bf16
+    deep = kv_width + ROPE + EXTRA
+    lines = shape((1, heads * group), f32)
+    partial_state = [shape((heads * VDIM, group), f32), lines, lines]
+    query, *state = call(
+        functools.partial(begin_kernel, span, count, own, q_width, kv_width), "begin",
+        [shape((deep, heads * group), bf16)] + partial_state,
+        (cosine, sine, limits, fresh_limits, w_kv_up, *query_weights, *blocks, *pieces[:2]),
         [
-            pltpu.VMEM((group, q_width), f32),
-            pltpu.VMEM((span * own, kv_width + ROPE), f32),
-            pltpu.VMEM((kv_width + ROPE + EXTRA, span * piece), bf16),
+            pltpu.VMEM((group, q_width), held_as),
+            pltpu.VMEM((span * own, kv_width + ROPE), held_as),
+            pltpu.VMEM((deep, 2 * piece), bf16),
         ],
-    )
-    states = [state] + [swap(state, d) for d in range(2, count, 2)]
+        1000,
+    )
+    for d in range(2, span, 2):
+        beyond = swap(cache, d)
+        beyond, query = lax.optimization_barrier((beyond, query))
+        for turn, keys in enumerate((beyond, swap(beyond, 1))):
+            last = d + turn == span - 1
+            state = call(
+                functools.partial(further_kernel, span, count, kv_width, last), "further",
+                [shape((heads * (VDIM + 8) + rows_more, group), bf16) for rows_more in (0, 16)]
+                if last
+                else partial_state,
+                (
+                    query, *state, limits[:, (d + turn) * piece : (d + turn + 1) * piece],
+                    w_kv_up, keys,
+                ),
+                [pltpu.VMEM((deep, piece), bf16)],
+                1_000_000_000,
+            )
+    state, far = state
+    states = [state] + [swap(far if d & (d - 1) else state, d) for d in range(2, count, 2)]
     mine, other = call(
         functools.partial(out_kernel, span, count, cols, wide), "out",
         [shape((cols, group), f32), shape((cols, group), bf16)],

time: 47 us -> 40.1 us (0.85)
  waiting for transfers between devices: 15.9 us -> 9.1 us
    ppermute x3, waiting for transfers between devices: 4.77 us -> 0.01 us  [pass_on(): lax.ppermute(value, 'row', [(s, (s + d) % rows) for s in range(rows)])]
    ppermute x19, waiting for transfers between devices: 11.1 us -> 9.09 us  [swap(): return lax.ppermute(value, 'col', [(s, s ^ d) for s in range(count)])]
    ppermute x19, starting transfers between devices: 16.2 us -> 15.4 us  [swap(): return lax.ppermute(value, 'col', [(s, s ^ d) for s in range(count)])]
    ppermute x3, starting transfers between devices: 5.41 us -> 6.17 us  [pass_on(): lax.ppermute(value, 'row', [(s, (s + d) % rows) for s in range(rows)])]
    pallas_call x6 -> x8, Pallas kernels: 5.72 us -> 5.61 us  [call(): pl.pallas_call(kernel, out_shape=shapes, in_specs=[SMEM] * scalars + [VME...]
  transfers between devices with their start and end apart: 22 -> 22, of which waited for: 12 -> 11; matrix products, arithmetic and copies ran while one was open for 0% -> 0% of each run, Pallas kernels for 2% -> 10%
where the time goes in v4:
time: 40.1 us; the launch traced here: 39.9 us
  starting transfers between devices  21.6 us (54%)
  waiting for transfers between devices  9.1 us (23%)
  Pallas kernels  5.61 us (14%)
  local copies, waits for them, and re-layouts  2.73 us (7%)
  other arithmetic  0.77 us (2%)
    ppermute x19, starting transfers between devices, swap(): return lax.ppermute(value, 'col', [(s, s ^ d) for s in range(count)])  15.4 us
    ppermute x19, waiting for transfers between devices, swap(): return lax.ppermute(value, 'col', [(s, s ^ d) for s in range(count)])  9.09 us
    ppermute x3, starting transfers between devices, pass_on(): lax.ppermute(value, 'row', [(s, (s + d) % rows) for s in range(rows)])  6.17 us
    pallas_call x8, Pallas kernels, call(): pl.pallas_call(kernel, out_shape=shapes, in_specs=[SMEM] * scalars + [VME...  5.61 us
    unnamed x24, local copies, waits for them, and re-layouts  2.72 us
  transfers between devices with their start and end apart: 22, of which 11 were waited for; matrix products, arithmetic and copies ran while one was open for 0% of the time, Pallas kernels for 10%

profile of v4, /device:TPU:0, one launch (start us, length us, event | category | flops | bytes accessed | tf_op | source)
XLA Modules:
  0.0 39.9 jit_solution(17538315188453541314)
XLA Ops:
  0.0 1.1 %copy-done = bf16[320,1056]{1,0:T(8,128)(2,1)S(1)} copy-done((bf16[320,1056]{1,0:T(8,128)(2,1)S(1)}, bf16[320,1056]{1,0:T(8,128)(2,1)}, u32[]{:S(2)}) %copy-start) | copy-done | bytes 675864
  1.1 0.9 %copy-done.3 = bf16[256,320]{0,1:T(8,128)(2,1)S(1)} copy-done((bf16[256,320]{0,1:T(8,128)(2,1)S(1)}, bf16[256,320]{0,1:T(8,128)(2,1)}, u32[]{:S(2)}) %copy-start.3) | copy-done | bytes 163864
  2.0 0.6 %down.1 = (bf16[4,32,1056]{2,1,0:T(8,128)(2,1)S(1)}, bf16[4,32,1056]{2,1,0:T(8,128)(2,1)S(1)}) custom-call(bf16[320,256]{1,0:T(8,128)(2,1)S(1)} %bitcast.9, bf16[320,1056]{1,0:T(8,128)(2,1)S(1)} %copy-done), custom_call_target="tpu_custom_call" | custom-call | flops 1000 | bytes 1000 | tf_op jit(solution)/shard_map/down/pallas_call | solution.py:328
  2.6 0.5 %collective-permute-start = (bf16[4,32,1056]{2,1,0:T(8,128)(2,1)S(1)}, bf16[4,32,1056]{2,1,0:T(8,128)(2,1)S(1)}, u32[]{:S(2)}, u32[]{:S(2)}) collective-permute-start(bf16[4,32,1056]{2,1,0:T(8,128)(2,1)S(1)} %get-tuple-element.40), channel_id=1, source_target_pairs={{0,1},{1,0},{2,3},{3,2},{4,5},{5,4},{6,7},{7,6},{8,9},{9,8},{10,11... | collective-permute-start | bytes 811016 | tf_op jit(solution)/shard_map/ppermute | solution.py:324
  3.1 2.8 %collective-permute-start.4 = (bf16[288,256]{1,0:T(8,128)(2,1)S(1)}, bf16[288,256]{1,0:T(8,128)(2,1)S(1)}, u32[]{:S(2)}, u32[]{:S(2)}) collective-permute-start(bf16[288,256]{1,0:T(8,128)(2,1)S(1)} %bitcast.13), channel_id=1, source_target_pairs={{0,8},{8,16},{16,24},{24,0},{1,9},{9,17},{17,25},{25,1},{2,10},{10... | collective-permute-start | bytes 442376 | tf_op jit(solution)/shard_map/ppermute | solution.py:344
  6.1 1.6 %collective-permute-start.1 = (bf16[32,2432]{1,0:T(8,128)(2,1)S(1)}, bf16[32,2432]{1,0:T(8,128)(2,1)S(1)}, u32[]{:S(2)}, u32[]{:S(2)}) collective-permute-start(bf16[32,2432]{1,0:T(8,128)(2,1)S(1)} %get-tuple-element.45), channel_id=1, source_target_pairs={{0,2},{1,3},{2,0},{3,1},{4,6},{5,7},{6,4},{7,5},{8,10},{9,11},{10,... | collective-permute-start | bytes 466952 | tf_op jit(solution)/shard_map/ppermute | solution.py:324
  7.7 1.5 %collective-permute-start.2 = (bf16[32,2432]{1,0:T(8,128)(2,1)S(1)}, bf16[32,2432]{1,0:T(8,128)(2,1)S(1)}, u32[]{:S(2)}, u32[]{:S(2)}) collective-permute-start(bf16[32,2432]{1,0:T(8,128)(2,1)S(1)} %get-tuple-element.46), channel_id=1, source_target_pairs={{0,4},{1,5},{2,6},{3,7},{4,0},{5,1},{6,2},{7,3},{8,12},{9,13},{10,... | collective-permute-start | bytes 466952 | tf_op jit(solution)/shard_map/ppermute | solution.py:324
  9.2 0.5 %collective-permute-start.3 = (bf16[32,2432]{1,0:T(8,128)(2,1)S(1)}, bf16[32,2432]{1,0:T(8,128)(2,1)S(1)}, u32[]{:S(2)}, u32[]{:S(2)}) collective-permute-start(bf16[32,2432]{1,0:T(8,128)(2,1)S(1)} %get-tuple-element.47), channel_id=1, source_target_pairs={{0,6},{1,7},{2,4},{3,5},{4,2},{5,3},{6,0},{7,1},{8,14},{9,15},{10,... | collective-permute-start | bytes 466952 | tf_op jit(solution)/shard_map/ppermute | solution.py:324
  9.7 3.3 %collective-permute-start.6 = (bf16[288,256]{1,0:T(8,128)(2,1)S(1)}, bf16[288,256]{1,0:T(8,128)(2,1)S(1)}, u32[]{:S(2)}, u32[]{:S(2)}) collective-permute-start(bf16[288,256]{1,0:T(8,128)(2,1)S(1)} %bitcast.14), channel_id=1, source_target_pairs={{0,24},{8,0},{16,8},{24,16},{1,25},{9,1},{17,9},{25,17},{2,26},{10... | collective-permute-start | bytes 442376 | tf_op jit(solution)/shard_map/ppermute | solution.py:344
  13.1 0.6 %copy-done.5 = s32[4,32]{1,0:T(4,128)S(1)} copy-done((s32[4,32]{1,0:T(4,128)S(1)}, s32[4,32]{1,0:T(4,128)}, u32[]{:S(2)}) %copy-start.5) | copy-done | bytes 536
  13.7 0.8 %prepare.1 = (f32[32,16]{1,0:T(8,128)S(1)}, f32[32,16]{1,0:T(8,128)S(1)}, f32[16,256]{1,0:T(8,128)S(1)}, f32[16,256]{1,0:T(8,128)S(1)}, bf16[16,1024]{1,0:T(8,12...) custom-call(s32[4]{0:T(128)S(1)} %copy-done.7, ...), custom_call_target="tpu_custom_call" | custom-call | flops 1000 | bytes 1000 | tf_op jit(solution)/shard_map/prepare/pallas_call | solution.py:328
  14.6 1.6 %collective-permute-start.8 = (bf16[96,768]{1,0:T(8,128)(2,1)S(1)}, bf16[96,768]{1,0:T(8,128)(2,1)S(1)}, u32[]{:S(2)}, u32[]{:S(2)}) collective-permute-start(bf16[96,768]{1,0:T(8,128)(2,1)S(1)} %bitcast.10), channel_id=1, source_target_pairs={{0,4},{1,5},{2,6},{3,7},{4,0},{5,1},{6,2},{7,3},{8,12},{9,13},{10,... | collective-permute-start | bytes 442376 | tf_op jit(solution)/shard_map/ppermute | solution.py:324
  16.2 0.5 %collective-permute-done.2.refs_2_ = bf16[32,2432]{1,0:T(8,128)(2,1)S(1)} collective-permute-done((bf16[32,2432]{1,0:T(8,128)(2,1)S(1)}, bf16[32,2432]{1,0:T(8,128)(2,1)S(1)}, u32[]{:S(2)}, u32[]{:S(2)}) %collective-permute-start.2) | collective-permute-done | bytes 155680 | tf_op jit(solution)/shard_map/ppermute | solution.py:324
  16.9 1.2 %collective-permute-start.10 = (bf16[32,1280]{1,0:T(8,128)(2,1)S(1)}, bf16[32,1280]{1,0:T(8,128)(2,1)S(1)}, u32[]{:S(2)}, u32[]{:S(2)}) collective-permute-start(bf16[32,1280]{1,0:T(8,128)(2,1)S(1)} %norm.1.refs_2_), channel_id=1, source_target_pairs={{0,2},{1,3},{2,0},{3,1},{4,6},{5,7},{6,4},{7,5},{8,10},{9,11},{10,... | collective-permute-start | bytes 245768 | tf_op jit(solution)/shard_map/ppermute | solution.py:324
  18.1 0.8 %collective-permute-start.12 = (bf16[32,1280]{1,0:T(8,128)(2,1)S(1)}, bf16[32,1280]{1,0:T(8,128)(2,1)S(1)}, u32[]{:S(2)}, u32[]{:S(2)}) collective-permute-start(bf16[32,1280]{1,0:T(8,128)(2,1)S(1)} %norm.1.refs_2_), channel_id=1, source_target_pairs={{0,4},{1,5},{2,6},{3,7},{4,0},{5,1},{6,2},{7,3},{8,12},{9,13},{10,... | collective-permute-start | bytes 245768 | tf_op jit(solution)/shard_map/ppermute | solution.py:324
  18.9 1.5 %collective-permute-start.14 = (bf16[32,1280]{1,0:T(8,128)(2,1)S(1)}, bf16[32,1280]{1,0:T(8,128)(2,1)S(1)}, u32[]{:S(2)}, u32[]{:S(2)}) collective-permute-start(bf16[32,1280]{1,0:T(8,128)(2,1)S(1)} %norm.1.refs_2_), channel_id=1, source_target_pairs={{0,6},{1,7},{2,4},{3,5},{4,2},{5,3},{6,0},{7,1},{8,14},{9,15},{10,... | collective-permute-start | bytes 245768 | tf_op jit(solution)/shard_map/ppermute | solution.py:324
  20.5 0.6 %collective-permute-start.16 = (bf16[288,256]{1,0:T(8,128)(2,1)S(1)}, bf16[288,256]{1,0:T(8,128)(2,1)S(1)}, u32[]{:S(2)}, u32[]{:S(2)}) collective-permute-start(bf16[288,256]{1,0:T(8,128)(2,1)S(1)} %select_select_fusion.refs_10_), channel_id=1, source_target_pairs={{0,1},{1,0},{2,3},{3,2},{4,5},{5,4},{6,7},{7,6},{8,9},{9,8},{10,11... | collective-permute-start | bytes 442376 | tf_op jit(solution)/shard_map/ppermute | solution.py:324
  21.1 0.7 %collective-permute-done.9.refs_3_ = bf16[32,1280]{1,0:T(8,128)(2,1)S(1)} collective-permute-done((bf16[32,1280]{1,0:T(8,128)(2,1)S(1)}, bf16[32,1280]{1,0:T(8,128)(2,1)S(1)}, u32[]{:S(2)}, u32[]{:S(2)}) %collective-permute-start.9) | collective-permute-done | bytes 81952 | tf_op jit(solution)/shard_map/ppermute | solution.py:324
  21.7 1.3 %collective-permute-start.7 = (bf16[288,256]{1,0:T(8,128)(2,1)S(1)}, bf16[288,256]{1,0:T(8,128)(2,1)S(1)}, u32[]{:S(2)}, u32[]{:S(2)}) collective-permute-start(bf16[288,256]{1,0:T(8,128)(2,1)S(1)} %select_select_fusion.refs_10_), channel_id=1, source_target_pairs={{0,2},{1,3},{2,0},{3,1},{4,6},{5,7},{6,4},{7,5},{8,10},{9,11},{10,... | collective-permute-start | bytes 442376 | tf_op jit(solution)/shard_map/ppermute | solution.py:324
  23.6 0.7 %collective-permute-done.14.refs_8_ = bf16[32,1280]{1,0:T(8,128)(2,1)S(1)} collective-permute-done((bf16[32,1280]{1,0:T(8,128)(2,1)S(1)}, bf16[32,1280]{1,0:T(8,128)(2,1)S(1)}, u32[]{:S(2)}, u32[]{:S(2)}) %collective-permute-start.14) | collective-permute-done | bytes 81952 | tf_op jit(solution)/shard_map/ppermute | solution.py:324
  24.6 1.0 %collective-permute-done.15.refs_9_ = bf16[32,1280]{1,0:T(8,128)(2,1)S(1)} collective-permute-done((bf16[32,1280]{1,0:T(8,128)(2,1)S(1)}, bf16[32,1280]{1,0:T(8,128)(2,1)S(1)}, u32[]{:S(2)}, u32[]{:S(2)}) %collective-permute-start.15) | collective-permute-done | bytes 81952 | tf_op jit(solution)/shard_map/ppermute | solution.py:324
  25.5 2.0 %begin.1 = (bf16[304,512]{1,0:T(8,128)(2,1)S(1)}, f32[128,256]{1,0:T(8,128)S(1)}, f32[1,512]{1,0:T(1,128)S(1)}, f32[1,512]{1,0:T(1,128)S(1)}) custom-call(f32[16,256]{1,0:T(8,128)S(1)} %get-tuple-element.55.cos_ref, f32[16,256]{1,0:T(8,128)S(1)} %get-tuple-element.56.sin_ref, bf16[16,1024]{1,0:T(8,128)(2,1)S(1)} %get-tuple-element.57.limits, ...), custom_call_target="tpu_custom_call" | custom-call | flops 1000 | bytes 1000 | tf_op jit(solution)/shard_map/begin/pallas_call | solution.py:328
  27.8 0.8 %further.2 = (f32[128,256]{1,0:T(8,128)S(1)}, f32[1,512]{1,0:T(1,128)S(1)}, f32[1,512]{1,0:T(1,128)S(1)}) custom-call(bf16[304,512]{1,0:T(8,128)(2,1)S(1)} %get-tuple-element.61.query_ref, f32[128,256]{1,0:T(8,128)S(1)} %get-tuple-element.62.summed_ref, f32[1,512]{1,0:T(1,128)S(1)} %get-tuple-element.63.peak_ref, f32[1,512]{1,0:T(1,128)S(1)} %get-tuple-element.64.total_ref, ...), custom_call_target="tpu_custom_call" | custom-call | flops 1000000000 | bytes 1000 | tf_op jit(solution)/shard_map/further/pallas_call | solution.py:328
  28.6 0.4 collective-permute-done.17.piece_ref
  29.0 0.8 %further.3 = (bf16[144,256]{1,0:T(8,128)(2,1)S(1)}, bf16[160,256]{1,0:T(8,128)(2,1)S(1)}) custom-call(bf16[304,512]{1,0:T(8,128)(2,1)S(1)} %get-tuple-element.61.query_ref, f32[128,256]{1,0:T(8,128)S(1)} %get-tuple-element.66.summed_ref, f32[1,512]{1,0:T(1,128)S(1)} %get-tuple-element.67.peak_ref, f32[1,512]{1,0:T(1,128)S(1)} %get-tuple-element.68.total_ref, ...), custom_call_target="tpu_custom_call" | custom-call | flops 1000000000 | bytes 1000 | tf_op jit(solution)/shard_map/further/pallas_call | solution.py:328
  29.8 2.2 %collective-permute-start.20 = (bf16[160,256]{1,0:T(8,128)(2,1)S(1)}, bf16[160,256]{1,0:T(8,128)(2,1)S(1)}, u32[]{:S(2)}, u32[]{:S(2)}) collective-permute-start(bf16[160,256]{1,0:T(8,128)(2,1)S(1)} %get-tuple-element.70), channel_id=1, source_target_pairs={{0,6},{1,7},{2,4},{3,5},{4,2},{5,3},{6,0},{7,1},{8,14},{9,15},{10,... | collective-permute-start | bytes 245768 | tf_op jit(solution)/shard_map/ppermute | solution.py:324
  32.0 1.1 %collective-permute-start.18 = (bf16[144,256]{1,0:T(8,128)(2,1)S(1)}, bf16[144,256]{1,0:T(8,128)(2,1)S(1)}, u32[]{:S(2)}, u32[]{:S(2)}) collective-permute-start(bf16[144,256]{1,0:T(8,128)(2,1)S(1)} %get-tuple-element.69.refs_4_), channel_id=1, source_target_pairs={{0,2},{1,3},{2,0},{3,1},{4,6},{5,7},{6,4},{7,5},{8,10},{9,11},{10,... | collective-permute-start | bytes 221192 | tf_op jit(solution)/shard_map/ppermute | solution.py:324
  33.1 0.3 collective-permute-start.19
  33.4 3.7 %collective-permute-done.18.refs_5_ = bf16[144,256]{1,0:T(8,128)(2,1)S(1)} collective-permute-done((bf16[144,256]{1,0:T(8,128)(2,1)S(1)}, bf16[144,256]{1,0:T(8,128)(2,1)S(1)}, u32[]{:S(2)}, u32[]{:S(2)}) %collective-permute-start.18) | collective-permute-done | bytes 73760 | tf_op jit(solution)/shard_map/ppermute | solution.py:324
  37.4 0.4 out.1
  37.9 1.4 %collective-permute-done.21 = bf16[320,256]{1,0:T(8,128)(2,1)S(1)} collective-permute-done((bf16[320,256]{1,0:T(8,128)(2,1)S(1)}, bf16[320,256]{1,0:T(8,128)(2,1)S(1)}, u32[]{:S(2)}, u32[]{:S(2)}) %collective-permute-start.21) | collective-permute-done | bytes 163872 | tf_op jit(solution)/shard_map/ppermute | solution.py:324
  39.2 0.7 %fusion = bf16[256,320]{0,1:T(8,128)(2,1)} fusion(f32[320,256]{1,0:T(8,128)S(1)} %get-tuple-element.71, bf16[320,256]{1,0:T(8,128)(2,1)S(1)} %collective-permute-done.21), kind=kLoop, calls=%fused_computation.1 | loop fusion | flops 245760 | bytes 655360 | tf_op jit(solution)/shard_map/transpose | solution.py:433
  (49 shorter events, 1.8 us)
Async XLA Ops:
  0.0 1.1 %copy-start = (bf16[320,1056]{1,0:T(8,128)(2,1)S(1)}, bf16[320,1056]{1,0:T(8,128)(2,1)}, u32[]{:S(2)}) copy-start(bf16[320,1056]{1,0:T(8,128)(2,1)} %w_ref.1) | copy-start | bytes 2027524
  1.1 0.9 %copy-start.3 = (bf16[256,320]{0,1:T(8,128)(2,1)S(1)}, bf16[256,320]{0,1:T(8,128)(2,1)}, u32[]{:S(2)}) copy-start(bf16[256,320]{0,1:T(8,128)(2,1)} %param.12) | copy-start | bytes 491524
  2.0 1.1 %copy-start.10 = (bf16[1,256,288]{1,2,0:T(8,128)(2,1)S(1)}, bf16[1,256,288]{1,2,0:T(8,128)(2,1)}, u32[]{:S(2)}) copy-start(bf16[1,256,288]{1,2,0:T(8,128)(2,1)} %param.19) | copy-start | bytes 442372
  2.0 3.9 %copy-start.2 = (bf16[64,2560]{1,0:T(8,128)(2,1)S(1)}, bf16[64,2560]{1,0:T(8,128)(2,1)}, u32[]{:S(2)}) copy-start(bf16[64,2560]{1,0:T(8,128)(2,1)} %w_out_ref.1) | copy-start | bytes 983044
  2.6 3.3 %collective-permute-start = (bf16[4,32,1056]{2,1,0:T(8,128)(2,1)S(1)}, bf16[4,32,1056]{2,1,0:T(8,128)(2,1)S(1)}, u32[]{:S(2)}, u32[]{:S(2)}) collective-permute-start(bf16[4,32,1056]{2,1,0:T(8,128)(2,1)S(1)} %get-tuple-element.40), channel_id=1, source_target_pairs={{0,1},{1,0},{2,3},{3,2},{4,5},{5,4},{6,7},{7,6},{8,9},{9,8},{10,11... | collective-permute-start | bytes 811016 | tf_op jit(solution)/shard_map/ppermute | solution.py:324
  3.1 9.8 %collective-permute-start.4 = (bf16[288,256]{1,0:T(8,128)(2,1)S(1)}, bf16[288,256]{1,0:T(8,128)(2,1)S(1)}, u32[]{:S(2)}, u32[]{:S(2)}) collective-permute-start(bf16[288,256]{1,0:T(8,128)(2,1)S(1)} %bitcast.13), channel_id=1, source_target_pairs={{0,8},{8,16},{16,24},{24,0},{1,9},{9,17},{17,25},{25,1},{2,10},{10... | collective-permute-start | bytes 442376 | tf_op jit(solution)/shard_map/ppermute | solution.py:344
  6.0 7.1 %copy-start.8 = (s32[4]{0:T(128)S(1)}, s32[4]{0:T(128)}, u32[]{:S(2)}) copy-start(s32[4]{0:T(128)} %cached_ref.1) | copy-start | bytes 52
  6.0 7.1 %copy-start.9 = (s32[4]{0:T(128)S(1)}, s32[4]{0:T(128)}, u32[]{:S(2)}) copy-start(s32[4]{0:T(128)} %live_ref.1) | copy-start | bytes 52
  6.0 8.6 %copy-start.4 = (bf16[768,96]{0,1:T(8,128)(2,1)S(1)}, bf16[768,96]{0,1:T(8,128)(2,1)}, u32[]{:S(2)}) copy-start(bf16[768,96]{0,1:T(8,128)(2,1)} %param.16) | copy-start | bytes 442372
  6.1 6.9 %copy-start.11 = (f32[768]{0:T(1024)S(1)}, f32[768]{0:T(1024)}, u32[]{:S(2)}) copy-start(f32[768]{0:T(1024)} %param.14) | copy-start | bytes 9220
  6.1 8.5 %collective-permute-start.1 = (bf16[32,2432]{1,0:T(8,128)(2,1)S(1)}, bf16[32,2432]{1,0:T(8,128)(2,1)S(1)}, u32[]{:S(2)}, u32[]{:S(2)}) collective-permute-start(bf16[32,2432]{1,0:T(8,128)(2,1)S(1)} %get-tuple-element.45), channel_id=1, source_target_pairs={{0,2},{1,3},{2,0},{3,1},{4,6},{5,7},{6,4},{7,5},{8,10},{9,11},{10,... | collective-permute-start | bytes 466952 | tf_op jit(solution)/shard_map/ppermute | solution.py:324
  7.7 9.1 %collective-permute-start.2 = (bf16[32,2432]{1,0:T(8,128)(2,1)S(1)}, bf16[32,2432]{1,0:T(8,128)(2,1)S(1)}, u32[]{:S(2)}, u32[]{:S(2)}) collective-permute-start(bf16[32,2432]{1,0:T(8,128)(2,1)S(1)} %get-tuple-element.46), channel_id=1, source_target_pairs={{0,4},{1,5},{2,6},{3,7},{4,0},{5,1},{6,2},{7,3},{8,12},{9,13},{10,... | collective-permute-start | bytes 466952 | tf_op jit(solution)/shard_map/ppermute | solution.py:324
  9.2 7.5 %collective-permute-start.3 = (bf16[32,2432]{1,0:T(8,128)(2,1)S(1)}, bf16[32,2432]{1,0:T(8,128)(2,1)S(1)}, u32[]{:S(2)}, u32[]{:S(2)}) collective-permute-start(bf16[32,2432]{1,0:T(8,128)(2,1)S(1)} %get-tuple-element.47), channel_id=1, source_target_pairs={{0,6},{1,7},{2,4},{3,5},{4,2},{5,3},{6,0},{7,1},{8,14},{9,15},{10,... | collective-permute-start | bytes 466952 | tf_op jit(solution)/shard_map/ppermute | solution.py:324
  9.7 9.3 %collective-permute-start.6 = (bf16[288,256]{1,0:T(8,128)(2,1)S(1)}, bf16[288,256]{1,0:T(8,128)(2,1)S(1)}, u32[]{:S(2)}, u32[]{:S(2)}) collective-permute-start(bf16[288,256]{1,0:T(8,128)(2,1)S(1)} %bitcast.14), channel_id=1, source_target_pairs={{0,24},{8,0},{16,8},{24,16},{1,25},{9,1},{17,9},{25,17},{2,26},{10... | collective-permute-start | bytes 442376 | tf_op jit(solution)/shard_map/ppermute | solution.py:344
  13.0 7.4 %collective-permute-start.5 = (bf16[288,256]{1,0:T(8,128)(2,1)S(1)}, bf16[288,256]{1,0:T(8,128)(2,1)S(1)}, u32[]{:S(2)}, u32[]{:S(2)}) collective-permute-start(bf16[288,256]{1,0:T(8,128)(2,1)S(1)} %collective-permute-done.4), channel_id=1, source_target_pairs={{0,8},{8,16},{16,24},{24,0},{1,9},{9,17},{17,25},{25,1},{2,10},{10... | collective-permute-start | bytes 442376 | tf_op jit(solution)/shard_map/ppermute | solution.py:344
  13.0 0.7 %copy-start.6 = (f32[256]{0:T(256)S(1)}, f32[256]{0:T(256)}, u32[]{:S(2)}) copy-start(f32[256]{0:T(256)} %param.15) | copy-start | bytes 3076
  14.6 5.9 %collective-permute-start.8 = (bf16[96,768]{1,0:T(8,128)(2,1)S(1)}, bf16[96,768]{1,0:T(8,128)(2,1)S(1)}, u32[]{:S(2)}, u32[]{:S(2)}) collective-permute-start(bf16[96,768]{1,0:T(8,128)(2,1)S(1)} %bitcast.10), channel_id=1, source_target_pairs={{0,4},{1,5},{2,6},{3,7},{4,0},{5,1},{6,2},{7,3},{8,12},{9,13},{10,... | collective-permute-start | bytes 442376 | tf_op jit(solution)/shard_map/ppermute | solution.py:324
  16.9 8.7 %copy-start.1 = (bf16[256,1024]{1,0:T(8,128)(2,1)S(1)}, bf16[256,1024]{1,0:T(8,128)(2,1)}, u32[]{:S(2)}) copy-start(bf16[256,1024]{1,0:T(8,128)(2,1)} %w_kv_ref.5) | copy-start | bytes 1572868
  16.9 6.2 %collective-permute-start.10 = (bf16[32,1280]{1,0:T(8,128)(2,1)S(1)}, bf16[32,1280]{1,0:T(8,128)(2,1)S(1)}, u32[]{:S(2)}, u32[]{:S(2)}) collective-permute-start(bf16[32,1280]{1,0:T(8,128)(2,1)S(1)} %norm.1.refs_2_), channel_id=1, source_target_pairs={{0,2},{1,3},{2,0},{3,1},{4,6},{5,7},{6,4},{7,5},{8,10},{9,11},{10,... | collective-permute-start | bytes 245768 | tf_op jit(solution)/shard_map/ppermute | solution.py:324
  18.1 5.2 %collective-permute-start.12 = (bf16[32,1280]{1,0:T(8,128)(2,1)S(1)}, bf16[32,1280]{1,0:T(8,128)(2,1)S(1)}, u32[]{:S(2)}, u32[]{:S(2)}) collective-permute-start(bf16[32,1280]{1,0:T(8,128)(2,1)S(1)} %norm.1.refs_2_), channel_id=1, source_target_pairs={{0,4},{1,5},{2,6},{3,7},{4,0},{5,1},{6,2},{7,3},{8,12},{9,13},{10,... | collective-permute-start | bytes 245768 | tf_op jit(solution)/shard_map/ppermute | solution.py:324
  18.9 5.3 %collective-permute-start.14 = (bf16[32,1280]{1,0:T(8,128)(2,1)S(1)}, bf16[32,1280]{1,0:T(8,128)(2,1)S(1)}, u32[]{:S(2)}, u32[]{:S(2)}) collective-permute-start(bf16[32,1280]{1,0:T(8,128)(2,1)S(1)} %norm.1.refs_2_), channel_id=1, source_target_pairs={{0,6},{1,7},{2,4},{3,5},{4,2},{5,3},{6,0},{7,1},{8,14},{9,15},{10,... | collective-permute-start | bytes 245768 | tf_op jit(solution)/shard_map/ppermute | solution.py:324
  20.4 1.3 %collective-permute-start.9 = (bf16[32,1280]{1,0:T(8,128)(2,1)S(1)}, bf16[32,1280]{1,0:T(8,128)(2,1)S(1)}, u32[]{:S(2)}, u32[]{:S(2)}) collective-permute-start(bf16[32,1280]{1,0:T(8,128)(2,1)S(1)} %norm.1.refs_2_), channel_id=1, source_target_pairs={{0,1},{1,0},{2,3},{3,2},{4,5},{5,4},{6,7},{7,6},{8,9},{9,8},{10,11... | collective-permute-start | bytes 245768 | tf_op jit(solution)/shard_map/ppermute | solution.py:324
  20.5 3.8 %collective-permute-start.16 = (bf16[288,256]{1,0:T(8,128)(2,1)S(1)}, bf16[288,256]{1,0:T(8,128)(2,1)S(1)}, u32[]{:S(2)}, u32[]{:S(2)}) collective-permute-start(bf16[288,256]{1,0:T(8,128)(2,1)S(1)} %select_select_fusion.refs_10_), channel_id=1, source_target_pairs={{0,1},{1,0},{2,3},{3,2},{4,5},{5,4},{6,7},{7,6},{8,9},{9,8},{10,11... | collective-permute-start | bytes 442376 | tf_op jit(solution)/shard_map/ppermute | solution.py:324
  21.7 5.9 %collective-permute-start.7 = (bf16[288,256]{1,0:T(8,128)(2,1)S(1)}, bf16[288,256]{1,0:T(8,128)(2,1)S(1)}, u32[]{:S(2)}, u32[]{:S(2)}) collective-permute-start(bf16[288,256]{1,0:T(8,128)(2,1)S(1)} %select_select_fusion.refs_10_), channel_id=1, source_target_pairs={{0,2},{1,3},{2,0},{3,1},{4,6},{5,7},{6,4},{7,5},{8,10},{9,11},{10,... | collective-permute-start | bytes 442376 | tf_op jit(solution)/shard_map/ppermute | solution.py:324
  23.0 1.3 %collective-permute-start.11 = (bf16[32,1280]{1,0:T(8,128)(2,1)S(1)}, bf16[32,1280]{1,0:T(8,128)(2,1)S(1)}, u32[]{:S(2)}, u32[]{:S(2)}) collective-permute-start(bf16[32,1280]{1,0:T(8,128)(2,1)S(1)} %collective-permute-done.10.refs_4_), channel_id=1, source_target_pairs={{0,1},{1,0},{2,3},{3,2},{4,5},{5,4},{6,7},{7,6},{8,9},{9,8},{10,11... | collective-permute-start | bytes 245768 | tf_op jit(solution)/shard_map/ppermute | solution.py:324
  23.3 1.3 %collective-permute-start.13 = (bf16[32,1280]{1,0:T(8,128)(2,1)S(1)}, bf16[32,1280]{1,0:T(8,128)(2,1)S(1)}, u32[]{:S(2)}, u32[]{:S(2)}) collective-permute-start(bf16[32,1280]{1,0:T(8,128)(2,1)S(1)} %collective-permute-done.12.refs_6_), channel_id=1, source_target_pairs={{0,1},{1,0},{2,3},{3,2},{4,5},{5,4},{6,7},{7,6},{8,9},{9,8},{10,11... | collective-permute-start | bytes 245768 | tf_op jit(solution)/shard_map/ppermute | solution.py:324
  24.2 1.3 %collective-permute-start.15 = (bf16[32,1280]{1,0:T(8,128)(2,1)S(1)}, bf16[32,1280]{1,0:T(8,128)(2,1)S(1)}, u32[]{:S(2)}, u32[]{:S(2)}) collective-permute-start(bf16[32,1280]{1,0:T(8,128)(2,1)S(1)} %collective-permute-done.14.refs_8_), channel_id=1, source_target_pairs={{0,1},{1,0},{2,3},{3,2},{4,5},{5,4},{6,7},{7,6},{8,9},{9,8},{10,11... | collective-permute-start | bytes 245768 | tf_op jit(solution)/shard_map/ppermute | solution.py:324
  27.6 1.4 %collective-permute-start.17 = (bf16[288,256]{1,0:T(8,128)(2,1)S(1)}, bf16[288,256]{1,0:T(8,128)(2,1)S(1)}, u32[]{:S(2)}, u32[]{:S(2)}) collective-permute-start(bf16[288,256]{1,0:T(8,128)(2,1)S(1)} %collective-permute-done.7.piece_ref), channel_id=1, source_target_pairs={{0,1},{1,0},{2,3},{3,2},{4,5},{5,4},{6,7},{7,6},{8,9},{9,8},{10,11... | collective-permute-start | bytes 442376 | tf_op jit(solution)/shard_map/ppermute | solution.py:324
  29.8 7.6 %collective-permute-start.20 = (bf16[160,256]{1,0:T(8,128)(2,1)S(1)}, bf16[160,256]{1,0:T(8,128)(2,1)S(1)}, u32[]{:S(2)}, u32[]{:S(2)}) collective-permute-start(bf16[160,256]{1,0:T(8,128)(2,1)S(1)} %get-tuple-element.70), channel_id=1, source_target_pairs={{0,6},{1,7},{2,4},{3,5},{4,2},{5,3},{6,0},{7,1},{8,14},{9,15},{10,... | collective-permute-start | bytes 245768 | tf_op jit(solution)/shard_map/ppermute | solution.py:324
  32.0 5.1 %collective-permute-start.18 = (bf16[144,256]{1,0:T(8,128)(2,1)S(1)}, bf16[144,256]{1,0:T(8,128)(2,1)S(1)}, u32[]{:S(2)}, u32[]{:S(2)}) collective-permute-start(bf16[144,256]{1,0:T(8,128)(2,1)S(1)} %get-tuple-element.69.refs_4_), channel_id=1, source_target_pairs={{0,2},{1,3},{2,0},{3,1},{4,6},{5,7},{6,4},{7,5},{8,10},{9,11},{10,... | collective-permute-start | bytes 221192 | tf_op jit(solution)/shard_map/ppermute | solution.py:324
  33.1 4.4 %collective-permute-start.19 = (bf16[144,256]{1,0:T(8,128)(2,1)S(1)}, bf16[144,256]{1,0:T(8,128)(2,1)S(1)}, u32[]{:S(2)}, u32[]{:S(2)}) collective-permute-start(bf16[144,256]{1,0:T(8,128)(2,1)S(1)} %get-tuple-element.69.refs_4_), channel_id=1, source_target_pairs={{0,4},{1,5},{2,6},{3,7},{4,0},{5,1},{6,2},{7,3},{8,12},{9,13},{10,... | collective-permute-start | bytes 221192 | tf_op jit(solution)/shard_map/ppermute | solution.py:324
  37.8 1.5 %collective-permute-start.21 = (bf16[320,256]{1,0:T(8,128)(2,1)S(1)}, bf16[320,256]{1,0:T(8,128)(2,1)S(1)}, u32[]{:S(2)}, u32[]{:S(2)}) collective-permute-start(bf16[320,256]{1,0:T(8,128)(2,1)S(1)} %get-tuple-element.72), channel_id=1, source_target_pairs={{0,1},{1,0},{2,3},{3,2},{4,5},{5,4},{6,7},{7,6},{8,9},{9,8},{10,11... | collective-permute-start | bytes 491528 | tf_op jit(solution)/shard_map/ppermute | solution.py:324
  (2 other events, 1.4 us)

commit v5 on v4

--- a/solution.py
+++ b/solution.py
@@ -15,6 +15,7 @@
 SPAN = 4
 EXTRA = 16
 epsilon = 1e-05
+SCALE = math.log2(math.e) / math.sqrt(NOPE + ROPE)
 MASKED = -1e30
 FLOOR = -1e29
 
@@ -27,6 +28,15 @@
 
 def cost(flops, moved, special=0):
     return pl.CostEstimate(flops=flops, bytes_accessed=moved, transcendentals=special)
+
+
+def near_offsets(span, count):
+    high = count // (span // 2)
+    return [i // 2 * high + i % 2 for i in range(span)]
+
+
+def across_offsets(span, count):
+    return [2 * k for k in range(count // span)]
 
 
 def padded(lanes):
@@ -60,6 +70,7 @@
     q_gain[...] = q_gain_ref[...]
     kv_gain[...] = kv_gain_ref[...]
     column = lax.axis_index("col")
+    near = near_offsets(span, count)
     row = lax.axis_index("row")
     slot = home_ref[row]
     live = live_ref[row]
@@ -87,13 +98,13 @@
     line = lax.broadcasted_iota(jnp.int32, (EXTRA, page), 0)
     for j in range(span):
         for p in range(per_piece):
-            seen = offset < cached - logical[(column ^ j) * per_piece + p] * page
+            seen = offset < cached - logical[(column ^ near[j]) * per_piece + p] * page
             start = (j * per_piece + p) * page
             limits[:, start : start + page] = jnp.where(seen | (line > 0), 0.0, MASKED).astype(bf16)
     query_id = lax.broadcasted_iota(jnp.int32, (own, group), 1)
     offset = lax.broadcasted_iota(jnp.int32, (own, group), 0)
     for j in range(span):
-        fresh_id = (column ^ j) * own + offset
+        fresh_id = (column ^ near[j]) * own + offset
         seen = (fresh_id <= query_id) & (fresh_id < live)
         fresh_limits[j * own : (j + 1) * own, :] = jnp.where(seen, 0.0, MASKED)
     token = lax.broadcasted_iota(jnp.int32, (1, group), 1)
@@ -150,7 +161,6 @@
 
 
 def weigh(query, keys, fresh, fresh_bias, kv_width):
-    scale = 1.0 / math.sqrt(NOPE + ROPE)
     scores = [
         lax.dot_general(keys, query, (((0,), (0,)), ((), ())), preferred_element_type=f32)
     ]
@@ -159,7 +169,7 @@
         scores.append(new + jnp.concatenate([fresh_bias] * (new.shape[1] // fresh_bias.shape[1]), 1))
     peak = functools.reduce(jnp.maximum, [jnp.max(s, 0, keepdims=True) for s in scores])
     peak = jnp.maximum(peak, FLOOR)
-    weights = [jnp.exp((s - peak) * scale) for s in scores]
+    weights = [jnp.exp2(s - peak) for s in scores]
     total = sum(jnp.sum(w, 0, keepdims=True) for w in weights)
     mixed = jnp.dot(keys[:kv_width], weights[0].astype(bf16), preferred_element_type=f32)
     if fresh is not None:
@@ -167,11 +177,11 @@
             fresh[:, :kv_width], weights[1].astype(bf16),
             (((0,), (0,)), ((), ())), preferred_element_type=f32,
         )
-    return peak, total, mixed.astype(bf16)
-
-
-def lifted(w_kv_ref, column, k, span):
-    head = column ^ (k * span)
+    return peak, total, mixed
+
+
+def lifted(w_kv_ref, column, k, count, span):
+    head = column ^ across_offsets(span, count)[k]
     return w_kv_ref[:, pl.ds(pl.multiple_of(head * HEAD, HEAD), HEAD)]
 
 
@@ -181,7 +191,7 @@
     heads = count // span
     weights, refs = refs[:heads], refs[heads:]
     blocks, refs = refs[:count], refs[count:]
-    pieces, (query_ref, summed_ref, peak_ref, total_ref, query_rows, fresh, keys) = refs[:2], refs[2:]
+    pieces, (query_ref, mixed_ref, peak_ref, total_ref, query_rows, fresh, keys) = refs[:2], refs[2:]
     column = lax.axis_index("col")
     group = count * own
     piece = pieces[0].shape[1]
@@ -189,8 +199,9 @@
     for j in range(count):
         start = pl.multiple_of((column ^ j) * own, own)
         query_rows[pl.ds(start, own), :] = blocks[j][:, :q_width].astype(query_rows.dtype)
-        if j < span:
-            fresh[j * own : (j + 1) * own, :] = blocks[j][:, q_width : q_width + wide].astype(fresh.dtype)
+    for j, offset in enumerate(near_offsets(span, count)):
+        latents = blocks[offset][:, q_width : q_width + wide]
+        fresh[j * own : (j + 1) * own, :] = latents.astype(fresh.dtype)
     for j in range(2):
         keys[:wide, j * piece : (j + 1) * piece] = pieces[j][...]
     keys[wide:, :] = limits[:, : 2 * piece]
@@ -203,64 +214,57 @@
         )
         turned = rotate(projected[NOPE:], cos_ref[...], sin_ref[...], 0)
         plain = jnp.dot(
-            lifted(w_kv_ref, column, k, span)[:, :NOPE],
+            lifted(w_kv_ref, column, k, count, span)[:, :NOPE],
             projected[:NOPE].astype(bf16), preferred_element_type=f32,
         )
         lanes = slice(k * group, (k + 1) * group)
-        query_ref[:kv_width, lanes] = plain.astype(bf16)
-        query_ref[kv_width:wide, lanes] = turned.astype(bf16)
+        query_ref[:kv_width, lanes] = (plain * SCALE).astype(bf16)
+        query_ref[kv_width:wide, lanes] = (turned * SCALE).astype(bf16)
         query_ref[wide:, lanes] = first_row
     peak, total, mixed = weigh(
         query_ref[...], keys[...], fresh[...].astype(bf16), fresh_limits[...], kv_width
     )
     peak_ref[...] = peak
     total_ref[...] = total
-    for k in range(heads):
-        summed = lax.dot_general(
-            lifted(w_kv_ref, column, k, span), mixed[:, k * group : (k + 1) * group],
-            (((0,), (0,)), ((), ())), preferred_element_type=f32,
-        )
-        summed_ref[k * VDIM : (k + 1) * VDIM, :] = summed[NOPE:]
+    mixed_ref[...] = mixed
 
 
 def further_kernel(
-    span, count, kv_width, last, query_ref, summed_ref, peak_ref, total_ref, limits, w_kv_ref,
+    span, count, kv_width, last, query_ref, mixed_ref, peak_ref, total_ref, limits, w_kv_ref,
     piece_ref, *refs,
 ):
     outs, keys = refs[:-1], refs[-1]
     heads = count // span
     column = lax.axis_index("col")
-    group = summed_ref.shape[1]
+    group = mixed_ref.shape[1] // heads
     wide = kv_width + ROPE
     keys[:wide, :] = piece_ref[...]
     keys[wide:, :] = limits[...]
     peak, total, mixed = weigh(query_ref[...], keys[...], None, None, kv_width)
-    scale = 1.0 / math.sqrt(NOPE + ROPE)
     top = jnp.maximum(peak, peak_ref[...])
-    before = jnp.exp((peak_ref[...] - top) * scale)
-    after = jnp.exp((peak - top) * scale)
+    before = jnp.exp2(peak_ref[...] - top)
+    after = jnp.exp2(peak - top)
     total = total_ref[...] * before + total * after
+    mixed = mixed_ref[...] * before + mixed * after
+    if not last:
+        outs[0][...] = mixed
+        outs[1][...] = top
+        outs[2][...] = total
+        return
+    mixed = mixed.astype(bf16)
     stats = []
     for k in range(heads):
         lanes = slice(k * group, (k + 1) * group)
         summed = lax.dot_general(
-            lifted(w_kv_ref, column, k, span), mixed[:, lanes],
+            lifted(w_kv_ref, column, k, count, span), mixed[:, lanes],
             (((0,), (0,)), ((), ())), preferred_element_type=f32,
         )
-        summed = (
-            summed_ref[k * VDIM : (k + 1) * VDIM, :] * before[:, lanes]
-            + summed[NOPE:] * after[:, lanes]
-        )
-        outs[0][k * VDIM : (k + 1) * VDIM, :] = summed.astype(outs[0].dtype)
+        outs[0][k * VDIM : (k + 1) * VDIM, :] = summed[NOPE:].astype(bf16)
         stats += split3(top[:, lanes]) + split3(total[:, lanes])
         stats += [jnp.zeros_like(total[:, lanes])] * 2
-    if last:
-        outs[0][heads * VDIM :, :] = jnp.concatenate(stats, axis=0).astype(bf16)
-        outs[1][: outs[0].shape[0], :] = outs[0][...]
-        outs[1][outs[0].shape[0] :, :] = jnp.zeros_like(outs[1][outs[0].shape[0] :, :])
-    else:
-        outs[1][...] = top
-        outs[2][...] = total
+    outs[0][heads * VDIM :, :] = jnp.concatenate(stats, axis=0).astype(bf16)
+    outs[1][: outs[0].shape[0], :] = outs[0][...]
+    outs[1][outs[0].shape[0] :, :] = jnp.zeros_like(outs[1][outs[0].shape[0] :, :])
 
 
 def out_kernel(span, count, width, wide, alive_ref, *refs):
@@ -268,16 +272,17 @@
     heads = count // span
     columns, refs = refs[:half], refs[half:]
     states, (mine_ref, other_ref, attended, weights) = refs[:half], refs[half:]
-    scale = 1.0 / math.sqrt(NOPE + ROPE)
     for i in range(half):
         own = columns[i].shape[0]
         for p in range(VDIM // own):
             lane = padded(wide) + p * padded(2 * width)
             row = i * VDIM + p * own
-            weights[row : row + own, :] = columns[i][:, lane : lane + 2 * width].astype(f32)
+            weights[row : row + own, :] = columns[i][:, lane : lane + 2 * width].astype(
+                weights.dtype
+            )
         parts = []
         for k in range(heads):
-            ref = states[i ^ (k * span // 2)]
+            ref = states[i ^ (across_offsets(span, count)[k] // 2)]
             lanes = ref[heads * VDIM :, :].astype(f32)[8 * k : 8 * k + 6]
             parts.append(
                 (
@@ -290,7 +295,7 @@
         total = 0.0
         summed = 0.0
         for part in parts:
-            factor = jnp.exp((part[1] - peak) * scale)
+            factor = jnp.exp2(part[1] - peak)
             total += part[2] * factor
             summed += part[0] * factor
         factor = jnp.where(alive_ref[...] > 0, 1.0 / total, 0.0)
@@ -348,7 +353,7 @@
         moved[d] = pass_on(moved[d - 1], 1)
         if rows - d > d:
             moved[rows - d] = pass_on(moved[(rows - d + 1) % rows], -1)
-    query_weights = [w_q_up.T] + [swap(w_q_up.T, d) for d in range(span, count, span)]
+    query_weights = [w_q_up.T] + [swap(w_q_up.T, d) for d in across_offsets(span, count)[1:]]
     even, odd = call(
         functools.partial(down_kernel, count, own), "down",
         [shape((half, own, wide), bf16)] * 2, (tokens.T, w_down),
@@ -366,7 +371,7 @@
         [shape((own, ROPE // 2), f32)] * 2
         + [shape((ROPE // 2, group), f32)] * 2
         + [shape((EXTRA, span * piece), bf16), shape((span * own, group), f32)]
-        + [shape((1, group), f32), shape((rows, group), f32)]
+        + [shape((1, group), f32), shape((rows, piece), f32)]
         + [shape((1, q_width), f32), shape((1, kv_width), f32)],
         (home_slot, cache_len, new_len, page_table, q_gain[None], kv_gain[None]),
         [pltpu.SMEM((page_table.shape[1],), jnp.int32)], scalars=4,
@@ -383,14 +388,14 @@
     blocks[0] = block
     cache = held
     for d in range(1, rows):
-        cache = jnp.where(choice[d, :piece] > 0, moved[d], cache)
+        cache = jnp.where(choice[d] > 0, moved[d], cache)
     for d in range(0, count, 2):
         blocks[d + 1] = swap(blocks[d], 1)
     pieces = [cache, swap(cache, 1)]
     held_as = f32 if own % 16 else bf16
     deep = kv_width + ROPE + EXTRA
     lines = shape((1, heads * group), f32)
-    partial_state = [shape((heads * VDIM, group), f32), lines, lines]
+    partial_state = [shape((kv_width, heads * group), f32), lines, lines]
     query, *state = call(
         functools.partial(begin_kernel, span, count, own, q_width, kv_width), "begin",
         [shape((deep, heads * group), bf16)] + partial_state,
@@ -402,8 +407,9 @@
         ],
         1000,
     )
+    near = near_offsets(span, count)
     for d in range(2, span, 2):
-        beyond = swap(cache, d)
+        beyond = swap(cache, near[d])
         beyond, query = lax.optimization_barrier((beyond, query))
         for turn, keys in enumerate((beyond, swap(beyond, 1))):
             last = d + turn == span - 1
@@ -427,7 +433,7 @@
         (alive, *partial, *states),
         [
             pltpu.VMEM((half * VDIM, group), bf16),
-            pltpu.VMEM((half * VDIM, 2 * cols), f32),
+            pltpu.VMEM((half * VDIM, 2 * cols), held_as),
         ],
     )
     return (mine + swap(other, 1).astype(f32)).astype(bf16).T

time: 40.1 us -> 39.8 us (level)
  transfers between devices with their start and end apart: 22 -> 22, of which waited for: 11 -> 12; matrix products, arithmetic and copies ran while one was open for 0% -> 0% of each run, Pallas kernels for 10% -> 9%
where the time goes in v5:
time: 39.8 us; the launch traced here: 39.6 us
  starting transfers between devices  21.4 us (54%)
  waiting for transfers between devices  9.36 us (24%)
  Pallas kernels  5.21 us (13%)
  local copies, waits for them, and re-layouts  2.73 us (7%)
  other arithmetic  0.78 us (2%)
    ppermute x19, starting transfers between devices, swap(): return lax.ppermute(value, 'col', [(s, s ^ d) for s in range(count)])  15.2 us
    ppermute x19, waiting for transfers between devices, swap(): return lax.ppermute(value, 'col', [(s, s ^ d) for s in range(count)])  9.35 us
    ppermute x3, starting transfers between devices, pass_on(): lax.ppermute(value, 'row', [(s, (s + d) % rows) for s in range(rows)])  6.17 us
    pallas_call x8, Pallas kernels, call(): pl.pallas_call(kernel, out_shape=shapes, in_specs=[SMEM] * scalars + [VME...  5.21 us
    unnamed x24, local copies, waits for them, and re-layouts  2.72 us
  transfers between devices with their start and end apart: 22, of which 12 were waited for; matrix products, arithmetic and copies ran while one was open for 0% of the time, Pallas kernels for 9%

profile of v5, /device:TPU:0, one launch (start us, length us, event | category | flops | bytes accessed | tf_op | source)
XLA Modules:
  0.0 39.6 jit_solution(9035225632215529419)
XLA Ops:
  0.0 1.1 %copy-done = bf16[320,1056]{1,0:T(8,128)(2,1)S(1)} copy-done((bf16[320,1056]{1,0:T(8,128)(2,1)S(1)}, bf16[320,1056]{1,0:T(8,128)(2,1)}, u32[]{:S(2)}) %copy-start) | copy-done | bytes 675864
  1.1 0.9 %copy-done.3 = bf16[256,320]{0,1:T(8,128)(2,1)S(1)} copy-done((bf16[256,320]{0,1:T(8,128)(2,1)S(1)}, bf16[256,320]{0,1:T(8,128)(2,1)}, u32[]{:S(2)}) %copy-start.3) | copy-done | bytes 163864
  2.0 0.6 %down.1 = (bf16[4,32,1056]{2,1,0:T(8,128)(2,1)S(1)}, bf16[4,32,1056]{2,1,0:T(8,128)(2,1)S(1)}) custom-call(bf16[320,256]{1,0:T(8,128)(2,1)S(1)} %bitcast.9, bf16[320,1056]{1,0:T(8,128)(2,1)S(1)} %copy-done), custom_call_target="tpu_custom_call" | custom-call | flops 1000 | bytes 1000 | tf_op jit(solution)/shard_map/down/pallas_call | solution.py:333
  2.6 0.5 %collective-permute-start = (bf16[4,32,1056]{2,1,0:T(8,128)(2,1)S(1)}, bf16[4,32,1056]{2,1,0:T(8,128)(2,1)S(1)}, u32[]{:S(2)}, u32[]{:S(2)}) collective-permute-start(bf16[4,32,1056]{2,1,0:T(8,128)(2,1)S(1)} %get-tuple-element.40), channel_id=1, source_target_pairs={{0,1},{1,0},{2,3},{3,2},{4,5},{5,4},{6,7},{7,6},{8,9},{9,8},{10,11... | collective-permute-start | bytes 811016 | tf_op jit(solution)/shard_map/ppermute | solution.py:329
  3.1 2.8 %collective-permute-start.4 = (bf16[288,256]{1,0:T(8,128)(2,1)S(1)}, bf16[288,256]{1,0:T(8,128)(2,1)S(1)}, u32[]{:S(2)}, u32[]{:S(2)}) collective-permute-start(bf16[288,256]{1,0:T(8,128)(2,1)S(1)} %bitcast.13), channel_id=1, source_target_pairs={{0,8},{8,16},{16,24},{24,0},{1,9},{9,17},{17,25},{25,1},{2,10},{10... | collective-permute-start | bytes 442376 | tf_op jit(solution)/shard_map/ppermute | solution.py:349
  6.1 1.6 %collective-permute-start.1 = (bf16[32,2432]{1,0:T(8,128)(2,1)S(1)}, bf16[32,2432]{1,0:T(8,128)(2,1)S(1)}, u32[]{:S(2)}, u32[]{:S(2)}) collective-permute-start(bf16[32,2432]{1,0:T(8,128)(2,1)S(1)} %get-tuple-element.45), channel_id=1, source_target_pairs={{0,2},{1,3},{2,0},{3,1},{4,6},{5,7},{6,4},{7,5},{8,10},{9,11},{10,... | collective-permute-start | bytes 466952 | tf_op jit(solution)/shard_map/ppermute | solution.py:329
  7.7 1.5 %collective-permute-start.2 = (bf16[32,2432]{1,0:T(8,128)(2,1)S(1)}, bf16[32,2432]{1,0:T(8,128)(2,1)S(1)}, u32[]{:S(2)}, u32[]{:S(2)}) collective-permute-start(bf16[32,2432]{1,0:T(8,128)(2,1)S(1)} %get-tuple-element.46), channel_id=1, source_target_pairs={{0,4},{1,5},{2,6},{3,7},{4,0},{5,1},{6,2},{7,3},{8,12},{9,13},{10,... | collective-permute-start | bytes 466952 | tf_op jit(solution)/shard_map/ppermute | solution.py:329
  9.2 0.5 %collective-permute-start.3 = (bf16[32,2432]{1,0:T(8,128)(2,1)S(1)}, bf16[32,2432]{1,0:T(8,128)(2,1)S(1)}, u32[]{:S(2)}, u32[]{:S(2)}) collective-permute-start(bf16[32,2432]{1,0:T(8,128)(2,1)S(1)} %get-tuple-element.47), channel_id=1, source_target_pairs={{0,6},{1,7},{2,4},{3,5},{4,2},{5,3},{6,0},{7,1},{8,14},{9,15},{10,... | collective-permute-start | bytes 466952 | tf_op jit(solution)/shard_map/ppermute | solution.py:329
  9.7 3.3 %collective-permute-start.6 = (bf16[288,256]{1,0:T(8,128)(2,1)S(1)}, bf16[288,256]{1,0:T(8,128)(2,1)S(1)}, u32[]{:S(2)}, u32[]{:S(2)}) collective-permute-start(bf16[288,256]{1,0:T(8,128)(2,1)S(1)} %bitcast.14), channel_id=1, source_target_pairs={{0,24},{8,0},{16,8},{24,16},{1,25},{9,1},{17,9},{25,17},{2,26},{10... | collective-permute-start | bytes 442376 | tf_op jit(solution)/shard_map/ppermute | solution.py:349
  13.1 0.6 %copy-done.5 = s32[4,32]{1,0:T(4,128)S(1)} copy-done((s32[4,32]{1,0:T(4,128)S(1)}, s32[4,32]{1,0:T(4,128)}, u32[]{:S(2)}) %copy-start.5) | copy-done | bytes 536
  13.7 0.8 %prepare.1 = (f32[32,16]{1,0:T(8,128)S(1)}, f32[32,16]{1,0:T(8,128)S(1)}, f32[16,256]{1,0:T(8,128)S(1)}, f32[16,256]{1,0:T(8,128)S(1)}, bf16[16,1024]{1,0:T(8,12...) custom-call(s32[4]{0:T(128)S(1)} %copy-done.7, ...), custom_call_target="tpu_custom_call" | custom-call | flops 1000 | bytes 1000 | tf_op jit(solution)/shard_map/prepare/pallas_call | solution.py:333
  14.6 1.6 %collective-permute-start.8 = (bf16[96,768]{1,0:T(8,128)(2,1)S(1)}, bf16[96,768]{1,0:T(8,128)(2,1)S(1)}, u32[]{:S(2)}, u32[]{:S(2)}) collective-permute-start(bf16[96,768]{1,0:T(8,128)(2,1)S(1)} %bitcast.10), channel_id=1, source_target_pairs={{0,2},{1,3},{2,0},{3,1},{4,6},{5,7},{6,4},{7,5},{8,10},{9,11},{10,... | collective-permute-start | bytes 442376 | tf_op jit(solution)/shard_map/ppermute | solution.py:329
  16.1 0.5 %collective-permute-done.2.refs_2_ = bf16[32,2432]{1,0:T(8,128)(2,1)S(1)} collective-permute-done((bf16[32,2432]{1,0:T(8,128)(2,1)S(1)}, bf16[32,2432]{1,0:T(8,128)(2,1)S(1)}, u32[]{:S(2)}, u32[]{:S(2)}) %collective-permute-start.2) | collective-permute-done | bytes 155680 | tf_op jit(solution)/shard_map/ppermute | solution.py:329
  16.8 1.3 %collective-permute-start.10 = (bf16[32,1280]{1,0:T(8,128)(2,1)S(1)}, bf16[32,1280]{1,0:T(8,128)(2,1)S(1)}, u32[]{:S(2)}, u32[]{:S(2)}) collective-permute-start(bf16[32,1280]{1,0:T(8,128)(2,1)S(1)} %norm.1.refs_2_), channel_id=1, source_target_pairs={{0,2},{1,3},{2,0},{3,1},{4,6},{5,7},{6,4},{7,5},{8,10},{9,11},{10,... | collective-permute-start | bytes 245768 | tf_op jit(solution)/shard_map/ppermute | solution.py:329
  18.1 0.8 %collective-permute-start.12 = (bf16[32,1280]{1,0:T(8,128)(2,1)S(1)}, bf16[32,1280]{1,0:T(8,128)(2,1)S(1)}, u32[]{:S(2)}, u32[]{:S(2)}) collective-permute-start(bf16[32,1280]{1,0:T(8,128)(2,1)S(1)} %norm.1.refs_2_), channel_id=1, source_target_pairs={{0,4},{1,5},{2,6},{3,7},{4,0},{5,1},{6,2},{7,3},{8,12},{9,13},{10,... | collective-permute-start | bytes 245768 | tf_op jit(solution)/shard_map/ppermute | solution.py:329
  18.9 1.4 %collective-permute-start.14 = (bf16[32,1280]{1,0:T(8,128)(2,1)S(1)}, bf16[32,1280]{1,0:T(8,128)(2,1)S(1)}, u32[]{:S(2)}, u32[]{:S(2)}) collective-permute-start(bf16[32,1280]{1,0:T(8,128)(2,1)S(1)} %norm.1.refs_2_), channel_id=1, source_target_pairs={{0,6},{1,7},{2,4},{3,5},{4,2},{5,3},{6,0},{7,1},{8,14},{9,15},{10,... | collective-permute-start | bytes 245768 | tf_op jit(solution)/shard_map/ppermute | solution.py:329
  21.0 0.7 %collective-permute-done.9.refs_3_ = bf16[32,1280]{1,0:T(8,128)(2,1)S(1)} collective-permute-done((bf16[32,1280]{1,0:T(8,128)(2,1)S(1)}, bf16[32,1280]{1,0:T(8,128)(2,1)S(1)}, u32[]{:S(2)}, u32[]{:S(2)}) %collective-permute-start.9) | collective-permute-done | bytes 81952 | tf_op jit(solution)/shard_map/ppermute | solution.py:329
  21.6 1.5 %collective-permute-start.7 = (bf16[288,256]{1,0:T(8,128)(2,1)S(1)}, bf16[288,256]{1,0:T(8,128)(2,1)S(1)}, u32[]{:S(2)}, u32[]{:S(2)}) collective-permute-start(bf16[288,256]{1,0:T(8,128)(2,1)S(1)} %select_select_fusion.refs_10_), channel_id=1, source_target_pairs={{0,4},{1,5},{2,6},{3,7},{4,0},{5,1},{6,2},{7,3},{8,12},{9,13},{10,... | collective-permute-start | bytes 442376 | tf_op jit(solution)/shard_map/ppermute | solution.py:329
  23.2 0.5 %collective-permute-start.13 = (bf16[32,1280]{1,0:T(8,128)(2,1)S(1)}, bf16[32,1280]{1,0:T(8,128)(2,1)S(1)}, u32[]{:S(2)}, u32[]{:S(2)}) collective-permute-start(bf16[32,1280]{1,0:T(8,128)(2,1)S(1)} %collective-permute-done.12.refs_6_), channel_id=1, source_target_pairs={{0,1},{1,0},{2,3},{3,2},{4,5},{5,4},{6,7},{7,6},{8,9},{9,8},{10,11... | collective-permute-start | bytes 245768 | tf_op jit(solution)/shard_map/ppermute | solution.py:329
  23.7 0.6 %collective-permute-done.14.refs_8_ = bf16[32,1280]{1,0:T(8,128)(2,1)S(1)} collective-permute-done((bf16[32,1280]{1,0:T(8,128)(2,1)S(1)}, bf16[32,1280]{1,0:T(8,128)(2,1)S(1)}, u32[]{:S(2)}, u32[]{:S(2)}) %collective-permute-start.14) | collective-permute-done | bytes 81952 | tf_op jit(solution)/shard_map/ppermute | solution.py:329
  24.6 0.9 %collective-permute-done.15.refs_9_ = bf16[32,1280]{1,0:T(8,128)(2,1)S(1)} collective-permute-done((bf16[32,1280]{1,0:T(8,128)(2,1)S(1)}, bf16[32,1280]{1,0:T(8,128)(2,1)S(1)}, u32[]{:S(2)}, u32[]{:S(2)}) %collective-permute-start.15) | collective-permute-done | bytes 81952 | tf_op jit(solution)/shard_map/ppermute | solution.py:329
  25.5 1.8 %begin.1 = (bf16[304,512]{1,0:T(8,128)(2,1)S(1)}, f32[256,512]{1,0:T(8,128)S(1)}, f32[1,512]{1,0:T(1,128)S(1)}, f32[1,512]{1,0:T(1,128)S(1)}) custom-call(f32[16,256]{1,0:T(8,128)S(1)} %get-tuple-element.55.cos_ref, f32[16,256]{1,0:T(8,128)S(1)} %get-tuple-element.56.sin_ref, bf16[16,1024]{1,0:T(8,128)(2,1)S(1)} %get-tuple-element.57.limits, ...), custom_call_target="tpu_custom_call" | custom-call | flops 1000 | bytes 1000 | tf_op jit(solution)/shard_map/begin/pallas_call | solution.py:333
  27.6 0.6 %further.2 = (f32[256,512]{1,0:T(8,128)S(1)}, f32[1,512]{1,0:T(1,128)S(1)}, f32[1,512]{1,0:T(1,128)S(1)}) custom-call(bf16[304,512]{1,0:T(8,128)(2,1)S(1)} %get-tuple-element.61.query_ref, f32[256,512]{1,0:T(8,128)S(1)} %get-tuple-element.62.mixed_ref, f32[1,512]{1,0:T(1,128)S(1)} %get-tuple-element.63.peak_ref, f32[1,512]{1,0:T(1,128)S(1)} %get-tuple-element.64.total_ref, ...), custom_call_target="tpu_custom_call" | custom-call | flops 1000000000 | bytes 1000 | tf_op jit(solution)/shard_map/further/pallas_call | solution.py:333
  28.2 0.7 %collective-permute-done.17.piece_ref = bf16[288,256]{1,0:T(8,128)(2,1)S(1)} collective-permute-done((bf16[288,256]{1,0:T(8,128)(2,1)S(1)}, bf16[288,256]{1,0:T(8,128)(2,1)S(1)}, u32[]{:S(2)}, u32[]{:S(2)}) %collective-permute-start.17) | collective-permute-done | bytes 147488 | tf_op jit(solution)/shard_map/ppermute | solution.py:329
  28.9 0.8 %further.3 = (bf16[144,256]{1,0:T(8,128)(2,1)S(1)}, bf16[160,256]{1,0:T(8,128)(2,1)S(1)}) custom-call(bf16[304,512]{1,0:T(8,128)(2,1)S(1)} %get-tuple-element.61.query_ref, f32[256,512]{1,0:T(8,128)S(1)} %get-tuple-element.66.mixed_ref, f32[1,512]{1,0:T(1,128)S(1)} %get-tuple-element.67.peak_ref, f32[1,512]{1,0:T(1,128)S(1)} %get-tuple-element.68.total_ref, ...), custom_call_target="tpu_custom_call" | custom-call | flops 1000000000 | bytes 1000 | tf_op jit(solution)/shard_map/further/pallas_call | solution.py:333
  29.7 2.4 %collective-permute-start.20 = (bf16[160,256]{1,0:T(8,128)(2,1)S(1)}, bf16[160,256]{1,0:T(8,128)(2,1)S(1)}, u32[]{:S(2)}, u32[]{:S(2)}) collective-permute-start(bf16[160,256]{1,0:T(8,128)(2,1)S(1)} %get-tuple-element.70), channel_id=1, source_target_pairs={{0,6},{1,7},{2,4},{3,5},{4,2},{5,3},{6,0},{7,1},{8,14},{9,15},{10,... | collective-permute-start | bytes 245768 | tf_op jit(solution)/shard_map/ppermute | solution.py:329
  32.1 0.6 %collective-permute-start.18 = (bf16[144,256]{1,0:T(8,128)(2,1)S(1)}, bf16[144,256]{1,0:T(8,128)(2,1)S(1)}, u32[]{:S(2)}, u32[]{:S(2)}) collective-permute-start(bf16[144,256]{1,0:T(8,128)(2,1)S(1)} %get-tuple-element.69.refs_4_), channel_id=1, source_target_pairs={{0,2},{1,3},{2,0},{3,1},{4,6},{5,7},{6,4},{7,5},{8,10},{9,11},{10,... | collective-permute-start | bytes 221192 | tf_op jit(solution)/shard_map/ppermute | solution.py:329
  32.7 0.5 %collective-permute-start.19 = (bf16[144,256]{1,0:T(8,128)(2,1)S(1)}, bf16[144,256]{1,0:T(8,128)(2,1)S(1)}, u32[]{:S(2)}, u32[]{:S(2)}) collective-permute-start(bf16[144,256]{1,0:T(8,128)(2,1)S(1)} %get-tuple-element.69.refs_4_), channel_id=1, source_target_pairs={{0,4},{1,5},{2,6},{3,7},{4,0},{5,1},{6,2},{7,3},{8,12},{9,13},{10,... | collective-permute-start | bytes 221192 | tf_op jit(solution)/shard_map/ppermute | solution.py:329
  33.2 3.5 %collective-permute-done.18.refs_5_ = bf16[144,256]{1,0:T(8,128)(2,1)S(1)} collective-permute-done((bf16[144,256]{1,0:T(8,128)(2,1)S(1)}, bf16[144,256]{1,0:T(8,128)(2,1)S(1)}, u32[]{:S(2)}, u32[]{:S(2)}) %collective-permute-start.18) | collective-permute-done | bytes 73760 | tf_op jit(solution)/shard_map/ppermute | solution.py:329
  37.1 0.4 out.1
  37.5 1.4 %collective-permute-done.21 = bf16[320,256]{1,0:T(8,128)(2,1)S(1)} collective-permute-done((bf16[320,256]{1,0:T(8,128)(2,1)S(1)}, bf16[320,256]{1,0:T(8,128)(2,1)S(1)}, u32[]{:S(2)}, u32[]{:S(2)}) %collective-permute-start.21) | collective-permute-done | bytes 163872 | tf_op jit(solution)/shard_map/ppermute | solution.py:329
  38.9 0.7 %fusion = bf16[256,320]{0,1:T(8,128)(2,1)} fusion(f32[320,256]{1,0:T(8,128)S(1)} %get-tuple-element.71, bf16[320,256]{1,0:T(8,128)(2,1)S(1)} %collective-permute-done.21), kind=kLoop, calls=%fused_computation.1 | loop fusion | flops 245760 | bytes 655360 | tf_op jit(solution)/shard_map/transpose | solution.py:439
  (49 shorter events, 1.9 us)
Async XLA Ops:
  0.0 1.1 %copy-start = (bf16[320,1056]{1,0:T(8,128)(2,1)S(1)}, bf16[320,1056]{1,0:T(8,128)(2,1)}, u32[]{:S(2)}) copy-start(bf16[320,1056]{1,0:T(8,128)(2,1)} %w_ref.1) | copy-start | bytes 2027524
  1.1 0.9 %copy-start.3 = (bf16[256,320]{0,1:T(8,128)(2,1)S(1)}, bf16[256,320]{0,1:T(8,128)(2,1)}, u32[]{:S(2)}) copy-start(bf16[256,320]{0,1:T(8,128)(2,1)} %param.12) | copy-start | bytes 491524
  2.0 1.1 %copy-start.10 = (bf16[1,256,288]{1,2,0:T(8,128)(2,1)S(1)}, bf16[1,256,288]{1,2,0:T(8,128)(2,1)}, u32[]{:S(2)}) copy-start(bf16[1,256,288]{1,2,0:T(8,128)(2,1)} %param.19) | copy-start | bytes 442372
  2.0 3.9 %copy-start.2 = (bf16[64,2560]{1,0:T(8,128)(2,1)S(1)}, bf16[64,2560]{1,0:T(8,128)(2,1)}, u32[]{:S(2)}) copy-start(bf16[64,2560]{1,0:T(8,128)(2,1)} %w_out_ref.1) | copy-start | bytes 983044
  2.6 3.3 %collective-permute-start = (bf16[4,32,1056]{2,1,0:T(8,128)(2,1)S(1)}, bf16[4,32,1056]{2,1,0:T(8,128)(2,1)S(1)}, u32[]{:S(2)}, u32[]{:S(2)}) collective-permute-start(bf16[4,32,1056]{2,1,0:T(8,128)(2,1)S(1)} %get-tuple-element.40), channel_id=1, source_target_pairs={{0,1},{1,0},{2,3},{3,2},{4,5},{5,4},{6,7},{7,6},{8,9},{9,8},{10,11... | collective-permute-start | bytes 811016 | tf_op jit(solution)/shard_map/ppermute | solution.py:329
  3.1 9.8 %collective-permute-start.4 = (bf16[288,256]{1,0:T(8,128)(2,1)S(1)}, bf16[288,256]{1,0:T(8,128)(2,1)S(1)}, u32[]{:S(2)}, u32[]{:S(2)}) collective-permute-start(bf16[288,256]{1,0:T(8,128)(2,1)S(1)} %bitcast.13), channel_id=1, source_target_pairs={{0,8},{8,16},{16,24},{24,0},{1,9},{9,17},{17,25},{25,1},{2,10},{10... | collective-permute-start | bytes 442376 | tf_op jit(solution)/shard_map/ppermute | solution.py:349
  6.0 7.1 %copy-start.8 = (s32[4]{0:T(128)S(1)}, s32[4]{0:T(128)}, u32[]{:S(2)}) copy-start(s32[4]{0:T(128)} %cached_ref.1) | copy-start | bytes 52
  6.0 7.1 %copy-start.9 = (s32[4]{0:T(128)S(1)}, s32[4]{0:T(128)}, u32[]{:S(2)}) copy-start(s32[4]{0:T(128)} %live_ref.1) | copy-start | bytes 52
  6.0 8.6 %copy-start.4 = (bf16[768,96]{0,1:T(8,128)(2,1)S(1)}, bf16[768,96]{0,1:T(8,128)(2,1)}, u32[]{:S(2)}) copy-start(bf16[768,96]{0,1:T(8,128)(2,1)} %param.16) | copy-start | bytes 442372
  6.1 6.9 %copy-start.11 = (f32[768]{0:T(1024)S(1)}, f32[768]{0:T(1024)}, u32[]{:S(2)}) copy-start(f32[768]{0:T(1024)} %param.14) | copy-start | bytes 9220
  6.1 8.5 %collective-permute-start.1 = (bf16[32,2432]{1,0:T(8,128)(2,1)S(1)}, bf16[32,2432]{1,0:T(8,128)(2,1)S(1)}, u32[]{:S(2)}, u32[]{:S(2)}) collective-permute-start(bf16[32,2432]{1,0:T(8,128)(2,1)S(1)} %get-tuple-element.45), channel_id=1, source_target_pairs={{0,2},{1,3},{2,0},{3,1},{4,6},{5,7},{6,4},{7,5},{8,10},{9,11},{10,... | collective-permute-start | bytes 466952 | tf_op jit(solution)/shard_map/ppermute | solution.py:329
  7.7 9.0 %collective-permute-start.2 = (bf16[32,2432]{1,0:T(8,128)(2,1)S(1)}, bf16[32,2432]{1,0:T(8,128)(2,1)S(1)}, u32[]{:S(2)}, u32[]{:S(2)}) collective-permute-start(bf16[32,2432]{1,0:T(8,128)(2,1)S(1)} %get-tuple-element.46), channel_id=1, source_target_pairs={{0,4},{1,5},{2,6},{3,7},{4,0},{5,1},{6,2},{7,3},{8,12},{9,13},{10,... | collective-permute-start | bytes 466952 | tf_op jit(solution)/shard_map/ppermute | solution.py:329
  9.2 7.4 %collective-permute-start.3 = (bf16[32,2432]{1,0:T(8,128)(2,1)S(1)}, bf16[32,2432]{1,0:T(8,128)(2,1)S(1)}, u32[]{:S(2)}, u32[]{:S(2)}) collective-permute-start(bf16[32,2432]{1,0:T(8,128)(2,1)S(1)} %get-tuple-element.47), channel_id=1, source_target_pairs={{0,6},{1,7},{2,4},{3,5},{4,2},{5,3},{6,0},{7,1},{8,14},{9,15},{10,... | collective-permute-start | bytes 466952 | tf_op jit(solution)/shard_map/ppermute | solution.py:329
  9.7 9.3 %collective-permute-start.6 = (bf16[288,256]{1,0:T(8,128)(2,1)S(1)}, bf16[288,256]{1,0:T(8,128)(2,1)S(1)}, u32[]{:S(2)}, u32[]{:S(2)}) collective-permute-start(bf16[288,256]{1,0:T(8,128)(2,1)S(1)} %bitcast.14), channel_id=1, source_target_pairs={{0,24},{8,0},{16,8},{24,16},{1,25},{9,1},{17,9},{25,17},{2,26},{10... | collective-permute-start | bytes 442376 | tf_op jit(solution)/shard_map/ppermute | solution.py:349
  13.0 7.4 %collective-permute-start.5 = (bf16[288,256]{1,0:T(8,128)(2,1)S(1)}, bf16[288,256]{1,0:T(8,128)(2,1)S(1)}, u32[]{:S(2)}, u32[]{:S(2)}) collective-permute-start(bf16[288,256]{1,0:T(8,128)(2,1)S(1)} %collective-permute-done.4), channel_id=1, source_target_pairs={{0,8},{8,16},{16,24},{24,0},{1,9},{9,17},{17,25},{25,1},{2,10},{10... | collective-permute-start | bytes 442376 | tf_op jit(solution)/shard_map/ppermute | solution.py:349
  13.0 0.7 %copy-start.6 = (f32[256]{0:T(256)S(1)}, f32[256]{0:T(256)}, u32[]{:S(2)}) copy-start(f32[256]{0:T(256)} %param.15) | copy-start | bytes 3076
  14.6 6.1 %collective-permute-start.8 = (bf16[96,768]{1,0:T(8,128)(2,1)S(1)}, bf16[96,768]{1,0:T(8,128)(2,1)S(1)}, u32[]{:S(2)}, u32[]{:S(2)}) collective-permute-start(bf16[96,768]{1,0:T(8,128)(2,1)S(1)} %bitcast.10), channel_id=1, source_target_pairs={{0,2},{1,3},{2,0},{3,1},{4,6},{5,7},{6,4},{7,5},{8,10},{9,11},{10,... | collective-permute-start | bytes 442376 | tf_op jit(solution)/shard_map/ppermute | solution.py:329
  16.8 8.8 %copy-start.1 = (bf16[256,1024]{1,0:T(8,128)(2,1)S(1)}, bf16[256,1024]{1,0:T(8,128)(2,1)}, u32[]{:S(2)}) copy-start(bf16[256,1024]{1,0:T(8,128)(2,1)} %w_kv_ref.5) | copy-start | bytes 1572868
  16.8 6.4 %collective-permute-start.10 = (bf16[32,1280]{1,0:T(8,128)(2,1)S(1)}, bf16[32,1280]{1,0:T(8,128)(2,1)S(1)}, u32[]{:S(2)}, u32[]{:S(2)}) collective-permute-start(bf16[32,1280]{1,0:T(8,128)(2,1)S(1)} %norm.1.refs_2_), channel_id=1, source_target_pairs={{0,2},{1,3},{2,0},{3,1},{4,6},{5,7},{6,4},{7,5},{8,10},{9,11},{10,... | collective-permute-start | bytes 245768 | tf_op jit(solution)/shard_map/ppermute | solution.py:329
  18.1 5.1 %collective-permute-start.12 = (bf16[32,1280]{1,0:T(8,128)(2,1)S(1)}, bf16[32,1280]{1,0:T(8,128)(2,1)S(1)}, u32[]{:S(2)}, u32[]{:S(2)}) collective-permute-start(bf16[32,1280]{1,0:T(8,128)(2,1)S(1)} %norm.1.refs_2_), channel_id=1, source_target_pairs={{0,4},{1,5},{2,6},{3,7},{4,0},{5,1},{6,2},{7,3},{8,12},{9,13},{10,... | collective-permute-start | bytes 245768 | tf_op jit(solution)/shard_map/ppermute | solution.py:329
  18.9 5.3 %collective-permute-start.14 = (bf16[32,1280]{1,0:T(8,128)(2,1)S(1)}, bf16[32,1280]{1,0:T(8,128)(2,1)S(1)}, u32[]{:S(2)}, u32[]{:S(2)}) collective-permute-start(bf16[32,1280]{1,0:T(8,128)(2,1)S(1)} %norm.1.refs_2_), channel_id=1, source_target_pairs={{0,6},{1,7},{2,4},{3,5},{4,2},{5,3},{6,0},{7,1},{8,14},{9,15},{10,... | collective-permute-start | bytes 245768 | tf_op jit(solution)/shard_map/ppermute | solution.py:329
  20.3 1.3 %collective-permute-start.9 = (bf16[32,1280]{1,0:T(8,128)(2,1)S(1)}, bf16[32,1280]{1,0:T(8,128)(2,1)S(1)}, u32[]{:S(2)}, u32[]{:S(2)}) collective-permute-start(bf16[32,1280]{1,0:T(8,128)(2,1)S(1)} %norm.1.refs_2_), channel_id=1, source_target_pairs={{0,1},{1,0},{2,3},{3,2},{4,5},{5,4},{6,7},{7,6},{8,9},{9,8},{10,11... | collective-permute-start | bytes 245768 | tf_op jit(solution)/shard_map/ppermute | solution.py:329
  20.7 3.6 %collective-permute-start.16 = (bf16[288,256]{1,0:T(8,128)(2,1)S(1)}, bf16[288,256]{1,0:T(8,128)(2,1)S(1)}, u32[]{:S(2)}, u32[]{:S(2)}) collective-permute-start(bf16[288,256]{1,0:T(8,128)(2,1)S(1)} %select_select_fusion.refs_10_), channel_id=1, source_target_pairs={{0,1},{1,0},{2,3},{3,2},{4,5},{5,4},{6,7},{7,6},{8,9},{9,8},{10,11... | collective-permute-start | bytes 442376 | tf_op jit(solution)/shard_map/ppermute | solution.py:329
  21.6 5.9 %collective-permute-start.7 = (bf16[288,256]{1,0:T(8,128)(2,1)S(1)}, bf16[288,256]{1,0:T(8,128)(2,1)S(1)}, u32[]{:S(2)}, u32[]{:S(2)}) collective-permute-start(bf16[288,256]{1,0:T(8,128)(2,1)S(1)} %select_select_fusion.refs_10_), channel_id=1, source_target_pairs={{0,4},{1,5},{2,6},{3,7},{4,0},{5,1},{6,2},{7,3},{8,12},{9,13},{10,... | collective-permute-start | bytes 442376 | tf_op jit(solution)/shard_map/ppermute | solution.py:329
  23.1 1.3 %collective-permute-start.11 = (bf16[32,1280]{1,0:T(8,128)(2,1)S(1)}, bf16[32,1280]{1,0:T(8,128)(2,1)S(1)}, u32[]{:S(2)}, u32[]{:S(2)}) collective-permute-start(bf16[32,1280]{1,0:T(8,128)(2,1)S(1)} %collective-permute-done.10.refs_4_), channel_id=1, source_target_pairs={{0,1},{1,0},{2,3},{3,2},{4,5},{5,4},{6,7},{7,6},{8,9},{9,8},{10,11... | collective-permute-start | bytes 245768 | tf_op jit(solution)/shard_map/ppermute | solution.py:329
  23.2 1.4 %collective-permute-start.13 = (bf16[32,1280]{1,0:T(8,128)(2,1)S(1)}, bf16[32,1280]{1,0:T(8,128)(2,1)S(1)}, u32[]{:S(2)}, u32[]{:S(2)}) collective-permute-start(bf16[32,1280]{1,0:T(8,128)(2,1)S(1)} %collective-permute-done.12.refs_6_), channel_id=1, source_target_pairs={{0,1},{1,0},{2,3},{3,2},{4,5},{5,4},{6,7},{7,6},{8,9},{9,8},{10,11... | collective-permute-start | bytes 245768 | tf_op jit(solution)/shard_map/ppermute | solution.py:329
  24.2 1.3 %collective-permute-start.15 = (bf16[32,1280]{1,0:T(8,128)(2,1)S(1)}, bf16[32,1280]{1,0:T(8,128)(2,1)S(1)}, u32[]{:S(2)}, u32[]{:S(2)}) collective-permute-start(bf16[32,1280]{1,0:T(8,128)(2,1)S(1)} %collective-permute-done.14.refs_8_), channel_id=1, source_target_pairs={{0,1},{1,0},{2,3},{3,2},{4,5},{5,4},{6,7},{7,6},{8,9},{9,8},{10,11... | collective-permute-start | bytes 245768 | tf_op jit(solution)/shard_map/ppermute | solution.py:329
  27.5 1.4 %collective-permute-start.17 = (bf16[288,256]{1,0:T(8,128)(2,1)S(1)}, bf16[288,256]{1,0:T(8,128)(2,1)S(1)}, u32[]{:S(2)}, u32[]{:S(2)}) collective-permute-start(bf16[288,256]{1,0:T(8,128)(2,1)S(1)} %collective-permute-done.7.piece_ref), channel_id=1, source_target_pairs={{0,1},{1,0},{2,3},{3,2},{4,5},{5,4},{6,7},{7,6},{8,9},{9,8},{10,11... | collective-permute-start | bytes 442376 | tf_op jit(solution)/shard_map/ppermute | solution.py:329
  29.7 7.4 %collective-permute-start.20 = (bf16[160,256]{1,0:T(8,128)(2,1)S(1)}, bf16[160,256]{1,0:T(8,128)(2,1)S(1)}, u32[]{:S(2)}, u32[]{:S(2)}) collective-permute-start(bf16[160,256]{1,0:T(8,128)(2,1)S(1)} %get-tuple-element.70), channel_id=1, source_target_pairs={{0,6},{1,7},{2,4},{3,5},{4,2},{5,3},{6,0},{7,1},{8,14},{9,15},{10,... | collective-permute-start | bytes 245768 | tf_op jit(solution)/shard_map/ppermute | solution.py:329
  32.1 4.7 %collective-permute-start.18 = (bf16[144,256]{1,0:T(8,128)(2,1)S(1)}, bf16[144,256]{1,0:T(8,128)(2,1)S(1)}, u32[]{:S(2)}, u32[]{:S(2)}) collective-permute-start(bf16[144,256]{1,0:T(8,128)(2,1)S(1)} %get-tuple-element.69.refs_4_), channel_id=1, source_target_pairs={{0,2},{1,3},{2,0},{3,1},{4,6},{5,7},{6,4},{7,5},{8,10},{9,11},{10,... | collective-permute-start | bytes 221192 | tf_op jit(solution)/shard_map/ppermute | solution.py:329
  32.7 4.4 %collective-permute-start.19 = (bf16[144,256]{1,0:T(8,128)(2,1)S(1)}, bf16[144,256]{1,0:T(8,128)(2,1)S(1)}, u32[]{:S(2)}, u32[]{:S(2)}) collective-permute-start(bf16[144,256]{1,0:T(8,128)(2,1)S(1)} %get-tuple-element.69.refs_4_), channel_id=1, source_target_pairs={{0,4},{1,5},{2,6},{3,7},{4,0},{5,1},{6,2},{7,3},{8,12},{9,13},{10,... | collective-permute-start | bytes 221192 | tf_op jit(solution)/shard_map/ppermute | solution.py:329
  37.5 1.5 %collective-permute-start.21 = (bf16[320,256]{1,0:T(8,128)(2,1)S(1)}, bf16[320,256]{1,0:T(8,128)(2,1)S(1)}, u32[]{:S(2)}, u32[]{:S(2)}) collective-permute-start(bf16[320,256]{1,0:T(8,128)(2,1)S(1)} %get-tuple-element.72), channel_id=1, source_target_pairs={{0,1},{1,0},{2,3},{3,2},{4,5},{5,4},{6,7},{7,6},{8,9},{9,8},{10,11... | collective-permute-start | bytes 491528 | tf_op jit(solution)/shard_map/ppermute | solution.py:329
  (2 other events, 1.4 us)
